TPU v7x, 32 devices: a whole 2x2x4 slice. The times are simulated.
32 devices in a mesh: frame: 8 (over z, x), mp: 4 (over y, core).
Axes of the slice: x: 2, y: 2, z: 4, core: 2. Of those that a mesh axis runs over, the one named last changes fastest.
Arguments:
- q_raw: bfloat16 [2048, 5120], P('frame', 'mp'), may hold values from -13 to 13
- k_raw: bfloat16 [2048, 5120], P('frame', 'mp'), may hold values from -13 to 13
- values: bfloat16 [2048, 5120], P('frame', 'mp'), may hold values from -6 to 6
- q_gain: float32 [5120], P('mp'), may hold values from 0.1 to 1.9
- k_gain: float32 [5120], P('mp'), may hold values from 0.1 to 1.9
- spatial_mask: int32 [8, 2, 2], P('frame'), may hold values from 0 to 1
- temporal_mask: int32 [8, 2, 2], P('frame'), may hold values from 0 to 1
- anchor_frame: int32 [1], replicated, may hold values from 0 to 7
Outputs:
- attended: bfloat16 [2048, 5120], P('frame', 'mp')
All inputs are finite; a program needn't handle non-finite values.
Results may differ from a plain program's by a relative error of at most 0.013.
Values may be sent and summed in bfloat16 or wider, within the bound.
No kernel may reach another device: no remote copies, remote signals or barrier semaphores. Data moves between devices by JAX's collectives and lax.ppermute only.
A program may use at most 64 MiB of HBM per device.

v0:
```python
import jax
import jax.numpy as jnp
from jax import lax
from jax.sharding import PartitionSpec as P

D = 5120
HD = 128
BLOCK = 128


def spread(value, axis, source):
    kept = jnp.where(lax.axis_index(axis) == source, value, 0).astype(value.dtype)
    return lax.psum(kept, axis)


def expand(block_mask):
    count = block_mask.shape[0]
    allowed = (block_mask == 1) | jnp.eye(count, dtype=jnp.bool_)
    return jnp.repeat(jnp.repeat(allowed, BLOCK, axis=0), BLOCK, axis=1)


def attend(query, keys, vals, allowed):
    rows = query.shape[0]
    width = query.shape[1]
    heads_dev = width // HD
    query3 = jnp.transpose(query.reshape(rows, heads_dev, HD), (1, 0, 2))
    keys3 = jnp.transpose(keys.reshape(keys.shape[0], heads_dev, HD), (1, 0, 2))
    vals3 = jnp.transpose(vals.reshape(vals.shape[0], heads_dev, HD), (1, 0, 2))
    scale = jnp.sqrt(jnp.float32(HD))

    def one_head(items):
        head_q, head_k, head_v = items
        scores = jnp.einsum("qd,kd->qk", head_q, head_k, preferred_element_type=jnp.float32) / scale
        scores = jnp.where(allowed, scores, -jnp.inf)
        probs = jax.nn.softmax(scores, axis=-1).astype(jnp.bfloat16)
        return jnp.dot(probs, head_v, preferred_element_type=jnp.float32)

    output = lax.map(one_head, (query3, keys3, vals3))
    return jnp.transpose(output, (1, 0, 2)).reshape(rows, width)


def local(q_raw, k_raw, values, q_gain, k_gain, spatial_mask, temporal_mask, anchor_frame):
    frame_tok = q_raw.shape[0]
    width = q_raw.shape[1]
    q_float = q_raw.astype(jnp.float32)
    k_float = k_raw.astype(jnp.float32)
    sum_q, sum_k = lax.psum(
        (jnp.sum(q_float * q_float, axis=1), jnp.sum(k_float * k_float, axis=1)), "mp"
    )
    q_norm = (q_float / jnp.sqrt(sum_q[:, None] / D + 1e-06) * q_gain[None, :]).astype(jnp.bfloat16)
    k_norm = (k_float / jnp.sqrt(sum_k[:, None] / D + 1e-06) * k_gain[None, :]).astype(jnp.bfloat16)
    n_frames = lax.axis_size("frame")
    group_pos = frame_tok // n_frames
    q_pencil, k_pencil, v_pencil = (
        lax.all_to_all(
            q_norm.reshape(n_frames, group_pos, width),
            "frame",
            split_axis=0,
            concat_axis=0,
            tiled=True,
        ),
        lax.all_to_all(
            k_norm.reshape(n_frames, group_pos, width),
            "frame",
            split_axis=0,
            concat_axis=0,
            tiled=True,
        ),
        lax.all_to_all(
            values.reshape(n_frames, group_pos, width),
            "frame",
            split_axis=0,
            concat_axis=0,
            tiled=True,
        ),
    )
    anchor = anchor_frame[0]
    k_anchor, v_anchor = (spread(k_norm, "frame", anchor), spread(values, "frame", anchor))
    own_allowed = jnp.concatenate(
        [expand(spatial_mask[0]), jnp.ones((frame_tok, frame_tok), dtype=jnp.bool_)], axis=1
    )
    spatial = attend(
        q_norm,
        jnp.concatenate([k_norm, k_anchor], 0),
        jnp.concatenate([values, v_anchor], 0),
        own_allowed,
    )
    temporal = attend(
        q_pencil.reshape(frame_tok, width),
        k_pencil.reshape(frame_tok, width),
        v_pencil.reshape(frame_tok, width),
        expand(temporal_mask[0]),
    )
    temporal = temporal.astype(jnp.bfloat16).reshape(n_frames, group_pos, width)
    returned = lax.all_to_all(temporal, "frame", split_axis=0, concat_axis=0, tiled=True).reshape(
        frame_tok, width
    )
    return (spatial + returned.astype(jnp.float32)).astype(jnp.bfloat16)


def solution(mesh):
    return jax.shard_map(
        local,
        mesh=mesh,
        in_specs=(
            P("frame", "mp"),
            P("frame", "mp"),
            P("frame", "mp"),
            P("mp"),
            P("mp"),
            P("frame", None, None),
            P("frame", None, None),
            P(),
        ),
        out_specs=P("frame", "mp"),
        check_vma=False,
    )
```

profile of v0, /device:TPU:0, one launch (start us, length us, event | category | flops | bytes accessed | tf_op | source)
XLA Modules:
  0.0 199.2 jit_solution(31403158812206427)
XLA Ops:
  9.2 8.4 %all-reduce.1 = (f32[256]{0:T(256)S(1)}, f32[256]{0:T(256)S(1)}) all-reduce(f32[256]{0:T(256)S(1)} %fusion.28, f32[256]{0:T(256)S(1)} %fusion.31), channel_id=1, replica_groups=mesh['frame'=8,'mp'=4] {'mp'}, use_global_device_ids=true, to_apply=%region_1.0 | all-reduce | flops 512 | bytes 4096 | tf_op jit(solution)/shard_map/psum | solution.py:47
  19.9 5.8 %all-to-all-start.1 = ((bf16[8,32,1280]{2,1,0:T(8,128)(2,1)}), bf16[8,32,1280]{2,1,0:T(8,128)(2,1)S(1)}, u32[]{:S(2)}, u32[]{:S(2)}) async-start(bf16[8,32,1280]{2,1,0:T(8,128)(2,1)} %bitcast.17), calls=%async_computation.1 | async-start | bytes 1310720 | tf_op jit(solution)/shard_map/all_to_all | solution.py:62
  27.0 14.8 %all-to-all-done.1 = bf16[8,32,1280]{2,1,0:T(8,128)(2,1)S(1)} async-done(((bf16[8,32,1280]{2,1,0:T(8,128)(2,1)}), bf16[8,32,1280]{2,1,0:T(8,128)(2,1)S(1)}, u32[]{:S(2)}, u32[]{:S(2)}) %all-to-all-start.1) | async-done | bytes 655392 | tf_op jit(solution)/shard_map/all_to_all | solution.py:62
  41.8 3.6 %all-to-all-start = ((bf16[8,32,1280]{2,1,0:T(8,128)(2,1)}), bf16[8,32,1280]{2,1,0:T(8,128)(2,1)S(1)}, u32[]{:S(2)}, u32[]{:S(2)}) async-start(bf16[8,32,1280]{2,1,0:T(8,128)(2,1)} %bitcast.15), calls=%async_computation | async-start | bytes 1310720 | tf_op jit(solution)/shard_map/all_to_all | solution.py:55
  46.7 15.1 %all-to-all-done = bf16[8,32,1280]{2,1,0:T(8,128)(2,1)S(1)} async-done(((bf16[8,32,1280]{2,1,0:T(8,128)(2,1)}), bf16[8,32,1280]{2,1,0:T(8,128)(2,1)S(1)}, u32[]{:S(2)}, u32[]{:S(2)}) %all-to-all-start) | async-done | bytes 655392 | tf_op jit(solution)/shard_map/all_to_all | solution.py:55
  61.8 4.2 %all-to-all-start.2 = ((bf16[8,32,1280]{2,1,0:T(8,128)(2,1)}), bf16[8,32,1280]{2,1,0:T(8,128)(2,1)}, u32[]{:S(2)}, u32[]{:S(2)}) async-start(bf16[8,32,1280]{2,1,0:T(8,128)(2,1)} %bitcast.19), calls=%async_computation.2 | async-start | bytes 1310720 | tf_op jit(solution)/shard_map/all_to_all | solution.py:69
  72.7 15.2 %all-to-all-done.2 = bf16[8,32,1280]{2,1,0:T(8,128)(2,1)} async-done(((bf16[8,32,1280]{2,1,0:T(8,128)(2,1)}), bf16[8,32,1280]{2,1,0:T(8,128)(2,1)}, u32[]{:S(2)}, u32[]{:S(2)}) %all-to-all-start.2) | async-done | bytes 655392 | tf_op jit(solution)/shard_map/all_to_all | solution.py:69
  90.4 29.1 %while.22 = (s32[]{:T(128)}, bf16[10,256,128]{2,1,0:T(8,128)(2,1)}, bf16[10,256,128]{2,1,0:T(8,128)(2,1)}, bf16[10,256,128]{2,1,0:T(8,128)(2,1)}, bf16[10,256,12...) while((s32[]{:T(128)}, bf16[10,256,128]{2,1,0:T(8,128)(2,1)}, ...), condition=%wide.region_13.14_spmd.clone, body=%wide.region_10.13_spmd.clone.sunk | while | flops 34078208 | bytes 1252941 | solution.py:38
  103.2 1.7 fusion.53
  109.1 1.7 fusion.53
  112.0 1.7 fusion.53
  122.3 4.2 %all-to-all-start.3 = ((bf16[8,32,1280]{2,1,0:T(8,128)(2,1)}), bf16[8,32,1280]{2,1,0:T(8,128)(2,1)}, u32[]{:S(2)}, u32[]{:S(2)}) async-start(bf16[8,32,1280]{2,1,0:T(8,128)(2,1)} %convert_element_type.46), calls=%async_computation.3 | async-start | bytes 1310720 | tf_op jit(solution)/shard_map/all_to_all | solution.py:95
  126.5 34.8 %all-reduce.5.cloned.1.call-done = (bf16[256,1280]{0,1:T(8,128)(2,1)}, bf16[256,1280]{0,1:T(8,128)(2,1)}) async-done(((bf16[256,1280]{0,1:T(8,128)(2,1)}, bf16[256,1280]{0,1:T(8,128)(2,1)}), (bf16[256,1280]{0,1:T(8,128)(2,1)}, bf16[256,1280]{0,1:T(8,128)(2,1)})) %all-reduce.5.cloned.1.call-update) | async-done | bytes 1310736 | tf_op jit(solution)/shard_map/psum | solution.py:13
  163.7 24.5 %while.21 = (s32[]{:T(128)}, f32[10,256,128]{1,2,0:T(8,128)}, bf16[10,256,128]{1,2,0:T(8,128)(2,1)S(1)}, bf16[10,512,128]{1,2,0:T(8,128)(2,1)S(1)}, pred[256,512...) while((s32[]{:T(128)}, f32[10,256,128]{1,2,0:T(8,128)}, ...), condition=%wide.region_9.10_spmd, body=%wide.region_6.9_spmd.sunk | while | flops 68156928 | bytes 2169933 | solution.py:38
  164.3 1.9 fusion.49
  166.8 1.9 fusion.49
  169.2 1.9 fusion.49
  171.6 1.9 fusion.49
  174.1 1.9 fusion.49
  176.5 1.9 fusion.49
  179.0 1.9 fusion.49
  181.4 1.9 fusion.49
  183.9 1.9 fusion.49
  186.4 1.9 fusion.49
  (114 shorter events, 54.8 us)
Async XLA Ops:
  6.5 1.6 copy-start.3
  7.9 9.7 %copy-start.4 = (f32[1280]{0:T(1024)S(1)}, f32[1280]{0:T(1024)}, u32[]{:S(2)}) copy-start(f32[1280]{0:T(1024)} %param.16) | copy-start | bytes 15364
  18.8 6.9 %copy-start.5 = (f32[1280]{0:T(1024)S(1)}, f32[1280]{0:T(1024)}, u32[]{:S(2)}) copy-start(f32[1280]{0:T(1024)} %param.15) | copy-start | bytes 15364
  19.9 21.9 %all-to-all-start.1 = ((bf16[8,32,1280]{2,1,0:T(8,128)(2,1)}), bf16[8,32,1280]{2,1,0:T(8,128)(2,1)S(1)}, u32[]{:S(2)}, u32[]{:S(2)}) async-start(bf16[8,32,1280]{2,1,0:T(8,128)(2,1)} %bitcast.17), calls=%async_computation.1 | async-start | bytes 1310720 | tf_op jit(solution)/shard_map/all_to_all | solution.py:62
  41.8 5.0 %copy-start = (bf16[8,32,1280]{2,1,0:T(8,128)(2,1)}, bf16[8,32,1280]{2,1,0:T(8,128)(2,1)S(1)}, u32[]{:S(2)}) copy-start(bf16[8,32,1280]{2,1,0:T(8,128)(2,1)S(1)} %all-to-all-done.1) | copy-start | bytes 1966084
  41.8 20.1 %all-to-all-start = ((bf16[8,32,1280]{2,1,0:T(8,128)(2,1)}), bf16[8,32,1280]{2,1,0:T(8,128)(2,1)S(1)}, u32[]{:S(2)}, u32[]{:S(2)}) async-start(bf16[8,32,1280]{2,1,0:T(8,128)(2,1)} %bitcast.15), calls=%async_computation | async-start | bytes 1310720 | tf_op jit(solution)/shard_map/all_to_all | solution.py:55
  61.8 5.2 %copy-start.1 = (bf16[8,32,1280]{2,1,0:T(8,128)(2,1)}, bf16[8,32,1280]{2,1,0:T(8,128)(2,1)S(1)}, u32[]{:S(2)}) copy-start(bf16[8,32,1280]{2,1,0:T(8,128)(2,1)S(1)} %all-to-all-done) | copy-start | bytes 1966084
  61.8 26.0 %all-to-all-start.2 = ((bf16[8,32,1280]{2,1,0:T(8,128)(2,1)}), bf16[8,32,1280]{2,1,0:T(8,128)(2,1)}, u32[]{:S(2)}, u32[]{:S(2)}) async-start(bf16[8,32,1280]{2,1,0:T(8,128)(2,1)} %bitcast.19), calls=%async_computation.2 | async-start | bytes 1310720 | tf_op jit(solution)/shard_map/all_to_all | solution.py:69
  66.0 1.0 copy-start.6
  66.0 1.4 copy-start.7
  66.1 95.2 %all-reduce.5.cloned.1.call-start = ((), (), s32[]{:S(2)}) async-start(), calls=%async_computation.4 | async-start | bytes 2621440 | tf_op jit(solution)/shard_map/psum | solution.py:13
  122.3 65.9 %all-to-all-start.3 = ((bf16[8,32,1280]{2,1,0:T(8,128)(2,1)}), bf16[8,32,1280]{2,1,0:T(8,128)(2,1)}, u32[]{:S(2)}, u32[]{:S(2)}) async-start(bf16[8,32,1280]{2,1,0:T(8,128)(2,1)} %convert_element_type.46), calls=%async_computation.3 | async-start | bytes 1310720 | tf_op jit(solution)/shard_map/all_to_all | solution.py:95
  161.3 1.3 copy-start.2
Sparse Core Ops, SparseCore 0:
  70.5 90.7 all-reduce.4
where the time goes:
time: 201 us; the launch traced here: 199 us
  waiting for transfers between devices  79.8 us (40%)
  matrix products  50.3 us (25%)
  starting transfers between devices  17.9 us (9%)
  local copies, waits for them, and re-layouts  17.7 us (9%)
  between operations  14.3 us (7%)
  other arithmetic  10.7 us (5%)
  blocking collectives  8.37 us (4%)
    dot_general x20, matrix products, one_head(): return jnp.dot(probs, head_v, preferred_element_type=jnp.float32)  36 us
    psum x1, waiting for transfers between devices, spread(): return lax.psum(kept, axis)  34.8 us
    all_to_all x1, waiting for transfers between devices, local(): lax.all_to_all(values.reshape(n_frames, group_pos, width), 'frame', split...  15.2 us
    all_to_all x1, waiting for transfers between devices, local(): lax.all_to_all(q_norm.reshape(n_frames, group_pos, width), 'frame', split...  15.1 us
    all_to_all x1, waiting for transfers between devices, local(): lax.all_to_all(k_norm.reshape(n_frames, group_pos, width), 'frame', split...  14.8 us
    dot_general x20, matrix products, one_head(): jnp.einsum('qd,kd->qk', head_q, head_k, preferred_element_type=jnp.float32)  14.3 us
    psum x1, blocking collectives, local(): lax.psum((jnp.sum(q_float * q_float, axis=1), jnp.sum(k_float * k_float,...  8.37 us
    unnamed x27, local copies, waits for them, and re-layouts  6.41 us
  transfers between devices with their start and end apart: 5, of which 4 were waited for; matrix products, arithmetic and copies ran while one was open for 35% of the time, Pallas kernels for 0%

commit v1 on v0

--- a/solution.py
+++ b/solution.py
@@ -1,11 +1,17 @@
+import functools
+
 import jax
 import jax.numpy as jnp
 from jax import lax
+from jax.experimental import pallas as pl
+from jax.experimental.pallas import tpu as pltpu
 from jax.sharding import PartitionSpec as P
 
 D = 5120
 HD = 128
 BLOCK = 128
+LOG2E = 1.4426950408889634
+NEG = -1e30
 
 
 def spread(value, axis, source):
@@ -39,7 +45,9 @@
     return jnp.transpose(output, (1, 0, 2)).reshape(rows, width)
 
 
-def local(q_raw, k_raw, values, q_gain, k_gain, spatial_mask, temporal_mask, anchor_frame):
+def local_general(
+    q_raw, k_raw, values, q_gain, k_gain, spatial_mask, temporal_mask, anchor_frame
+):
     frame_tok = q_raw.shape[0]
     width = q_raw.shape[1]
     q_float = q_raw.astype(jnp.float32)
@@ -51,29 +59,16 @@
     k_norm = (k_float / jnp.sqrt(sum_k[:, None] / D + 1e-06) * k_gain[None, :]).astype(jnp.bfloat16)
     n_frames = lax.axis_size("frame")
     group_pos = frame_tok // n_frames
-    q_pencil, k_pencil, v_pencil = (
-        lax.all_to_all(
-            q_norm.reshape(n_frames, group_pos, width),
+
+    def regroup(array):
+        return lax.all_to_all(
+            array.reshape(n_frames, group_pos, width),
             "frame",
             split_axis=0,
             concat_axis=0,
             tiled=True,
-        ),
-        lax.all_to_all(
-            k_norm.reshape(n_frames, group_pos, width),
-            "frame",
-            split_axis=0,
-            concat_axis=0,
-            tiled=True,
-        ),
-        lax.all_to_all(
-            values.reshape(n_frames, group_pos, width),
-            "frame",
-            split_axis=0,
-            concat_axis=0,
-            tiled=True,
-        ),
-    )
+        ).reshape(frame_tok, width)
+
     anchor = anchor_frame[0]
     k_anchor, v_anchor = (spread(k_norm, "frame", anchor), spread(values, "frame", anchor))
     own_allowed = jnp.concatenate(
@@ -86,19 +81,257 @@
         own_allowed,
     )
     temporal = attend(
-        q_pencil.reshape(frame_tok, width),
-        k_pencil.reshape(frame_tok, width),
-        v_pencil.reshape(frame_tok, width),
-        expand(temporal_mask[0]),
-    )
-    temporal = temporal.astype(jnp.bfloat16).reshape(n_frames, group_pos, width)
-    returned = lax.all_to_all(temporal, "frame", split_axis=0, concat_axis=0, tiled=True).reshape(
-        frame_tok, width
-    )
+        regroup(q_norm), regroup(k_norm), regroup(values), expand(temporal_mask[0])
+    ).astype(jnp.bfloat16)
+    returned = regroup(temporal)
     return (spatial + returned.astype(jnp.float32)).astype(jnp.bfloat16)
 
 
+def dot_t(a, b):
+    return lax.dot_general(a, b, (((1,), (1,)), ((), ())), preferred_element_type=jnp.float32)
+
+
+def softmax_parts(scores):
+    top = jnp.max(scores, axis=1, keepdims=True)
+    weights = jnp.exp2(scores - top)
+    total = jnp.sum(weights, axis=1, keepdims=True)
+    return top, weights.astype(jnp.bfloat16), total
+
+
+def pack_kernel(half, n_half, pos, heads2, k_ref, v_ref, out_ref):
+    for hh in range(half):
+        for p in range(n_half):
+            dst = hh * n_half + p
+            for h in range(heads2):
+                cols = slice((hh * heads2 + h) * HD, (hh * heads2 + h + 1) * HD)
+                rows = slice(p * pos, (p + 1) * pos)
+                out_ref[dst, h * pos : (h + 1) * pos, :] = k_ref[rows, cols]
+                out_ref[dst, (heads2 + h) * pos : (heads2 + h + 1) * pos, :] = v_ref[rows, cols]
+
+
+def squares_kernel(heads, q_ref, k_ref, out_ref):
+    rows = []
+    for ref in (q_ref, k_ref):
+        total = None
+        for h in range(heads):
+            part = ref[:, h * HD : (h + 1) * HD].astype(jnp.float32)
+            total = part * part if total is None else total + part * part
+        rows.append(jnp.sum(total.T, axis=0, keepdims=True))
+    pad = jnp.zeros((6, rows[0].shape[1]), jnp.float32)
+    out_ref[...] = jnp.concatenate(rows + [pad], axis=0)
+
+
+def own_kernel(
+    n_half, pos, heads2, q_ref, k_ref, v_ref, sums_ref, qg_ref, kg_ref, bias_ref, mask_ref,
+    qb_ref, own_ref, side_ref,
+):
+    heads = 2 * heads2
+    inv = lax.rsqrt(sums_ref[...] / D + 1e-06)
+    inv_t = inv.T
+    inv_q, inv_k = inv_t[:, 0:1], inv_t[:, 1:2]
+    tok = q_ref.shape[0]
+    lses = []
+    for hi in range(heads):
+        cols = slice(hi * HD, (hi + 1) * HD)
+        gain_q = qg_ref[:, cols] * (LOG2E / float(HD) ** 0.5)
+        query = (q_ref[:, cols].astype(jnp.float32) * inv_q * gain_q).astype(jnp.bfloat16)
+        keys = (k_ref[:, cols].astype(jnp.float32) * inv_k * kg_ref[:, cols]).astype(jnp.bfloat16)
+        hh, h = hi // heads2, hi % heads2
+        for p in range(n_half):
+            qb_ref[hh * n_half + p, h * pos : (h + 1) * pos, :] = query[p * pos : (p + 1) * pos]
+        parts = []
+        for i in range(tok // BLOCK):
+            rows = slice(i * BLOCK, (i + 1) * BLOCK)
+            scores = dot_t(query[rows], keys) + bias_ref[i : i + 1, :]
+            top, weights, total = softmax_parts(scores)
+            out = jnp.dot(weights, v_ref[:, cols], preferred_element_type=jnp.float32)
+            own_ref[rows, cols] = out / total
+            parts.append(top + jnp.log2(total))
+        lses.append(jnp.concatenate(parts, axis=0))
+    lane = lax.broadcasted_iota(jnp.int32, (tok, HD), 1)
+    packed = jnp.where(lane == heads, inv_k, 0.0)
+    for hi in range(heads):
+        packed = jnp.where(lane == hi, lses[hi], packed)
+    rows = packed.T[: side_ref.shape[0]]
+    sub = lax.broadcasted_iota(jnp.int32, rows.shape, 0)
+    side_ref[...] = jnp.where(sub == heads + 1, mask_ref[...], rows)
+
+
+def far_kernel(
+    n, pos, heads2, q_ref, kv_ref, a0_ref, a1_ref, a2_ref, a3_ref, col_ref, acol_ref, kg_ref,
+    bias_ref, out_ref,
+):
+    gp = pos // 2
+    rows_u = n * gp
+    anchors = (a0_ref, a1_ref, a2_ref, a3_ref)
+    lane = lax.broadcasted_iota(jnp.int32, (rows_u, HD), 1)
+    sig = [jnp.zeros((rows_u, HD), jnp.float32) for _ in range(2)]
+    v_off = heads2 * pos
+    for h in range(heads2):
+        gain = kg_ref[h : h + 1, :]
+        ka = jnp.concatenate([a[h * pos : (h + 1) * pos, :] for a in anchors], axis=0)
+        va = jnp.concatenate([a[v_off + h * pos : v_off + (h + 1) * pos, :] for a in anchors], axis=0)
+        ka = (ka.astype(jnp.float32) * acol_ref[:, 0:1] * gain).astype(jnp.bfloat16)
+        for u in range(2):
+            at = h * pos + u * gp
+            query = q_ref[:, at : at + gp, :].reshape(rows_u, HD)
+            keys = kv_ref[:, at : at + gp, :].reshape(rows_u, HD)
+            vals = kv_ref[:, v_off + at : v_off + at + gp, :].reshape(rows_u, HD)
+            keys = (keys.astype(jnp.float32) * col_ref[u, :, heads2 : heads2 + 1] * gain).astype(
+                jnp.bfloat16
+            )
+            temporal = []
+            for i in range(rows_u // BLOCK):
+                rows = slice(i * BLOCK, (i + 1) * BLOCK)
+                scores = dot_t(query[rows], keys) + bias_ref[2 * u + i : 2 * u + i + 1, :]
+                _, weights, total = softmax_parts(scores)
+                temporal.append(jnp.dot(weights, vals, preferred_element_type=jnp.float32) / total)
+            top, weights, total = softmax_parts(dot_t(query, ka))
+            anchored = jnp.dot(weights, va, preferred_element_type=jnp.float32)
+            gap = col_ref[u, :, h : h + 1] - (top + jnp.log2(total))
+            share = 1.0 / (1.0 + jnp.exp2(jnp.clip(gap, -126.0, 126.0)))
+            result = jnp.concatenate(temporal, axis=0) + anchored * (share / total)
+            out_ref[:, at : at + gp, :] = result.astype(jnp.bfloat16).reshape(n, gp, HD)
+            sig[u] = jnp.where(lane == h, 1.0 - share, sig[u])
+    for u in range(2):
+        out_ref[:, v_off + u * gp : v_off + (u + 1) * gp, :] = (
+            sig[u].astype(jnp.bfloat16).reshape(n, gp, HD)
+        )
+
+
+def join_kernel(n_half, pos, heads2, own_ref, back_ref, out_ref):
+    for hh in range(2):
+        for p in range(n_half):
+            src = hh * n_half + p
+            rows = slice(p * pos, (p + 1) * pos)
+            keep = back_ref[src, heads2 * pos : (heads2 + 1) * pos, :].astype(jnp.float32)
+            for h in range(heads2):
+                cols = slice((hh * heads2 + h) * HD, (hh * heads2 + h + 1) * HD)
+                got = back_ref[src, h * pos : (h + 1) * pos, :].astype(jnp.float32)
+                out_ref[rows, cols] = (own_ref[rows, cols] * keep[:, h : h + 1] + got).astype(
+                    jnp.bfloat16
+                )
+
+
+def call(kernel, out_shape, *args):
+    return pl.pallas_call(
+        kernel,
+        out_shape=out_shape,
+        compiler_params=pltpu.CompilerParams(vmem_limit_bytes=40 * 1024 * 1024),
+    )(*args)
+
+
+def exchange(array):
+    return lax.all_to_all(array, "frame", split_axis=0, concat_axis=0, tiled=True)
+
+
+def local_halves(
+    q_raw, k_raw, values, q_gain, k_gain, spatial_mask, temporal_mask, anchor_frame
+):
+    tok, width = q_raw.shape
+    n = lax.axis_size("frame")
+    n_mp = lax.axis_size("mp")
+    n_half = n // 2
+    heads = width // HD
+    heads2 = heads // 2
+    pos = tok // n_half
+    gp = pos // 2
+    me = lax.axis_index("frame")
+    my_half, my_quarter = me // n_half, me % n_half
+    shape = jax.ShapeDtypeStruct
+
+    kv_blocks = call(
+        functools.partial(pack_kernel, 2, n_half, pos, heads2),
+        shape((n, 2 * heads2 * pos, HD), jnp.bfloat16),
+        k_raw,
+        values,
+    )
+    kv_far = exchange(kv_blocks)
+
+    sums = call(
+        functools.partial(squares_kernel, heads), shape((8, tok), jnp.float32), q_raw, k_raw
+    )
+    total = sums
+    for step in range(1, n_mp):
+        total = total + lax.ppermute(sums, "mp", [(i, (i + step) % n_mp) for i in range(n_mp)])
+
+    blocks = tok // BLOCK
+    own_bias = jnp.where(expand(spatial_mask[0])[::BLOCK], 0.0, NEG)
+    mask_row = jnp.zeros((1, tok), jnp.float32)
+    mask_row = lax.dynamic_update_slice(
+        mask_row, temporal_mask.reshape(1, blocks * blocks).astype(jnp.float32), (0, 0)
+    )
+    side_rows = -(-(heads + 2) // 8) * 8
+    q_blocks, own, side = call(
+        functools.partial(own_kernel, n_half, pos, heads2),
+        (
+            shape((n, heads2 * pos, HD), jnp.bfloat16),
+            shape((tok, width), jnp.float32),
+            shape((side_rows, tok), jnp.float32),
+        ),
+        q_raw,
+        k_raw,
+        values,
+        total,
+        q_gain[None, :],
+        k_gain[None, :],
+        own_bias,
+        mask_row,
+    )
+    sides = lax.all_gather(side, "frame", axis=0)
+
+    lse = lax.dynamic_slice(
+        sides, (0, my_half * heads2, my_quarter * pos), (n, heads2, pos)
+    )
+    inv_k = lax.dynamic_slice(sides, (0, heads, my_quarter * pos), (n, 1, pos))
+    columns = jnp.concatenate([lse, inv_k], axis=1).reshape(n, heads2 + 1, 2, gp)
+    columns = jnp.transpose(columns, (2, 0, 3, 1)).reshape(2, n * gp, heads2 + 1)
+    anchor = anchor_frame[0]
+    inv_anchor = lax.dynamic_slice(sides, (anchor, heads, 0), (1, 1, tok)).reshape(n_half, pos)
+    inv_anchor = jnp.concatenate(
+        [lax.dynamic_slice(inv_anchor, (my_quarter ^ s, 0), (1, pos)) for s in range(n_half)], 0
+    ).reshape(tok, 1)
+    masks = lax.dynamic_slice(
+        sides, (2 * my_quarter, heads + 1, 0), (2, 1, blocks * blocks)
+    ).reshape(2, blocks, blocks)
+    far_bias = jnp.concatenate(
+        [jnp.where(expand(masks[u])[::BLOCK], 0.0, NEG) for u in range(2)], axis=0
+    )
+    gain_half = lax.dynamic_slice(k_gain.reshape(heads, HD), (my_half * heads2, 0), (heads2, HD))
+
+    q_far = exchange(q_blocks)
+    mine = lax.dynamic_index_in_dim(kv_far, anchor, 0, keepdims=False)
+    anchors = [mine] + [
+        lax.ppermute(mine, "frame", [(i, i ^ s) for i in range(n)]) for s in range(1, n_half)
+    ]
+    result = call(
+        functools.partial(far_kernel, n, pos, heads2),
+        shape((n, (heads2 + 1) * pos, HD), jnp.bfloat16),
+        q_far,
+        kv_far,
+        *anchors,
+        columns,
+        inv_anchor,
+        gain_half,
+        far_bias,
+    )
+    back = exchange(result)
+    return call(
+        functools.partial(join_kernel, n_half, pos, heads2),
+        shape((tok, width), jnp.bfloat16),
+        own,
+        back,
+    )
+
+
 def solution(mesh):
+    n = mesh.shape["frame"]
+
+    def local(*args):
+        tok, width = args[0].shape
+        fits = n == 8 and (width // HD) % 2 == 0 and tok % (n * 16) == 0
+        return local_halves(*args) if fits else local_general(*args)
+
     return jax.shard_map(
         local,
         mesh=mesh,

time: 201 us -> 112 us (0.56)
  waiting for transfers between devices: 79.8 us -> 11.7 us
  blocking collectives: 8.37 us -> 60.1 us
  matrix products: 50.3 us -> 0 us
  Pallas kernels: 0 us -> 15.2 us
  between operations: 14.3 us -> 0.96 us
  local copies, waits for them, and re-layouts: 17.7 us -> 6.88 us
  other arithmetic: 10.7 us -> 0.11 us
    dot_general x40 -> x0, matrix products: 50.3 us -> none  [the longest x20 36 us: one_head(): return jnp.dot(probs, head_v, preferred_element_type=jnp.float32)]
    all_gather x0 -> x1, blocking collectives: none -> 39.4 us  [local_halves(): sides = lax.all_gather(side, 'frame', axis=0)]
    all_to_all x4 -> x2, waiting for transfers between devices: 45 us -> 8.17 us  [exchange(): lax.all_to_all(array, 'frame', split_axis=0, concat_axis=0, tiled=True)]
    psum x1 -> x0, waiting for transfers between devices: 34.8 us -> none  [spread(): return lax.psum(kept, axis)]
    all_to_all x0 -> x1, blocking collectives: none -> 20.7 us  [exchange(): lax.all_to_all(array, 'frame', split_axis=0, concat_axis=0, tiled=True)]
    pallas_call x0 -> x5, Pallas kernels: none -> 15.2 us  [call(): pl.pallas_call(kernel, out_shape=out_shape, compiler_params=pltpu.Compile...]
    psum x1 -> x0, blocking collectives: 8.37 us -> none  [local(): lax.psum((jnp.sum(q_float * q_float, axis=1), jnp.sum(k_float * k_float,...]
    all_to_all x4 -> x2, starting transfers between devices: 17.9 us -> 11 us  [exchange(): lax.all_to_all(array, 'frame', split_axis=0, concat_axis=0, tiled=True)]
  transfers between devices with their start and end apart: 5 -> 8, of which waited for: 4 -> 5; matrix products, arithmetic and copies ran while one was open for 35% -> 3% of each run, Pallas kernels for 0% -> 5%
where the time goes in v1:
time: 112 us; the launch traced here: 111 us
  blocking collectives  60.1 us (54%)
  starting transfers between devices  16.5 us (15%)
  Pallas kernels  15.2 us (14%)
  waiting for transfers between devices  11.7 us (10%)
  local copies, waits for them, and re-layouts  6.88 us (6%)
    all_gather x1, blocking collectives, local_halves(): sides = lax.all_gather(side, 'frame', axis=0)  39.4 us
    all_to_all x1, blocking collectives, exchange(): lax.all_to_all(array, 'frame', split_axis=0, concat_axis=0, tiled=True)  20.7 us
    pallas_call x5, Pallas kernels, call(): pl.pallas_call(kernel, out_shape=out_shape, compiler_params=pltpu.Compile...  15.2 us
    all_to_all x2, starting transfers between devices, exchange(): lax.all_to_all(array, 'frame', split_axis=0, concat_axis=0, tiled=True)  11 us
    all_to_all x2, waiting for transfers between devices, exchange(): lax.all_to_all(array, 'frame', split_axis=0, concat_axis=0, tiled=True)  8.17 us
    unnamed x33, local copies, waits for them, and re-layouts  4.66 us
    ppermute x3, starting transfers between devices, local_halves(): lax.ppermute(mine, 'frame', [(i, i ^ s) for i in range(n)])  3.63 us
  transfers between devices with their start and end apart: 8, of which 5 were waited for; matrix products, arithmetic and copies ran while one was open for 3% of the time, Pallas kernels for 5%

profile of v1, /device:TPU:0, one launch (start us, length us, event | category | flops | bytes accessed | tf_op | source)
XLA Modules:
  0.0 111.4 jit_solution(5153829224504502385)
XLA Ops:
  0.0 1.1 copy-done
  1.1 1.1 copy-done.3
  2.2 1.3 %shard_map.84 = bf16[8,640,128]{2,1,0:T(8,128)(2,1)} custom-call(bf16[256,1280]{1,0:T(8,128)(2,1)S(1)} %copy-done, bf16[256,1280]{1,0:T(8,128)(2,1)S(1)} %copy-done.3), custom_call_target="tpu_custom_call" | custom-call | tf_op jit(solution)/shard_map/pallas_call | solution.py:217
  3.5 7.4 %all-to-all-start.1 = ((bf16[8,640,128]{2,1,0:T(8,128)(2,1)}), bf16[8,640,128]{2,1,0:T(8,128)(2,1)S(1)}, u32[]{:S(2)}, u32[]{:S(2)}) async-start(bf16[8,640,128]{2,1,0:T(8,128)(2,1)} %shard_map.84), calls=%async_computation.1 | async-start | bytes 2621440 | tf_op jit(solution)/shard_map/all_to_all | solution.py:225
  10.9 0.3 shard_map.82
  11.3 0.7 collective-permute-start.2
  12.0 0.9 collective-permute-start.1
  14.6 1.1 collective-permute-done.1
  15.7 0.3 collective-permute-done
  16.0 5.0 %shard_map.83 = (bf16[8,320,128]{2,1,0:T(8,128)(2,1)S(1)}, f32[256,1280]{1,0:T(8,128)S(1)}, f32[16,256]{1,0:T(8,128)S(1)}) custom-call(bf16[256,1280]{1,0:T(8,128)(2,1)S(1)} %copy-done.2, bf16[256,1280]{1,0:T(8,128)(2,1)S(1)} %copy-done.1, bf16[256,1280]{1,0:T(8,128)(2,1)S(1)} %copy-done.4, f32[8,256]{1,0:T(8,128)S(1)} %add_add_fusion.sums_ref, ...), custom_call_target="tpu_custom_call" | custom-call | tf_op jit(solution)/shard_map/pallas_call | solution.py:217
  21.0 1.1 copy-done.5
  22.1 0.8 copy-done.7
  23.0 39.4 %all-gather = f32[128,256]{1,0:T(8,128)S(1)} all-gather(f32[16,256]{1,0:T(8,128)S(1)} %get-tuple-element.10), channel_id=2, replica_groups=mesh['frame'=8,'mp'=4] {'frame'}, dimensions={0}, use_global_device_ids=true | all-gather | bytes 147456 | tf_op jit(solution)/shard_map/all_gather | solution.py:281
  62.9 3.6 %all-to-all-start = ((bf16[8,320,128]{2,1,0:T(8,128)(2,1)}), bf16[8,320,128]{2,1,0:T(8,128)(2,1)S(1)}, u32[]{:S(2)}, u32[]{:S(2)}) async-start(bf16[8,320,128]{2,1,0:T(8,128)(2,1)} %copy-done.7), calls=%async_computation | async-start | bytes 1310720 | tf_op jit(solution)/shard_map/all_to_all | solution.py:225
  66.8 0.3 slice.21
  67.2 0.3 slice.19
  67.8 3.0 %collective-permute-start.5 = (bf16[640,128]{1,0:T(8,128)(2,1)S(1)}, bf16[640,128]{1,0:T(8,128)(2,1)S(1)}, u32[]{:S(2)}, u32[]{:S(2)}) collective-permute-start(bf16[640,128]{1,0:T(8,128)(2,1)S(1)} %dynamic-slice_bitcast_fusion.a0_ref), channel_id=1, source_target_pairs={{0,12},{4,8},{8,4},{12,0},{16,28},{20,24},{24,20},{28,16},{1,13},{... | collective-permute-start | bytes 491528 | tf_op jit(solution)/shard_map/ppermute | solution.py:305
  70.8 0.6 collective-permute-start.4
  71.9 8.2 %all-to-all-done.q_ref = bf16[8,320,128]{2,1,0:T(8,128)(2,1)S(1)} async-done(((bf16[8,320,128]{2,1,0:T(8,128)(2,1)}), bf16[8,320,128]{2,1,0:T(8,128)(2,1)S(1)}, u32[]{:S(2)}, u32[]{:S(2)}) %all-to-all-start) | async-done | bytes 655392 | tf_op jit(solution)/shard_map/all_to_all | solution.py:225
  80.1 0.7 collective-permute-done.5.a3_ref
  80.7 1.5 %collective-permute-done.4.a2_ref = bf16[640,128]{1,0:T(8,128)(2,1)S(1)} collective-permute-done((bf16[640,128]{1,0:T(8,128)(2,1)S(1)}, bf16[640,128]{1,0:T(8,128)(2,1)S(1)}, u32[]{:S(2)}, u32[]{:S(2)}) %collective-permute-start.4) | collective-permute-done | bytes 163872 | tf_op jit(solution)/shard_map/ppermute | solution.py:305
  82.2 7.4 %shard_map.85 = bf16[8,384,128]{2,1,0:T(8,128)(2,1)S(1)} custom-call(bf16[8,320,128]{2,1,0:T(8,128)(2,1)S(1)} %all-to-all-done.q_ref, bf16[8,640,128]{2,1,0:T(8,128)(2,1)S(1)} %all-to-all-done.1.kv_ref, bf16[640,128]{1,0:T(8,128)(2,1)S(1)} %dynamic-slice_bitcast_fusion.a0_ref, bf16[640,128]{1,0:T(8,128)(2,1)S(1)} %collective-permute-done.3.a1_ref, ...), custom_call_target="tpu_custom_call" | custom-call | tf_op jit(solution)/shard_map/pallas_call | solution.py:217
  89.6 20.7 %all_to_all.15.back_ref = bf16[8,384,128]{2,1,0:T(8,128)(2,1)S(1)} all-to-all(bf16[8,384,128]{2,1,0:T(8,128)(2,1)S(1)} %shard_map.85), channel_id=1, replica_groups=mesh['frame'=8,'mp'=4] {'frame'}, dimensions={0} | all-to-all | bytes 1572864 | tf_op jit(solution)/shard_map/all_to_all | solution.py:225
  110.3 1.1 %shard_map.86 = bf16[256,1280]{1,0:T(8,128)(2,1)} custom-call(f32[256,1280]{1,0:T(8,128)S(1)} %copy-done.6, bf16[8,384,128]{2,1,0:T(8,128)(2,1)S(1)} %all_to_all.15.back_ref), custom_call_target="tpu_custom_call" | custom-call | tf_op jit(solution)/shard_map/pallas_call | solution.py:217
  (69 shorter events, 2.6 us)
Async XLA Ops:
  0.0 1.1 copy-start
  1.1 1.1 copy-start.3
  3.5 7.4 %copy-start.1 = (bf16[256,1280]{1,0:T(8,128)(2,1)S(1)}, bf16[256,1280]{1,0:T(8,128)(2,1)}, u32[]{:S(2)}) copy-start(bf16[256,1280]{1,0:T(8,128)(2,1)} %k_ref.5) | copy-start | bytes 1966084
  3.5 7.4 %copy-start.2 = (bf16[256,1280]{1,0:T(8,128)(2,1)S(1)}, bf16[256,1280]{1,0:T(8,128)(2,1)}, u32[]{:S(2)}) copy-start(bf16[256,1280]{1,0:T(8,128)(2,1)} %q_ref.3) | copy-start | bytes 1966084
  3.5 59.4 %all-to-all-start.1 = ((bf16[8,640,128]{2,1,0:T(8,128)(2,1)}), bf16[8,640,128]{2,1,0:T(8,128)(2,1)S(1)}, u32[]{:S(2)}, u32[]{:S(2)}) async-start(bf16[8,640,128]{2,1,0:T(8,128)(2,1)} %shard_map.84), calls=%async_computation.1 | async-start | bytes 2621440 | tf_op jit(solution)/shard_map/all_to_all | solution.py:225
  10.9 2.2 %copy-start.11 = (s32[1,2,2]{2,1,0:T(2,128)S(1)}, s32[1,2,2]{2,1,0:T(2,128)}, u32[]{:S(2)}) copy-start(s32[1,2,2]{2,1,0:T(2,128)} %param.13) | copy-start | bytes 52
  10.9 2.8 %copy-start.8 = (f32[1280]{0:T(1024)S(1)}, f32[1280]{0:T(1024)}, u32[]{:S(2)}) copy-start(f32[1280]{0:T(1024)} %param.12) | copy-start | bytes 15364
  10.9 3.5 %copy-start.10 = (s32[1,2,2]{2,1,0:T(2,128)S(1)}, s32[1,2,2]{2,1,0:T(2,128)}, u32[]{:S(2)}) copy-start(s32[1,2,2]{2,1,0:T(2,128)} %param.14) | copy-start | bytes 52
  10.9 3.6 %copy-start.9 = (f32[1280]{0:T(1024)S(1)}, f32[1280]{0:T(1024)}, u32[]{:S(2)}) copy-start(f32[1280]{0:T(1024)} %param.11) | copy-start | bytes 15364
  10.9 5.1 %copy-start.4 = (bf16[256,1280]{1,0:T(8,128)(2,1)S(1)}, bf16[256,1280]{1,0:T(8,128)(2,1)}, u32[]{:S(2)}) copy-start(bf16[256,1280]{1,0:T(8,128)(2,1)} %v_ref.3) | copy-start | bytes 1966084
  11.3 3.3 %collective-permute-start.2 = (f32[8,256]{1,0:T(8,128)S(1)}, f32[8,256]{1,0:T(8,128)S(1)}, u32[]{:S(2)}, u32[]{:S(2)}) collective-permute-start(f32[8,256]{1,0:T(8,128)S(1)} %shard_map.82), channel_id=1, source_target_pairs={{0,3},{1,0},{2,1},{3,2},{4,7},{5,4},{6,5},{7,6},{8,11},{9,8},{10,9... | collective-permute-start | bytes 24584 | tf_op jit(solution)/shard_map/ppermute | solution.py:256
  12.0 3.7 %collective-permute-start.1 = (f32[8,256]{1,0:T(8,128)S(1)}, f32[8,256]{1,0:T(8,128)S(1)}, u32[]{:S(2)}, u32[]{:S(2)}) collective-permute-start(f32[8,256]{1,0:T(8,128)S(1)} %shard_map.82), channel_id=1, source_target_pairs={{0,2},{1,3},{2,0},{3,1},{4,6},{5,7},{6,4},{7,5},{8,10},{9,11},{10,... | collective-permute-start | bytes 24584 | tf_op jit(solution)/shard_map/ppermute | solution.py:256
  12.9 3.1 %collective-permute-start = (f32[8,256]{1,0:T(8,128)S(1)}, f32[8,256]{1,0:T(8,128)S(1)}, u32[]{:S(2)}, u32[]{:S(2)}) collective-permute-start(f32[8,256]{1,0:T(8,128)S(1)} %shard_map.82), channel_id=1, source_target_pairs={{0,1},{1,2},{2,3},{3,0},{4,5},{5,6},{6,7},{7,4},{8,9},{9,10},{10,1... | collective-permute-start | bytes 24584 | tf_op jit(solution)/shard_map/ppermute | solution.py:256
  21.0 1.1 copy-start.5
  22.1 0.8 copy-start.7
  62.9 17.1 %all-to-all-start = ((bf16[8,320,128]{2,1,0:T(8,128)(2,1)}), bf16[8,320,128]{2,1,0:T(8,128)(2,1)S(1)}, u32[]{:S(2)}, u32[]{:S(2)}) async-start(bf16[8,320,128]{2,1,0:T(8,128)(2,1)} %copy-done.7), calls=%async_computation | async-start | bytes 1310720 | tf_op jit(solution)/shard_map/all_to_all | solution.py:225
  67.8 12.9 %collective-permute-start.5 = (bf16[640,128]{1,0:T(8,128)(2,1)S(1)}, bf16[640,128]{1,0:T(8,128)(2,1)S(1)}, u32[]{:S(2)}, u32[]{:S(2)}) collective-permute-start(bf16[640,128]{1,0:T(8,128)(2,1)S(1)} %dynamic-slice_bitcast_fusion.a0_ref), channel_id=1, source_target_pairs={{0,12},{4,8},{8,4},{12,0},{16,28},{20,24},{24,20},{28,16},{1,13},{... | collective-permute-start | bytes 491528 | tf_op jit(solution)/shard_map/ppermute | solution.py:305
  70.8 11.4 %collective-permute-start.4 = (bf16[640,128]{1,0:T(8,128)(2,1)S(1)}, bf16[640,128]{1,0:T(8,128)(2,1)S(1)}, u32[]{:S(2)}, u32[]{:S(2)}) collective-permute-start(bf16[640,128]{1,0:T(8,128)(2,1)S(1)} %dynamic-slice_bitcast_fusion.a0_ref), channel_id=1, source_target_pairs={{0,8},{4,12},{8,0},{12,4},{16,24},{20,28},{24,16},{28,20},{1,9},{5... | collective-permute-start | bytes 491528 | tf_op jit(solution)/shard_map/ppermute | solution.py:305
  71.4 10.8 %collective-permute-start.3 = (bf16[640,128]{1,0:T(8,128)(2,1)S(1)}, bf16[640,128]{1,0:T(8,128)(2,1)S(1)}, u32[]{:S(2)}, u32[]{:S(2)}) collective-permute-start(bf16[640,128]{1,0:T(8,128)(2,1)S(1)} %dynamic-slice_bitcast_fusion.a0_ref), channel_id=1, source_target_pairs={{0,4},{4,0},{8,12},{12,8},{16,20},{20,16},{24,28},{28,24},{1,5},{5... | collective-permute-start | bytes 491528 | tf_op jit(solution)/shard_map/ppermute | solution.py:305
  89.6 20.7 %copy-start.6 = (f32[256,1280]{1,0:T(8,128)S(1)}, f32[256,1280]{1,0:T(8,128)}, u32[]{:S(2)}) copy-start(f32[256,1280]{1,0:T(8,128)} %copy-done.5) | copy-start | bytes 3932164

commit v2 on v1

--- a/solution.py
+++ b/solution.py
@@ -278,7 +278,12 @@
         own_bias,
         mask_row,
     )
-    sides = lax.all_gather(side, "frame", axis=0)
+    sides = jnp.zeros((n,) + side.shape, side.dtype)
+    for s in range(n):
+        came = side
+        if s > 0:
+            came = lax.ppermute(side, "frame", [(i, i ^ s) for i in range(n)])
+        sides = lax.dynamic_update_slice(sides, came[None], (me ^ s, 0, 0))
 
     lse = lax.dynamic_slice(
         sides, (0, my_half * heads2, my_quarter * pos), (n, heads2, pos)

time: 112 us -> 107 us (0.955)
  blocking collectives: 60.1 us -> 24.2 us
  starting transfers between devices: 16.5 us -> 33.8 us
  waiting for transfers between devices: 11.7 us -> 25.1 us
    all_gather x1 -> x0, blocking collectives: 39.4 us -> none  [local_halves(): sides = lax.all_gather(side, 'frame', axis=0)]
    ppermute x0 -> x7, starting transfers between devices: none -> 17.3 us  [local_halves(): came = lax.ppermute(side, 'frame', [(i, i ^ s) for i in range(n)])]
    ppermute x0 -> x7, waiting for transfers between devices: none -> 10.2 us  [local_halves(): came = lax.ppermute(side, 'frame', [(i, i ^ s) for i in range(n)])]
    all_to_all x2, waiting for transfers between devices: 8.17 us -> 12.5 us  [exchange(): lax.all_to_all(array, 'frame', split_axis=0, concat_axis=0, tiled=True)]
    all_to_all x1, blocking collectives: 20.7 us -> 24.2 us  [exchange(): lax.all_to_all(array, 'frame', split_axis=0, concat_axis=0, tiled=True)]
    ppermute x3, starting transfers between devices: 1.82 us -> 3.26 us  [local_halves(): lax.ppermute(sums, 'mp', [(i, (i + step) % n_mp) for i in range(n_mp)])]
    ppermute x3, waiting for transfers between devices: 1.41 us -> 0.01 us  [local_halves(): lax.ppermute(sums, 'mp', [(i, (i + step) % n_mp) for i in range(n_mp)])]
    all_to_all x2, starting transfers between devices: 11 us -> 9.67 us  [exchange(): lax.all_to_all(array, 'frame', split_axis=0, concat_axis=0, tiled=True)]
  transfers between devices with their start and end apart: 8 -> 15, of which waited for: 5 -> 8; matrix products, arithmetic and copies ran while one was open for 3% -> 3% of each run, Pallas kernels for 5% -> 6%
where the time goes in v2:
time: 107 us; the launch traced here: 106 us
  starting transfers between devices  33.8 us (32%)
  waiting for transfers between devices  25.1 us (23%)
  blocking collectives  24.2 us (23%)
  Pallas kernels  15.2 us (14%)
  local copies, waits for them, and re-layouts  6.89 us (6%)
  between operations  1.09 us (1%)
    all_to_all x1, blocking collectives, exchange(): lax.all_to_all(array, 'frame', split_axis=0, concat_axis=0, tiled=True)  24.2 us
    ppermute x7, starting transfers between devices, local_halves(): came = lax.ppermute(side, 'frame', [(i, i ^ s) for i in range(n)])  17.3 us
    pallas_call x5, Pallas kernels, call(): pl.pallas_call(kernel, out_shape=out_shape, compiler_params=pltpu.Compile...  15.2 us
    all_to_all x2, waiting for transfers between devices, exchange(): lax.all_to_all(array, 'frame', split_axis=0, concat_axis=0, tiled=True)  12.5 us
    ppermute x7, waiting for transfers between devices, local_halves(): came = lax.ppermute(side, 'frame', [(i, i ^ s) for i in range(n)])  10.2 us
    all_to_all x2, starting transfers between devices, exchange(): lax.all_to_all(array, 'frame', split_axis=0, concat_axis=0, tiled=True)  9.67 us
    unnamed x33, local copies, waits for them, and re-layouts  4.63 us
    ppermute x3, starting transfers between devices, local_halves(): lax.ppermute(mine, 'frame', [(i, i ^ s) for i in range(n)])  3.55 us
  transfers between devices with their start and end apart: 15, of which 8 were waited for; matrix products, arithmetic and copies ran while one was open for 3% of the time, Pallas kernels for 6%

profile of v2, /device:TPU:0, one launch (start us, length us, event | category | flops | bytes accessed | tf_op | source)
XLA Modules:
  0.0 106.4 jit_solution(1379564714598051755)
XLA Ops:
  0.0 1.1 %copy-done = bf16[256,1280]{1,0:T(8,128)(2,1)S(1)} copy-done((bf16[256,1280]{1,0:T(8,128)(2,1)S(1)}, bf16[256,1280]{1,0:T(8,128)(2,1)}, u32[]{:S(2)}) %copy-start) | copy-done | bytes 655384
  1.1 1.1 %copy-done.2 = bf16[256,1280]{1,0:T(8,128)(2,1)S(1)} copy-done((bf16[256,1280]{1,0:T(8,128)(2,1)S(1)}, bf16[256,1280]{1,0:T(8,128)(2,1)}, u32[]{:S(2)}) %copy-start.2) | copy-done | bytes 655384
  2.5 2.5 %collective-permute-start.2 = (f32[8,256]{1,0:T(8,128)S(1)}, f32[8,256]{1,0:T(8,128)S(1)}, u32[]{:S(2)}, u32[]{:S(2)}) collective-permute-start(f32[8,256]{1,0:T(8,128)S(1)} %shard_map.82), channel_id=1, source_target_pairs={{0,3},{1,0},{2,1},{3,2},{4,7},{5,4},{6,5},{7,6},{8,11},{9,8},{10,9... | collective-permute-start | bytes 24584 | tf_op jit(solution)/shard_map/ppermute | solution.py:256
  5.8 1.3 %shard_map.84 = bf16[8,640,128]{2,1,0:T(8,128)(2,1)} custom-call(bf16[256,1280]{1,0:T(8,128)(2,1)S(1)} %copy-done.1, bf16[256,1280]{1,0:T(8,128)(2,1)S(1)} %copy-done.4), custom_call_target="tpu_custom_call" | custom-call | tf_op jit(solution)/shard_map/pallas_call | solution.py:217
  7.1 5.9 %all-to-all-start.1 = ((bf16[8,640,128]{2,1,0:T(8,128)(2,1)}), bf16[8,640,128]{2,1,0:T(8,128)(2,1)S(1)}, u32[]{:S(2)}, u32[]{:S(2)}) async-start(bf16[8,640,128]{2,1,0:T(8,128)(2,1)} %shard_map.84), calls=%async_computation.1 | async-start | bytes 2621440 | tf_op jit(solution)/shard_map/all_to_all | solution.py:225
  14.7 5.0 %shard_map.83 = (bf16[8,320,128]{2,1,0:T(8,128)(2,1)S(1)}, f32[256,1280]{1,0:T(8,128)S(1)}, f32[16,256]{1,0:T(8,128)S(1)}) custom-call(bf16[256,1280]{1,0:T(8,128)(2,1)S(1)} %copy-done.3, bf16[256,1280]{1,0:T(8,128)(2,1)S(1)} %copy-done.1, bf16[256,1280]{1,0:T(8,128)(2,1)S(1)} %copy-done.4, f32[8,256]{1,0:T(8,128)S(1)} %add_add_fusion.sums_ref, ...), custom_call_target="tpu_custom_call" | custom-call | tf_op jit(solution)/shard_map/pallas_call | solution.py:217
  19.7 1.1 %copy-done.5 = f32[256,1280]{1,0:T(8,128)} copy-done((f32[256,1280]{1,0:T(8,128)}, f32[256,1280]{1,0:T(8,128)S(1)}, u32[]{:S(2)}) %copy-start.5) | copy-done | bytes 1310744
  21.6 4.7 %collective-permute-start.12 = (f32[16,256]{1,0:T(8,128)S(1)}, f32[16,256]{1,0:T(8,128)S(1)}, u32[]{:S(2)}, u32[]{:S(2)}) collective-permute-start(f32[16,256]{1,0:T(8,128)S(1)} %get-tuple-element.10), channel_id=1, source_target_pairs={{0,28},{4,24},{8,20},{12,16},{16,12},{20,8},{24,4},{28,0},{1,29},{... | collective-permute-start | bytes 49160 | tf_op jit(solution)/shard_map/ppermute | solution.py:285
  27.4 1.8 %collective-permute-start.9 = (f32[16,256]{1,0:T(8,128)S(1)}, f32[16,256]{1,0:T(8,128)S(1)}, u32[]{:S(2)}, u32[]{:S(2)}) collective-permute-start(f32[16,256]{1,0:T(8,128)S(1)} %get-tuple-element.10), channel_id=1, source_target_pairs={{0,16},{4,20},{8,24},{12,28},{16,0},{20,4},{24,8},{28,12},{1,17},{... | collective-permute-start | bytes 49160 | tf_op jit(solution)/shard_map/ppermute | solution.py:285
  29.3 2.0 %collective-permute-start.6 = (f32[16,256]{1,0:T(8,128)S(1)}, f32[16,256]{1,0:T(8,128)S(1)}, u32[]{:S(2)}, u32[]{:S(2)}) collective-permute-start(f32[16,256]{1,0:T(8,128)S(1)} %get-tuple-element.10), channel_id=1, source_target_pairs={{0,4},{4,0},{8,12},{12,8},{16,20},{20,16},{24,28},{28,24},{1,5},{5... | collective-permute-start | bytes 49160 | tf_op jit(solution)/shard_map/ppermute | solution.py:285
  31.3 1.7 %collective-permute-done.6 = f32[16,256]{1,0:T(8,128)S(1)} collective-permute-done((f32[16,256]{1,0:T(8,128)S(1)}, f32[16,256]{1,0:T(8,128)S(1)}, u32[]{:S(2)}, u32[]{:S(2)}) %collective-permute-start.6) | collective-permute-done | bytes 16416 | tf_op jit(solution)/shard_map/ppermute | solution.py:285
  33.0 4.4 %collective-permute-start.7 = (f32[16,256]{1,0:T(8,128)S(1)}, f32[16,256]{1,0:T(8,128)S(1)}, u32[]{:S(2)}, u32[]{:S(2)}) collective-permute-start(f32[16,256]{1,0:T(8,128)S(1)} %get-tuple-element.10), channel_id=1, source_target_pairs={{0,8},{4,12},{8,0},{12,4},{16,24},{20,28},{24,16},{28,20},{1,9},{5... | collective-permute-start | bytes 49160 | tf_op jit(solution)/shard_map/ppermute | solution.py:285
  37.4 1.7 %collective-permute-done.7 = f32[16,256]{1,0:T(8,128)S(1)} collective-permute-done((f32[16,256]{1,0:T(8,128)S(1)}, f32[16,256]{1,0:T(8,128)S(1)}, u32[]{:S(2)}, u32[]{:S(2)}) %collective-permute-start.7) | collective-permute-done | bytes 16416 | tf_op jit(solution)/shard_map/ppermute | solution.py:285
  39.1 3.3 %collective-permute-start.8 = (f32[16,256]{1,0:T(8,128)S(1)}, f32[16,256]{1,0:T(8,128)S(1)}, u32[]{:S(2)}, u32[]{:S(2)}) collective-permute-start(f32[16,256]{1,0:T(8,128)S(1)} %get-tuple-element.10), channel_id=1, source_target_pairs={{0,12},{4,8},{8,4},{12,0},{16,28},{20,24},{24,20},{28,16},{1,13},{... | collective-permute-start | bytes 49160 | tf_op jit(solution)/shard_map/ppermute | solution.py:285
  42.4 1.7 %collective-permute-done.8 = f32[16,256]{1,0:T(8,128)S(1)} collective-permute-done((f32[16,256]{1,0:T(8,128)S(1)}, f32[16,256]{1,0:T(8,128)S(1)}, u32[]{:S(2)}, u32[]{:S(2)}) %collective-permute-start.8) | collective-permute-done | bytes 16416 | tf_op jit(solution)/shard_map/ppermute | solution.py:285
  44.1 4.9 %collective-permute-done.9 = f32[16,256]{1,0:T(8,128)S(1)} collective-permute-done((f32[16,256]{1,0:T(8,128)S(1)}, f32[16,256]{1,0:T(8,128)S(1)}, u32[]{:S(2)}, u32[]{:S(2)}) %collective-permute-start.9) | collective-permute-done | bytes 16416 | tf_op jit(solution)/shard_map/ppermute | solution.py:285
  49.7 3.7 %all-to-all-start = ((bf16[8,320,128]{2,1,0:T(8,128)(2,1)}), bf16[8,320,128]{2,1,0:T(8,128)(2,1)S(1)}, u32[]{:S(2)}, u32[]{:S(2)}) async-start(bf16[8,320,128]{2,1,0:T(8,128)(2,1)} %copy-done.7), calls=%async_computation | async-start | bytes 1310720 | tf_op jit(solution)/shard_map/all_to_all | solution.py:225
  54.7 2.9 %collective-permute-start.5 = (bf16[640,128]{1,0:T(8,128)(2,1)S(1)}, bf16[640,128]{1,0:T(8,128)(2,1)S(1)}, u32[]{:S(2)}, u32[]{:S(2)}) collective-permute-start(bf16[640,128]{1,0:T(8,128)(2,1)S(1)} %dynamic-slice_bitcast_fusion.a0_ref), channel_id=1, source_target_pairs={{0,12},{4,8},{8,4},{12,0},{16,28},{20,24},{24,20},{28,16},{1,13},{... | collective-permute-start | bytes 491528 | tf_op jit(solution)/shard_map/ppermute | solution.py:310
  58.7 12.5 %all-to-all-done.q_ref = bf16[8,320,128]{2,1,0:T(8,128)(2,1)S(1)} async-done(((bf16[8,320,128]{2,1,0:T(8,128)(2,1)}), bf16[8,320,128]{2,1,0:T(8,128)(2,1)S(1)}, u32[]{:S(2)}, u32[]{:S(2)}) %all-to-all-start) | async-done | bytes 655392 | tf_op jit(solution)/shard_map/all_to_all | solution.py:225
  71.2 0.9 collective-permute-done.5.a3_ref
  72.1 1.6 %collective-permute-done.4.a2_ref = bf16[640,128]{1,0:T(8,128)(2,1)S(1)} collective-permute-done((bf16[640,128]{1,0:T(8,128)(2,1)S(1)}, bf16[640,128]{1,0:T(8,128)(2,1)S(1)}, u32[]{:S(2)}, u32[]{:S(2)}) %collective-permute-start.4) | collective-permute-done | bytes 163872 | tf_op jit(solution)/shard_map/ppermute | solution.py:310
  73.7 7.4 %shard_map.85 = bf16[8,384,128]{2,1,0:T(8,128)(2,1)S(1)} custom-call(bf16[8,320,128]{2,1,0:T(8,128)(2,1)S(1)} %all-to-all-done.q_ref, bf16[8,640,128]{2,1,0:T(8,128)(2,1)S(1)} %all-to-all-done.1.kv_ref, bf16[640,128]{1,0:T(8,128)(2,1)S(1)} %dynamic-slice_bitcast_fusion.a0_ref, bf16[640,128]{1,0:T(8,128)(2,1)S(1)} %collective-permute-done.3.a1_ref, ...), custom_call_target="tpu_custom_call" | custom-call | tf_op jit(solution)/shard_map/pallas_call | solution.py:217
  81.1 24.2 %all_to_all.15.back_ref = bf16[8,384,128]{2,1,0:T(8,128)(2,1)S(1)} all-to-all(bf16[8,384,128]{2,1,0:T(8,128)(2,1)S(1)} %shard_map.85), channel_id=1, replica_groups=mesh['frame'=8,'mp'=4] {'frame'}, dimensions={0} | all-to-all | bytes 1572864 | tf_op jit(solution)/shard_map/all_to_all | solution.py:225
  105.2 1.1 %shard_map.86 = bf16[256,1280]{1,0:T(8,128)(2,1)} custom-call(f32[256,1280]{1,0:T(8,128)S(1)} %copy-done.6, bf16[8,384,128]{2,1,0:T(8,128)(2,1)S(1)} %all_to_all.15.back_ref), custom_call_target="tpu_custom_call" | custom-call | tf_op jit(solution)/shard_map/pallas_call | solution.py:217
  (91 shorter events, 6.8 us)
Async XLA Ops:
  0.0 1.1 %copy-start = (bf16[256,1280]{1,0:T(8,128)(2,1)S(1)}, bf16[256,1280]{1,0:T(8,128)(2,1)}, u32[]{:S(2)}) copy-start(bf16[256,1280]{1,0:T(8,128)(2,1)} %k_ref.5) | copy-start | bytes 1966084
  2.2 3.6 %copy-start.1 = (bf16[256,1280]{1,0:T(8,128)(2,1)S(1)}, bf16[256,1280]{1,0:T(8,128)(2,1)}, u32[]{:S(2)}) copy-start(bf16[256,1280]{1,0:T(8,128)(2,1)} %k_ref.5) | copy-start | bytes 1966084
  2.2 3.6 %copy-start.4 = (bf16[256,1280]{1,0:T(8,128)(2,1)S(1)}, bf16[256,1280]{1,0:T(8,128)(2,1)}, u32[]{:S(2)}) copy-start(bf16[256,1280]{1,0:T(8,128)(2,1)} %v_ref.3) | copy-start | bytes 1966084
  2.5 12.1 %collective-permute-start.2 = (f32[8,256]{1,0:T(8,128)S(1)}, f32[8,256]{1,0:T(8,128)S(1)}, u32[]{:S(2)}, u32[]{:S(2)}) collective-permute-start(f32[8,256]{1,0:T(8,128)S(1)} %shard_map.82), channel_id=1, source_target_pairs={{0,3},{1,0},{2,1},{3,2},{4,7},{5,4},{6,5},{7,6},{8,11},{9,8},{10,9... | collective-permute-start | bytes 24584 | tf_op jit(solution)/shard_map/ppermute | solution.py:256
  5.0 9.7 %collective-permute-start.1 = (f32[8,256]{1,0:T(8,128)S(1)}, f32[8,256]{1,0:T(8,128)S(1)}, u32[]{:S(2)}, u32[]{:S(2)}) collective-permute-start(f32[8,256]{1,0:T(8,128)S(1)} %shard_map.82), channel_id=1, source_target_pairs={{0,2},{1,3},{2,0},{3,1},{4,6},{5,7},{6,4},{7,5},{8,10},{9,11},{10,... | collective-permute-start | bytes 24584 | tf_op jit(solution)/shard_map/ppermute | solution.py:256
  5.6 9.0 %collective-permute-start = (f32[8,256]{1,0:T(8,128)S(1)}, f32[8,256]{1,0:T(8,128)S(1)}, u32[]{:S(2)}, u32[]{:S(2)}) collective-permute-start(f32[8,256]{1,0:T(8,128)S(1)} %shard_map.82), channel_id=1, source_target_pairs={{0,1},{1,2},{2,3},{3,0},{4,5},{5,6},{6,7},{7,4},{8,9},{9,10},{10,1... | collective-permute-start | bytes 24584 | tf_op jit(solution)/shard_map/ppermute | solution.py:256
  7.1 6.0 %copy-start.11 = (s32[1,2,2]{2,1,0:T(2,128)S(1)}, s32[1,2,2]{2,1,0:T(2,128)}, u32[]{:S(2)}) copy-start(s32[1,2,2]{2,1,0:T(2,128)} %param.13) | copy-start | bytes 52
  7.1 6.6 %copy-start.8 = (f32[1280]{0:T(1024)S(1)}, f32[1280]{0:T(1024)}, u32[]{:S(2)}) copy-start(f32[1280]{0:T(1024)} %param.12) | copy-start | bytes 15364
  7.1 7.4 %copy-start.10 = (s32[1,2,2]{2,1,0:T(2,128)S(1)}, s32[1,2,2]{2,1,0:T(2,128)}, u32[]{:S(2)}) copy-start(s32[1,2,2]{2,1,0:T(2,128)} %param.14) | copy-start | bytes 52
  7.1 7.5 %copy-start.9 = (f32[1280]{0:T(1024)S(1)}, f32[1280]{0:T(1024)}, u32[]{:S(2)}) copy-start(f32[1280]{0:T(1024)} %param.11) | copy-start | bytes 15364
  7.1 7.6 %copy-start.3 = (bf16[256,1280]{1,0:T(8,128)(2,1)S(1)}, bf16[256,1280]{1,0:T(8,128)(2,1)}, u32[]{:S(2)}) copy-start(bf16[256,1280]{1,0:T(8,128)(2,1)} %q_ref.3) | copy-start | bytes 1966084
  7.1 42.6 %all-to-all-start.1 = ((bf16[8,640,128]{2,1,0:T(8,128)(2,1)}), bf16[8,640,128]{2,1,0:T(8,128)(2,1)S(1)}, u32[]{:S(2)}, u32[]{:S(2)}) async-start(bf16[8,640,128]{2,1,0:T(8,128)(2,1)} %shard_map.84), calls=%async_computation.1 | async-start | bytes 2621440 | tf_op jit(solution)/shard_map/all_to_all | solution.py:225
  21.6 27.5 %collective-permute-start.12 = (f32[16,256]{1,0:T(8,128)S(1)}, f32[16,256]{1,0:T(8,128)S(1)}, u32[]{:S(2)}, u32[]{:S(2)}) collective-permute-start(f32[16,256]{1,0:T(8,128)S(1)} %get-tuple-element.10), channel_id=1, source_target_pairs={{0,28},{4,24},{8,20},{12,16},{16,12},{20,8},{24,4},{28,0},{1,29},{... | collective-permute-start | bytes 49160 | tf_op jit(solution)/shard_map/ppermute | solution.py:285
  26.3 22.8 %collective-permute-start.11 = (f32[16,256]{1,0:T(8,128)S(1)}, f32[16,256]{1,0:T(8,128)S(1)}, u32[]{:S(2)}, u32[]{:S(2)}) collective-permute-start(f32[16,256]{1,0:T(8,128)S(1)} %get-tuple-element.10), channel_id=1, source_target_pairs={{0,24},{4,28},{8,16},{12,20},{16,8},{20,12},{24,0},{28,4},{1,25},{... | collective-permute-start | bytes 49160 | tf_op jit(solution)/shard_map/ppermute | solution.py:285
  26.9 22.2 %collective-permute-start.10 = (f32[16,256]{1,0:T(8,128)S(1)}, f32[16,256]{1,0:T(8,128)S(1)}, u32[]{:S(2)}, u32[]{:S(2)}) collective-permute-start(f32[16,256]{1,0:T(8,128)S(1)} %get-tuple-element.10), channel_id=1, source_target_pairs={{0,20},{4,16},{8,28},{12,24},{16,4},{20,0},{24,12},{28,8},{1,21},{... | collective-permute-start | bytes 49160 | tf_op jit(solution)/shard_map/ppermute | solution.py:285
  27.4 21.6 %collective-permute-start.9 = (f32[16,256]{1,0:T(8,128)S(1)}, f32[16,256]{1,0:T(8,128)S(1)}, u32[]{:S(2)}, u32[]{:S(2)}) collective-permute-start(f32[16,256]{1,0:T(8,128)S(1)} %get-tuple-element.10), channel_id=1, source_target_pairs={{0,16},{4,20},{8,24},{12,28},{16,0},{20,4},{24,8},{28,12},{1,17},{... | collective-permute-start | bytes 49160 | tf_op jit(solution)/shard_map/ppermute | solution.py:285
  29.3 3.7 %collective-permute-start.6 = (f32[16,256]{1,0:T(8,128)S(1)}, f32[16,256]{1,0:T(8,128)S(1)}, u32[]{:S(2)}, u32[]{:S(2)}) collective-permute-start(f32[16,256]{1,0:T(8,128)S(1)} %get-tuple-element.10), channel_id=1, source_target_pairs={{0,4},{4,0},{8,12},{12,8},{16,20},{20,16},{24,28},{28,24},{1,5},{5... | collective-permute-start | bytes 49160 | tf_op jit(solution)/shard_map/ppermute | solution.py:285
  33.0 6.1 %collective-permute-start.7 = (f32[16,256]{1,0:T(8,128)S(1)}, f32[16,256]{1,0:T(8,128)S(1)}, u32[]{:S(2)}, u32[]{:S(2)}) collective-permute-start(f32[16,256]{1,0:T(8,128)S(1)} %get-tuple-element.10), channel_id=1, source_target_pairs={{0,8},{4,12},{8,0},{12,4},{16,24},{20,28},{24,16},{28,20},{1,9},{5... | collective-permute-start | bytes 49160 | tf_op jit(solution)/shard_map/ppermute | solution.py:285
  39.1 5.0 %collective-permute-start.8 = (f32[16,256]{1,0:T(8,128)S(1)}, f32[16,256]{1,0:T(8,128)S(1)}, u32[]{:S(2)}, u32[]{:S(2)}) collective-permute-start(f32[16,256]{1,0:T(8,128)S(1)} %get-tuple-element.10), channel_id=1, source_target_pairs={{0,12},{4,8},{8,4},{12,0},{16,28},{20,24},{24,20},{28,16},{1,13},{... | collective-permute-start | bytes 49160 | tf_op jit(solution)/shard_map/ppermute | solution.py:285
  49.7 21.5 %all-to-all-start = ((bf16[8,320,128]{2,1,0:T(8,128)(2,1)}), bf16[8,320,128]{2,1,0:T(8,128)(2,1)S(1)}, u32[]{:S(2)}, u32[]{:S(2)}) async-start(bf16[8,320,128]{2,1,0:T(8,128)(2,1)} %copy-done.7), calls=%async_computation | async-start | bytes 1310720 | tf_op jit(solution)/shard_map/all_to_all | solution.py:225
  54.7 17.4 %collective-permute-start.5 = (bf16[640,128]{1,0:T(8,128)(2,1)S(1)}, bf16[640,128]{1,0:T(8,128)(2,1)S(1)}, u32[]{:S(2)}, u32[]{:S(2)}) collective-permute-start(bf16[640,128]{1,0:T(8,128)(2,1)S(1)} %dynamic-slice_bitcast_fusion.a0_ref), channel_id=1, source_target_pairs={{0,12},{4,8},{8,4},{12,0},{16,28},{20,24},{24,20},{28,16},{1,13},{... | collective-permute-start | bytes 491528 | tf_op jit(solution)/shard_map/ppermute | solution.py:310
  57.6 16.1 %collective-permute-start.4 = (bf16[640,128]{1,0:T(8,128)(2,1)S(1)}, bf16[640,128]{1,0:T(8,128)(2,1)S(1)}, u32[]{:S(2)}, u32[]{:S(2)}) collective-permute-start(bf16[640,128]{1,0:T(8,128)(2,1)S(1)} %dynamic-slice_bitcast_fusion.a0_ref), channel_id=1, source_target_pairs={{0,8},{4,12},{8,0},{12,4},{16,24},{20,28},{24,16},{28,20},{1,9},{5... | collective-permute-start | bytes 491528 | tf_op jit(solution)/shard_map/ppermute | solution.py:310
  58.1 15.5 %collective-permute-start.3 = (bf16[640,128]{1,0:T(8,128)(2,1)S(1)}, bf16[640,128]{1,0:T(8,128)(2,1)S(1)}, u32[]{:S(2)}, u32[]{:S(2)}) collective-permute-start(bf16[640,128]{1,0:T(8,128)(2,1)S(1)} %dynamic-slice_bitcast_fusion.a0_ref), channel_id=1, source_target_pairs={{0,4},{4,0},{8,12},{12,8},{16,20},{20,16},{24,28},{28,24},{1,5},{5... | collective-permute-start | bytes 491528 | tf_op jit(solution)/shard_map/ppermute | solution.py:310
  81.1 24.2 %copy-start.6 = (f32[256,1280]{1,0:T(8,128)S(1)}, f32[256,1280]{1,0:T(8,128)}, u32[]{:S(2)}) copy-start(f32[256,1280]{1,0:T(8,128)} %copy-done.5) | copy-start | bytes 3932164
  (3 other events, 3.0 us)

commit v3 on v1

v3 whole, which is shorter than its diff:
```python
import functools

import jax
import jax.numpy as jnp
from jax import lax
from jax.experimental import pallas as pl
from jax.experimental.pallas import tpu as pltpu
from jax.sharding import PartitionSpec as P

D = 5120
HD = 128
BLOCK = 128
LOG2E = 1.4426950408889634
NEG = -1e30


def spread(value, axis, source):
    kept = jnp.where(lax.axis_index(axis) == source, value, 0).astype(value.dtype)
    return lax.psum(kept, axis)


def expand(block_mask):
    count = block_mask.shape[0]
    allowed = (block_mask == 1) | jnp.eye(count, dtype=jnp.bool_)
    return jnp.repeat(jnp.repeat(allowed, BLOCK, axis=0), BLOCK, axis=1)


def attend(query, keys, vals, allowed):
    rows = query.shape[0]
    width = query.shape[1]
    heads_dev = width // HD
    query3 = jnp.transpose(query.reshape(rows, heads_dev, HD), (1, 0, 2))
    keys3 = jnp.transpose(keys.reshape(keys.shape[0], heads_dev, HD), (1, 0, 2))
    vals3 = jnp.transpose(vals.reshape(vals.shape[0], heads_dev, HD), (1, 0, 2))
    scale = jnp.sqrt(jnp.float32(HD))

    def one_head(items):
        head_q, head_k, head_v = items
        scores = jnp.einsum("qd,kd->qk", head_q, head_k, preferred_element_type=jnp.float32) / scale
        scores = jnp.where(allowed, scores, -jnp.inf)
        probs = jax.nn.softmax(scores, axis=-1).astype(jnp.bfloat16)
        return jnp.dot(probs, head_v, preferred_element_type=jnp.float32)

    output = lax.map(one_head, (query3, keys3, vals3))
    return jnp.transpose(output, (1, 0, 2)).reshape(rows, width)


def local_general(
    q_raw, k_raw, values, q_gain, k_gain, spatial_mask, temporal_mask, anchor_frame
):
    frame_tok = q_raw.shape[0]
    width = q_raw.shape[1]
    q_float = q_raw.astype(jnp.float32)
    k_float = k_raw.astype(jnp.float32)
    sum_q, sum_k = lax.psum(
        (jnp.sum(q_float * q_float, axis=1), jnp.sum(k_float * k_float, axis=1)), "mp"
    )
    q_norm = (q_float / jnp.sqrt(sum_q[:, None] / D + 1e-06) * q_gain[None, :]).astype(jnp.bfloat16)
    k_norm = (k_float / jnp.sqrt(sum_k[:, None] / D + 1e-06) * k_gain[None, :]).astype(jnp.bfloat16)
    n_frames = lax.axis_size("frame")
    group_pos = frame_tok // n_frames

    def regroup(array):
        return lax.all_to_all(
            array.reshape(n_frames, group_pos, width),
            "frame",
            split_axis=0,
            concat_axis=0,
            tiled=True,
        ).reshape(frame_tok, width)

    anchor = anchor_frame[0]
    k_anchor, v_anchor = (spread(k_norm, "frame", anchor), spread(values, "frame", anchor))
    own_allowed = jnp.concatenate(
        [expand(spatial_mask[0]), jnp.ones((frame_tok, frame_tok), dtype=jnp.bool_)], axis=1
    )
    spatial = attend(
        q_norm,
        jnp.concatenate([k_norm, k_anchor], 0),
        jnp.concatenate([values, v_anchor], 0),
        own_allowed,
    )
    temporal = attend(
        regroup(q_norm), regroup(k_norm), regroup(values), expand(temporal_mask[0])
    ).astype(jnp.bfloat16)
    returned = regroup(temporal)
    return (spatial + returned.astype(jnp.float32)).astype(jnp.bfloat16)


ROWS = 16
LANES = 32


def dot_t(a, b):
    return lax.dot_general(a, b, (((1,), (1,)), ((), ())), preferred_element_type=jnp.float32)


def weigh(weights, vals):
    ones = jnp.ones(vals.shape, vals.dtype)
    both = jnp.dot(
        weights.astype(jnp.bfloat16),
        jnp.concatenate([vals, ones], axis=1),
        preferred_element_type=jnp.float32,
    )
    return both[:, :HD], both[:, HD:]


def blocked_scores(query, keys, flag, i):
    scores = dot_t(query, keys)
    near = scores[:, i * BLOCK : (i + 1) * BLOCK]
    away = scores[:, (1 - i) * BLOCK : (2 - i) * BLOCK] + flag
    return jnp.concatenate([near, away] if i == 0 else [away, near], axis=1)


def fold(parts, lane):
    out = parts[0]
    for g in range(1, len(parts)):
        out = jnp.where(lane // LANES == g, parts[g], out)
    return out


def pack_kernel(n_half, pos, wide, k_ref, v_ref, out_ref, sems):
    copies = []
    for hh in range(2):
        for p in range(n_half):
            dst = hh * n_half + p
            for t, ref in enumerate((k_ref, v_ref)):
                copies.append(
                    pltpu.make_async_copy(
                        ref.at[pl.ds(p * pos, pos), pl.ds(hh * wide, wide)],
                        out_ref.at[dst, :, pl.ds(t * wide, wide)],
                        sems.at[2 * dst + t],
                    )
                )
    for copy in copies:
        copy.start()
    for copy in copies:
        copy.wait()


def squares_kernel(heads, q_ref, k_ref, out_ref):
    rows = []
    for ref in (q_ref, k_ref):
        total = None
        for h in range(heads):
            part = ref[:, h * HD : (h + 1) * HD].astype(jnp.float32)
            total = part * part if total is None else total + part * part
        rows.append(jnp.sum(total.T, axis=0, keepdims=True))
    pad = jnp.zeros((6, rows[0].shape[1]), jnp.float32)
    out_ref[...] = jnp.concatenate(rows + [pad], axis=0)


def own_kernel(
    n_half, pos, heads2, q_ref, k_ref, v_ref, sums_ref, qg_ref, kg_ref, flag_ref, qb_ref, own_ref
):
    inv = lax.rsqrt(sums_ref[...] / D + 1e-06)
    inv_t = inv.T
    inv_q, inv_k = inv_t[:, 0:1], inv_t[:, 1:2]
    tok = q_ref.shape[0]
    lane = lax.broadcasted_iota(jnp.int32, (tok, HD), 1) % LANES
    short = lax.broadcasted_iota(jnp.int32, (ROWS, HD), 1)
    for hh in range(2):
        side = jnp.zeros((tok, HD), jnp.bfloat16)
        for h in range(heads2):
            cols = slice((hh * heads2 + h) * HD, (hh * heads2 + h + 1) * HD)
            gain_q = qg_ref[:, cols] * (LOG2E / float(HD) ** 0.5)
            query = (q_ref[:, cols].astype(jnp.float32) * inv_q * gain_q).astype(jnp.bfloat16)
            keys = (k_ref[:, cols].astype(jnp.float32) * inv_k * kg_ref[:, cols]).astype(
                jnp.bfloat16
            )
            for p in range(n_half):
                qb_ref[hh * n_half + p, h * pos : (h + 1) * pos, :] = query[
                    p * pos : (p + 1) * pos
                ]
            lse = []
            for i in range(tok // BLOCK):
                rows = slice(i * BLOCK, (i + 1) * BLOCK)
                scores = blocked_scores(query[rows], keys, flag_ref[i : i + 1, :], i)
                top = jnp.max(scores, axis=1, keepdims=True)
                out, total = weigh(jnp.exp2(scores - top), v_ref[:, cols])
                own_ref[rows, cols] = out / total
                lse.append(top + jnp.log2(total))
            rest = jnp.concatenate(lse, axis=0)
            for part in range(3):
                piece = rest.astype(jnp.bfloat16)
                side = jnp.where(lane == 3 * h + part, piece, side)
                rest = rest - piece.astype(jnp.float32)
        for p in range(n_half):
            at = p * pos
            groups = [side[at + g * ROWS : at + (g + 1) * ROWS] for g in range(pos // ROWS)]
            qb_ref[hh * n_half + p, heads2 * pos : heads2 * pos + ROWS, :] = fold(groups, short)


def far_kernel(
    n, pos, heads2, q_ref, kv_ref, a0_ref, a1_ref, a2_ref, a3_ref, col_ref, acol_ref, kg_ref,
    flag_ref, out_ref,
):
    gp = pos // 2
    rows_u = n * gp
    wide = heads2 * HD
    per = gp // ROWS
    anchors = (a0_ref, a1_ref, a2_ref, a3_ref)
    lane = lax.broadcasted_iota(jnp.int32, (rows_u, HD), 1) % LANES
    group = lax.broadcasted_iota(jnp.int32, (n, ROWS, HD), 2) // LANES
    at_side = heads2 * pos
    came = q_ref[:, at_side : at_side + ROWS, :].astype(jnp.float32).reshape(n * ROWS, HD)
    lses = []
    for u in range(2):
        turned = []
        for g in range(u * per, (u + 1) * per):
            turn = came if g == 0 else pltpu.roll(came, HD - LANES * g, 1)
            turned.append(turn.reshape(n, ROWS, HD))
        lses.append(jnp.concatenate(turned, axis=1).reshape(rows_u, HD))
    sig = [jnp.zeros((rows_u, HD), jnp.float32) for _ in range(2)]
    for h in range(heads2):
        cols = slice(h * HD, (h + 1) * HD)
        vcols = slice(wide + h * HD, wide + (h + 1) * HD)
        gain = kg_ref[h : h + 1, :]
        ka = jnp.concatenate([a[:, cols] for a in anchors], axis=0)
        va = jnp.concatenate([a[:, vcols] for a in anchors], axis=0)
        ka = (ka.astype(jnp.float32) * acol_ref[:, 0:1] * gain).astype(jnp.bfloat16)
        for u in range(2):
            at = h * pos + u * gp
            span = slice(u * gp, (u + 1) * gp)
            query = q_ref[:, at : at + gp, :].reshape(rows_u, HD)
            keys = kv_ref[:, span, cols].reshape(rows_u, HD)
            vals = kv_ref[:, span, vcols].reshape(rows_u, HD)
            keys = (keys.astype(jnp.float32) * col_ref[u] * gain).astype(jnp.bfloat16)
            lse = lses[u][:, 3 * h : 3 * h + 1]
            lse = lse + lses[u][:, 3 * h + 1 : 3 * h + 2] + lses[u][:, 3 * h + 2 : 3 * h + 3]
            keep = []
            for i in range(rows_u // BLOCK):
                rows = slice(i * BLOCK, (i + 1) * BLOCK)
                flag = flag_ref[2 * u + i : 2 * u + i + 1, :]
                scores = blocked_scores(query[rows], keys, flag, i)
                top = jnp.max(scores, axis=1, keepdims=True)
                out, total = weigh(jnp.exp2(scores - top), vals)
                temporal = out / total
                scores = dot_t(query[rows], ka)
                top = jnp.maximum(jnp.max(scores, axis=1, keepdims=True), lse[rows])
                own = jnp.exp2(lse[rows] - top)
                out, total = weigh(jnp.exp2(scores - top), va)
                scale = 1.0 / (total + own)
                result = temporal + out * scale
                keep.append(own * scale)
                f0 = i * BLOCK // gp
                out_ref[f0 : f0 + BLOCK // gp, at : at + gp, :] = result.astype(
                    jnp.bfloat16
                ).reshape(BLOCK // gp, gp, HD)
            sig[u] = jnp.where(lane == h, jnp.concatenate(keep, axis=0), sig[u])
    groups = []
    for u in range(2):
        back = sig[u].reshape(n, gp, HD)
        groups += [back[:, g * ROWS : (g + 1) * ROWS, :] for g in range(per)]
    out_ref[:, at_side : at_side + ROWS, :] = fold(
        groups, group * LANES
    ).astype(jnp.bfloat16)


def join_kernel(n_half, pos, heads2, own_ref, back_ref, out_ref):
    for hh in range(2):
        for p in range(n_half):
            src = hh * n_half + p
            rows = slice(p * pos, (p + 1) * pos)
            side = back_ref[src, heads2 * pos : heads2 * pos + ROWS, :].astype(jnp.float32)
            keep = jnp.concatenate(
                [
                    side if g == 0 else pltpu.roll(side, HD - LANES * g, 1)
                    for g in range(pos // ROWS)
                ],
                axis=0,
            )
            for h in range(heads2):
                cols = slice((hh * heads2 + h) * HD, (hh * heads2 + h + 1) * HD)
                got = back_ref[src, h * pos : (h + 1) * pos, :].astype(jnp.float32)
                out_ref[rows, cols] = (own_ref[rows, cols] * keep[:, h : h + 1] + got).astype(
                    jnp.bfloat16
                )


def call(kernel, out_shape, *args, **more):
    return pl.pallas_call(
        kernel,
        out_shape=out_shape,
        compiler_params=pltpu.CompilerParams(vmem_limit_bytes=40 * 1024 * 1024),
        **more,
    )(*args)


def exchange(array):
    return lax.all_to_all(array, "frame", split_axis=0, concat_axis=0, tiled=True)


def pairwise(array, axis, step):
    size = lax.axis_size(axis)
    return lax.ppermute(array, axis, [(i, i ^ step) for i in range(size)])


def local_halves(
    q_raw, k_raw, values, q_gain, k_gain, spatial_mask, temporal_mask, anchor_frame
):
    tok, width = q_raw.shape
    n = lax.axis_size("frame")
    n_mp = lax.axis_size("mp")
    n_half = n // 2
    heads = width // HD
    heads2 = heads // 2
    wide = heads2 * HD
    pos = tok // n_half
    gp = pos // 2
    blocks = tok // BLOCK
    me = lax.axis_index("frame")
    my_half, my_quarter = me // n_half, me % n_half
    shape = jax.ShapeDtypeStruct

    kv_blocks = call(
        functools.partial(pack_kernel, n_half, pos, wide),
        shape((n, pos, 2 * wide), jnp.bfloat16),
        k_raw,
        values,
        in_specs=[pl.BlockSpec(memory_space=pltpu.HBM)] * 2,
        out_specs=pl.BlockSpec(memory_space=pltpu.HBM),
        scratch_shapes=[pltpu.SemaphoreType.DMA((2 * n,))],
    )
    kv_far = exchange(kv_blocks)

    sums = call(
        functools.partial(squares_kernel, heads), shape((8, tok), jnp.float32), q_raw, k_raw
    )
    total = sums
    for step in range(1, n_mp):
        total = total + lax.ppermute(sums, "mp", [(i, (i + step) % n_mp) for i in range(n_mp)])

    sides = jnp.zeros((2 * n, tok), jnp.float32)
    sides = lax.dynamic_update_slice(sides, lax.rsqrt(total[1:2] / D + 1e-06), (me, 0))
    sides = lax.dynamic_update_slice(
        sides,
        temporal_mask.reshape(1, blocks * blocks).astype(jnp.float32),
        (n, me * blocks * blocks),
    )
    step = 1
    while step < n:
        sides = sides + pairwise(sides, "frame", step)
        step *= 2

    def flags(mask):
        away = jnp.stack([mask[..., i, 1 - i] for i in range(blocks)], axis=-1).reshape(-1, 1)
        return jnp.broadcast_to(jnp.where(away == 1, 0.0, NEG), (away.shape[0], BLOCK))

    q_blocks, own = call(
        functools.partial(own_kernel, n_half, pos, heads2),
        (
            shape((n, heads2 * pos + ROWS, HD), jnp.bfloat16),
            shape((tok, width), jnp.float32),
        ),
        q_raw,
        k_raw,
        values,
        total,
        q_gain[None, :],
        k_gain[None, :],
        flags(spatial_mask),
    )
    q_far = exchange(q_blocks)

    inv_k = lax.dynamic_slice(sides, (0, my_quarter * pos), (n, pos)).reshape(n, 2, gp)
    inv_k = jnp.transpose(inv_k, (1, 0, 2)).reshape(2, n * gp, 1)
    anchor = anchor_frame[0]
    inv_anchor = lax.dynamic_slice(sides, (anchor, 0), (1, tok)).reshape(n_half, pos)
    inv_anchor = jnp.concatenate(
        [lax.dynamic_slice(inv_anchor, (my_quarter ^ s, 0), (1, pos)) for s in range(n_half)], 0
    ).reshape(tok, 1)
    masks = lax.dynamic_slice(
        sides, (n, 2 * my_quarter * blocks * blocks), (1, 2 * blocks * blocks)
    ).reshape(2, blocks, blocks)
    gain_half = lax.dynamic_slice(k_gain.reshape(heads, HD), (my_half * heads2, 0), (heads2, HD))

    mine = lax.dynamic_index_in_dim(kv_far, anchor, 0, keepdims=False)
    anchors = [mine] + [pairwise(mine, "frame", s) for s in range(1, n_half)]
    result = call(
        functools.partial(far_kernel, n, pos, heads2),
        shape((n, heads2 * pos + ROWS, HD), jnp.bfloat16),
        q_far,
        kv_far,
        *anchors,
        inv_k,
        inv_anchor,
        gain_half,
        flags(masks),
    )
    back = exchange(result)
    return call(
        functools.partial(join_kernel, n_half, pos, heads2),
        shape((tok, width), jnp.bfloat16),
        own,
        back,
    )


def solution(mesh):
    n = mesh.shape["frame"]

    def local(*args):
        tok, width = args[0].shape
        fits = n == 8 and (width // HD) % 2 == 0 and tok == 2 * BLOCK
        return local_halves(*args) if fits else local_general(*args)

    return jax.shard_map(
        local,
        mesh=mesh,
        in_specs=(
            P("frame", "mp"),
            P("frame", "mp"),
            P("frame", "mp"),
            P("mp"),
            P("mp"),
            P("frame", None, None),
            P("frame", None, None),
            P(),
        ),
        out_specs=P("frame", "mp"),
        check_vma=False,
    )
```

time: 112 us -> 104 us (0.929)
  blocking collectives: 60.1 us -> 21.7 us
  waiting for transfers between devices: 11.7 us -> 38.5 us
  starting transfers between devices: 16.5 us -> 24.7 us
  Pallas kernels: 15.2 us -> 10.5 us
  other arithmetic: 0.11 us -> 1.41 us
  local copies, waits for them, and re-layouts: 6.88 us -> 5.61 us
    all_gather x1 -> x0, blocking collectives: 39.4 us -> none  [local_halves(): sides = lax.all_gather(side, 'frame', axis=0)]
    all_to_all x2, waiting for transfers between devices: 8.17 us -> 22.8 us  [exchange(): lax.all_to_all(array, 'frame', split_axis=0, concat_axis=0, tiled=True)]
    ppermute x3 -> x6, waiting for transfers between devices: 2.11 us -> 14.8 us  [pairwise(): return lax.ppermute(array, axis, [(i, i ^ step) for i in range(size)])]
    ppermute x3 -> x6, starting transfers between devices: 3.63 us -> 11.8 us  [pairwise(): return lax.ppermute(array, axis, [(i, i ^ step) for i in range(size)])]
    pallas_call x5, Pallas kernels: 15.2 us -> 10.5 us  [call(): pl.pallas_call(kernel, out_shape=out_shape, compiler_params=pltpu.Compile...]
    unnamed x33 -> x22, local copies, waits for them, and re-layouts: 4.66 us -> 3.3 us
    select_n x2, other arithmetic: 0.01 us -> 1.37 us  [flags(): jnp.where(away == 1, 0.0, NEG)]
  transfers between devices with their start and end apart: 8 -> 11, of which waited for: 5 -> 9; matrix products, arithmetic and copies ran while one was open for 3% -> 4% of each run, Pallas kernels for 5% -> 3%
where the time goes in v3:
time: 104 us; the launch traced here: 103 us
  waiting for transfers between devices  38.5 us (37%)
  starting transfers between devices  24.7 us (24%)
  blocking collectives  21.7 us (21%)
  Pallas kernels  10.5 us (10%)
  local copies, waits for them, and re-layouts  5.61 us (5%)
  other arithmetic  1.41 us (1%)
    all_to_all x2, waiting for transfers between devices, exchange(): lax.all_to_all(array, 'frame', split_axis=0, concat_axis=0, tiled=True)  22.8 us
    all_to_all x1, blocking collectives, exchange(): lax.all_to_all(array, 'frame', split_axis=0, concat_axis=0, tiled=True)  21.7 us
    ppermute x6, waiting for transfers between devices, pairwise(): return lax.ppermute(array, axis, [(i, i ^ step) for i in range(size)])  14.8 us
    ppermute x6, starting transfers between devices, pairwise(): return lax.ppermute(array, axis, [(i, i ^ step) for i in range(size)])  11.8 us
    all_to_all x2, starting transfers between devices, exchange(): lax.all_to_all(array, 'frame', split_axis=0, concat_axis=0, tiled=True)  11 us
    pallas_call x5, Pallas kernels, call(): pl.pallas_call(kernel, out_shape=out_shape, compiler_params=pltpu.Compile...  10.5 us
    unnamed x22, local copies, waits for them, and re-layouts  3.3 us
  transfers between devices with their start and end apart: 11, of which 9 were waited for; matrix products, arithmetic and copies ran while one was open for 4% of the time, Pallas kernels for 3%

profile of v3, /device:TPU:0, one launch (start us, length us, event | category | flops | bytes accessed | tf_op | source)
XLA Modules:
  0.0 103.3 jit_solution(6582643382252732959)
XLA Ops:
  0.0 1.1 %copy-done = bf16[256,1280]{1,0:T(8,128)(2,1)S(1)} copy-done((bf16[256,1280]{1,0:T(8,128)(2,1)S(1)}, bf16[256,1280]{1,0:T(8,128)(2,1)}, u32[]{:S(2)}) %copy-start) | copy-done | bytes 655384
  1.1 1.1 %copy-done.2 = bf16[256,1280]{1,0:T(8,128)(2,1)S(1)} copy-done((bf16[256,1280]{1,0:T(8,128)(2,1)S(1)}, bf16[256,1280]{1,0:T(8,128)(2,1)}, u32[]{:S(2)}) %copy-start.2) | copy-done | bytes 655384
  2.2 1.2 %shard_map.84 = bf16[8,64,1280]{2,1,0:T(8,128)(2,1)} custom-call(bf16[256,1280]{1,0:T(8,128)(2,1)S(1)} %copy-done, bf16[256,1280]{1,0:T(8,128)(2,1)S(1)} %copy-done.2), custom_call_target="tpu_custom_call" | custom-call | tf_op jit(solution)/shard_map/pallas_call | solution.py:282
  3.4 7.4 %all-to-all-start.1 = ((bf16[8,64,1280]{2,1,0:T(8,128)(2,1)}), bf16[8,64,1280]{2,1,0:T(8,128)(2,1)S(1)}, u32[]{:S(2)}, u32[]{:S(2)}) async-start(bf16[8,64,1280]{2,1,0:T(8,128)(2,1)} %shard_map.84), calls=%async_computation.1 | async-start | bytes 2621440 | tf_op jit(solution)/shard_map/all_to_all | solution.py:291
  11.9 0.9 collective-permute-start.1
  13.6 1.4 %fusion.3 = f32[2]{0:T(128)S(1)} fusion(s32[1,1]{1,0:T(1,128)} %bitcast.1, s32[1,1]{1,0:T(1,128)} %bitcast), kind=kLoop, calls=%fused_computation.18 | loop fusion | flops 6 | bytes 16 | tf_op jit(solution)/shard_map/jit(_where)/select_n | solution.py:348
  16.0 2.3 %shard_map.83 = (bf16[8,336,128]{2,1,0:T(8,128)(2,1)}, f32[256,1280]{1,0:T(8,128)S(1)}) custom-call(bf16[256,1280]{1,0:T(8,128)(2,1)S(1)} %copy-done.4, bf16[256,1280]{1,0:T(8,128)(2,1)S(1)} %copy-done.1, bf16[256,1280]{1,0:T(8,128)(2,1)S(1)} %copy-done.3, f32[8,256]{1,0:T(8,128)S(1)} %add_add_fusion.sums_ref, f32[1,1280]{1,0:T(1,128)S(1)} %broadcast_in_dim.35.qg_ref, ...), custom_call_target="tpu_custom_call" | custom-call | tf_op jit(solution)/shard_map/pallas_call | solution.py:282
  18.3 1.1 %copy-done.5 = f32[256,1280]{1,0:T(8,128)} copy-done((f32[256,1280]{1,0:T(8,128)}, f32[256,1280]{1,0:T(8,128)S(1)}, u32[]{:S(2)}) %copy-start.5) | copy-done | bytes 1310744
  19.4 22.8 %all-to-all-done.1.kv_ref = bf16[8,64,1280]{2,1,0:T(8,128)(2,1)S(1)} async-done(((bf16[8,64,1280]{2,1,0:T(8,128)(2,1)}), bf16[8,64,1280]{2,1,0:T(8,128)(2,1)S(1)}, u32[]{:S(2)}, u32[]{:S(2)}) %all-to-all-start.1) | async-done | bytes 1310752 | tf_op jit(solution)/shard_map/all_to_all | solution.py:291
  42.2 3.6 %all-to-all-start = ((bf16[8,336,128]{2,1,0:T(8,128)(2,1)}), bf16[8,336,128]{2,1,0:T(8,128)(2,1)S(1)}, u32[]{:S(2)}, u32[]{:S(2)}) async-start(bf16[8,336,128]{2,1,0:T(8,128)(2,1)} %get-tuple-element.8), calls=%async_computation | async-start | bytes 1376256 | tf_op jit(solution)/shard_map/all_to_all | solution.py:291
  46.2 2.2 %collective-permute-start.6 = (f32[16,256]{1,0:T(8,128)S(1)}, f32[16,256]{1,0:T(8,128)S(1)}, u32[]{:S(2)}, u32[]{:S(2)}) collective-permute-start(f32[16,256]{1,0:T(8,128)S(1)} %dynamic_update_slice.7), channel_id=1, source_target_pairs={{0,4},{4,0},{8,12},{12,8},{16,20},{20,16},{24,28},{28,24},{1,5},{5... | collective-permute-start | bytes 49160 | tf_op jit(solution)/shard_map/ppermute | solution.py:296
  48.4 3.9 %collective-permute-done.6 = f32[16,256]{1,0:T(8,128)S(1)} collective-permute-done((f32[16,256]{1,0:T(8,128)S(1)}, f32[16,256]{1,0:T(8,128)S(1)}, u32[]{:S(2)}, u32[]{:S(2)}) %collective-permute-start.6) | collective-permute-done | bytes 16416 | tf_op jit(solution)/shard_map/ppermute | solution.py:296
  52.3 1.5 %collective-permute-start.7 = (f32[16,256]{1,0:T(8,128)S(1)}, f32[16,256]{1,0:T(8,128)S(1)}, u32[]{:S(2)}, u32[]{:S(2)}) collective-permute-start(f32[16,256]{1,0:T(8,128)S(1)} %add.71), channel_id=1, source_target_pairs={{0,8},{4,12},{8,0},{12,4},{16,24},{20,28},{24,16},{28,20},{1,9},{5... | collective-permute-start | bytes 49160 | tf_op jit(solution)/shard_map/ppermute | solution.py:296
  53.8 3.8 %collective-permute-done.7 = f32[16,256]{1,0:T(8,128)S(1)} collective-permute-done((f32[16,256]{1,0:T(8,128)S(1)}, f32[16,256]{1,0:T(8,128)S(1)}, u32[]{:S(2)}, u32[]{:S(2)}) %collective-permute-start.7) | collective-permute-done | bytes 16416 | tf_op jit(solution)/shard_map/ppermute | solution.py:296
  57.6 4.6 %collective-permute-start.8 = (f32[16,256]{1,0:T(8,128)S(1)}, f32[16,256]{1,0:T(8,128)S(1)}, u32[]{:S(2)}, u32[]{:S(2)}) collective-permute-start(f32[16,256]{1,0:T(8,128)S(1)} %add.72), channel_id=1, source_target_pairs={{0,16},{4,20},{8,24},{12,28},{16,0},{20,4},{24,8},{28,12},{1,17},{... | collective-permute-start | bytes 49160 | tf_op jit(solution)/shard_map/ppermute | solution.py:296
  62.8 1.9 %collective-permute-done.8 = f32[16,256]{1,0:T(8,128)S(1)} collective-permute-done((f32[16,256]{1,0:T(8,128)S(1)}, f32[16,256]{1,0:T(8,128)S(1)}, u32[]{:S(2)}, u32[]{:S(2)}) %collective-permute-start.8) | collective-permute-done | bytes 16416 | tf_op jit(solution)/shard_map/ppermute | solution.py:296
  65.3 1.5 %collective-permute-start.3 = (bf16[64,1280]{1,0:T(8,128)(2,1)S(1)}, bf16[64,1280]{1,0:T(8,128)(2,1)S(1)}, u32[]{:S(2)}, u32[]{:S(2)}) collective-permute-start(bf16[64,1280]{1,0:T(8,128)(2,1)S(1)} %dynamic-slice_bitcast_fusion.a0_ref), channel_id=1, source_target_pairs={{0,4},{4,0},{8,12},{12,8},{16,20},{20,16},{24,28},{28,24},{1,5},{5... | collective-permute-start | bytes 491528 | tf_op jit(solution)/shard_map/ppermute | solution.py:296
  67.2 1.6 %collective-permute-start.5 = (bf16[64,1280]{1,0:T(8,128)(2,1)S(1)}, bf16[64,1280]{1,0:T(8,128)(2,1)S(1)}, u32[]{:S(2)}, u32[]{:S(2)}) collective-permute-start(bf16[64,1280]{1,0:T(8,128)(2,1)S(1)} %dynamic-slice_bitcast_fusion.a0_ref), channel_id=1, source_target_pairs={{0,12},{4,8},{8,4},{12,0},{16,28},{20,24},{24,20},{28,16},{1,13},{... | collective-permute-start | bytes 491528 | tf_op jit(solution)/shard_map/ppermute | solution.py:296
  69.6 2.9 %collective-permute-done.3.a1_ref = bf16[64,1280]{1,0:T(8,128)(2,1)S(1)} collective-permute-done((bf16[64,1280]{1,0:T(8,128)(2,1)S(1)}, bf16[64,1280]{1,0:T(8,128)(2,1)S(1)}, u32[]{:S(2)}, u32[]{:S(2)}) %collective-permute-start.3) | collective-permute-done | bytes 163872 | tf_op jit(solution)/shard_map/ppermute | solution.py:296
  72.4 0.9 collective-permute-done.4.a2_ref
  73.3 1.6 %collective-permute-done.5.a3_ref = bf16[64,1280]{1,0:T(8,128)(2,1)S(1)} collective-permute-done((bf16[64,1280]{1,0:T(8,128)(2,1)S(1)}, bf16[64,1280]{1,0:T(8,128)(2,1)S(1)}, u32[]{:S(2)}, u32[]{:S(2)}) %collective-permute-start.5) | collective-permute-done | bytes 163872 | tf_op jit(solution)/shard_map/ppermute | solution.py:296
  74.9 5.1 %shard_map.85 = bf16[8,336,128]{2,1,0:T(8,128)(2,1)S(1)} custom-call(bf16[8,336,128]{2,1,0:T(8,128)(2,1)S(1)} %all-to-all-done.q_ref, bf16[8,64,1280]{2,1,0:T(8,128)(2,1)S(1)} %all-to-all-done.1.kv_ref, bf16[64,1280]{1,0:T(8,128)(2,1)S(1)} %dynamic-slice_bitcast_fusion.a0_ref, bf16[64,1280]{1,0:T(8,128)(2,1)S(1)} %collective-permute-done.3.a1_ref, ...), custom_call_target="tpu_custom_call" | custom-call | tf_op jit(solution)/shard_map/pallas_call | solution.py:282
  80.0 21.7 %all_to_all.15.back_ref = bf16[8,336,128]{2,1,0:T(8,128)(2,1)S(1)} all-to-all(bf16[8,336,128]{2,1,0:T(8,128)(2,1)S(1)} %shard_map.85), channel_id=1, replica_groups=mesh['frame'=8,'mp'=4] {'frame'}, dimensions={0} | all-to-all | bytes 1376256 | tf_op jit(solution)/shard_map/all_to_all | solution.py:291
  101.7 1.5 %shard_map.86 = bf16[256,1280]{1,0:T(8,128)(2,1)} custom-call(f32[256,1280]{1,0:T(8,128)S(1)} %copy-done.6, bf16[8,336,128]{2,1,0:T(8,128)(2,1)S(1)} %all_to_all.15.back_ref), custom_call_target="tpu_custom_call" | custom-call | tf_op jit(solution)/shard_map/pallas_call | solution.py:282
  (59 shorter events, 5.0 us)
Async XLA Ops:
  0.0 1.1 %copy-start = (bf16[256,1280]{1,0:T(8,128)(2,1)S(1)}, bf16[256,1280]{1,0:T(8,128)(2,1)}, u32[]{:S(2)}) copy-start(bf16[256,1280]{1,0:T(8,128)(2,1)} %k_ref.5) | copy-start | bytes 1966084
  1.1 1.1 %copy-start.2 = (bf16[256,1280]{1,0:T(8,128)(2,1)S(1)}, bf16[256,1280]{1,0:T(8,128)(2,1)}, u32[]{:S(2)}) copy-start(bf16[256,1280]{1,0:T(8,128)(2,1)} %v_ref.3) | copy-start | bytes 1966084
  3.4 7.4 %copy-start.1 = (bf16[256,1280]{1,0:T(8,128)(2,1)S(1)}, bf16[256,1280]{1,0:T(8,128)(2,1)}, u32[]{:S(2)}) copy-start(bf16[256,1280]{1,0:T(8,128)(2,1)} %k_ref.5) | copy-start | bytes 1966084
  3.4 7.4 %copy-start.4 = (bf16[256,1280]{1,0:T(8,128)(2,1)S(1)}, bf16[256,1280]{1,0:T(8,128)(2,1)}, u32[]{:S(2)}) copy-start(bf16[256,1280]{1,0:T(8,128)(2,1)} %q_ref.3) | copy-start | bytes 1966084
  3.4 38.8 %all-to-all-start.1 = ((bf16[8,64,1280]{2,1,0:T(8,128)(2,1)}), bf16[8,64,1280]{2,1,0:T(8,128)(2,1)S(1)}, u32[]{:S(2)}, u32[]{:S(2)}) async-start(bf16[8,64,1280]{2,1,0:T(8,128)(2,1)} %shard_map.84), calls=%async_computation.1 | async-start | bytes 2621440 | tf_op jit(solution)/shard_map/all_to_all | solution.py:291
  10.8 2.2 %copy-start.9 = (s32[1,2,2]{2,1,0:T(2,128)S(1)}, s32[1,2,2]{2,1,0:T(2,128)}, u32[]{:S(2)}) copy-start(s32[1,2,2]{2,1,0:T(2,128)} %param.13) | copy-start | bytes 52
  10.8 4.1 %copy-start.8 = (f32[1280]{0:T(1024)S(1)}, f32[1280]{0:T(1024)}, u32[]{:S(2)}) copy-start(f32[1280]{0:T(1024)} %param.11) | copy-start | bytes 15364
  10.9 4.1 %copy-start.7 = (f32[1280]{0:T(1024)S(1)}, f32[1280]{0:T(1024)}, u32[]{:S(2)}) copy-start(f32[1280]{0:T(1024)} %param.12) | copy-start | bytes 15364
  10.9 5.1 %copy-start.3 = (bf16[256,1280]{1,0:T(8,128)(2,1)S(1)}, bf16[256,1280]{1,0:T(8,128)(2,1)}, u32[]{:S(2)}) copy-start(bf16[256,1280]{1,0:T(8,128)(2,1)} %v_ref.3) | copy-start | bytes 1966084
  11.2 3.8 %collective-permute-start.2 = (f32[8,256]{1,0:T(8,128)S(1)}, f32[8,256]{1,0:T(8,128)S(1)}, u32[]{:S(2)}, u32[]{:S(2)}) collective-permute-start(f32[8,256]{1,0:T(8,128)S(1)} %shard_map.82), channel_id=1, source_target_pairs={{0,3},{1,0},{2,1},{3,2},{4,7},{5,4},{6,5},{7,6},{8,11},{9,8},{10,9... | collective-permute-start | bytes 24584 | tf_op jit(solution)/shard_map/ppermute | solution.py:332
  11.9 3.7 %collective-permute-start.1 = (f32[8,256]{1,0:T(8,128)S(1)}, f32[8,256]{1,0:T(8,128)S(1)}, u32[]{:S(2)}, u32[]{:S(2)}) collective-permute-start(f32[8,256]{1,0:T(8,128)S(1)} %shard_map.82), channel_id=1, source_target_pairs={{0,2},{1,3},{2,0},{3,1},{4,6},{5,7},{6,4},{7,5},{8,10},{9,11},{10,... | collective-permute-start | bytes 24584 | tf_op jit(solution)/shard_map/ppermute | solution.py:332
  12.9 3.1 %collective-permute-start = (f32[8,256]{1,0:T(8,128)S(1)}, f32[8,256]{1,0:T(8,128)S(1)}, u32[]{:S(2)}, u32[]{:S(2)}) collective-permute-start(f32[8,256]{1,0:T(8,128)S(1)} %shard_map.82), channel_id=1, source_target_pairs={{0,1},{1,2},{2,3},{3,0},{4,5},{5,6},{6,7},{7,4},{8,9},{9,10},{10,1... | collective-permute-start | bytes 24584 | tf_op jit(solution)/shard_map/ppermute | solution.py:332
  16.0 29.8 %copy-start.10 = (s32[1,2,2]{2,1,0:T(2,128)S(1)}, s32[1,2,2]{2,1,0:T(2,128)}, u32[]{:S(2)}) copy-start(s32[1,2,2]{2,1,0:T(2,128)} %param.14) | copy-start | bytes 52
  18.3 1.1 %copy-start.5 = (f32[256,1280]{1,0:T(8,128)}, f32[256,1280]{1,0:T(8,128)S(1)}, u32[]{:S(2)}) copy-start(f32[256,1280]{1,0:T(8,128)S(1)} %get-tuple-element.7.own_ref) | copy-start | bytes 3932164
  42.2 27.4 %all-to-all-start = ((bf16[8,336,128]{2,1,0:T(8,128)(2,1)}), bf16[8,336,128]{2,1,0:T(8,128)(2,1)S(1)}, u32[]{:S(2)}, u32[]{:S(2)}) async-start(bf16[8,336,128]{2,1,0:T(8,128)(2,1)} %get-tuple-element.8), calls=%async_computation | async-start | bytes 1376256 | tf_op jit(solution)/shard_map/all_to_all | solution.py:291
  46.2 6.0 %collective-permute-start.6 = (f32[16,256]{1,0:T(8,128)S(1)}, f32[16,256]{1,0:T(8,128)S(1)}, u32[]{:S(2)}, u32[]{:S(2)}) collective-permute-start(f32[16,256]{1,0:T(8,128)S(1)} %dynamic_update_slice.7), channel_id=1, source_target_pairs={{0,4},{4,0},{8,12},{12,8},{16,20},{20,16},{24,28},{28,24},{1,5},{5... | collective-permute-start | bytes 49160 | tf_op jit(solution)/shard_map/ppermute | solution.py:296
  52.3 5.3 %collective-permute-start.7 = (f32[16,256]{1,0:T(8,128)S(1)}, f32[16,256]{1,0:T(8,128)S(1)}, u32[]{:S(2)}, u32[]{:S(2)}) collective-permute-start(f32[16,256]{1,0:T(8,128)S(1)} %add.71), channel_id=1, source_target_pairs={{0,8},{4,12},{8,0},{12,4},{16,24},{20,28},{24,16},{28,20},{1,9},{5... | collective-permute-start | bytes 49160 | tf_op jit(solution)/shard_map/ppermute | solution.py:296
  57.6 7.1 %collective-permute-start.8 = (f32[16,256]{1,0:T(8,128)S(1)}, f32[16,256]{1,0:T(8,128)S(1)}, u32[]{:S(2)}, u32[]{:S(2)}) collective-permute-start(f32[16,256]{1,0:T(8,128)S(1)} %add.72), channel_id=1, source_target_pairs={{0,16},{4,20},{8,24},{12,28},{16,0},{20,4},{24,8},{28,12},{1,17},{... | collective-permute-start | bytes 49160 | tf_op jit(solution)/shard_map/ppermute | solution.py:296
  65.3 7.1 %collective-permute-start.3 = (bf16[64,1280]{1,0:T(8,128)(2,1)S(1)}, bf16[64,1280]{1,0:T(8,128)(2,1)S(1)}, u32[]{:S(2)}, u32[]{:S(2)}) collective-permute-start(bf16[64,1280]{1,0:T(8,128)(2,1)S(1)} %dynamic-slice_bitcast_fusion.a0_ref), channel_id=1, source_target_pairs={{0,4},{4,0},{8,12},{12,8},{16,20},{20,16},{24,28},{28,24},{1,5},{5... | collective-permute-start | bytes 491528 | tf_op jit(solution)/shard_map/ppermute | solution.py:296
  66.8 6.5 %collective-permute-start.4 = (bf16[64,1280]{1,0:T(8,128)(2,1)S(1)}, bf16[64,1280]{1,0:T(8,128)(2,1)S(1)}, u32[]{:S(2)}, u32[]{:S(2)}) collective-permute-start(bf16[64,1280]{1,0:T(8,128)(2,1)S(1)} %dynamic-slice_bitcast_fusion.a0_ref), channel_id=1, source_target_pairs={{0,8},{4,12},{8,0},{12,4},{16,24},{20,28},{24,16},{28,20},{1,9},{5... | collective-permute-start | bytes 491528 | tf_op jit(solution)/shard_map/ppermute | solution.py:296
  67.2 7.6 %collective-permute-start.5 = (bf16[64,1280]{1,0:T(8,128)(2,1)S(1)}, bf16[64,1280]{1,0:T(8,128)(2,1)S(1)}, u32[]{:S(2)}, u32[]{:S(2)}) collective-permute-start(bf16[64,1280]{1,0:T(8,128)(2,1)S(1)} %dynamic-slice_bitcast_fusion.a0_ref), channel_id=1, source_target_pairs={{0,12},{4,8},{8,4},{12,0},{16,28},{20,24},{24,20},{28,16},{1,13},{... | collective-permute-start | bytes 491528 | tf_op jit(solution)/shard_map/ppermute | solution.py:296
  80.0 21.7 %copy-start.6 = (f32[256,1280]{1,0:T(8,128)S(1)}, f32[256,1280]{1,0:T(8,128)}, u32[]{:S(2)}) copy-start(f32[256,1280]{1,0:T(8,128)} %copy-done.5) | copy-start | bytes 3932164

commit v4 on v0

--- a/solution.py
+++ b/solution.py
@@ -1,11 +1,17 @@
+import functools
+
 import jax
 import jax.numpy as jnp
 from jax import lax
+from jax.experimental import pallas as pl
+from jax.experimental.pallas import tpu as pltpu
 from jax.sharding import PartitionSpec as P
 
 D = 5120
 HD = 128
 BLOCK = 128
+LOG2E = 1.4426950408889634
+NEG = -1e30
 
 
 def spread(value, axis, source):
@@ -39,7 +45,9 @@
     return jnp.transpose(output, (1, 0, 2)).reshape(rows, width)
 
 
-def local(q_raw, k_raw, values, q_gain, k_gain, spatial_mask, temporal_mask, anchor_frame):
+def local_general(
+    q_raw, k_raw, values, q_gain, k_gain, spatial_mask, temporal_mask, anchor_frame
+):
     frame_tok = q_raw.shape[0]
     width = q_raw.shape[1]
     q_float = q_raw.astype(jnp.float32)
@@ -51,29 +59,16 @@
     k_norm = (k_float / jnp.sqrt(sum_k[:, None] / D + 1e-06) * k_gain[None, :]).astype(jnp.bfloat16)
     n_frames = lax.axis_size("frame")
     group_pos = frame_tok // n_frames
-    q_pencil, k_pencil, v_pencil = (
-        lax.all_to_all(
-            q_norm.reshape(n_frames, group_pos, width),
+
+    def regroup(array):
+        return lax.all_to_all(
+            array.reshape(n_frames, group_pos, width),
             "frame",
             split_axis=0,
             concat_axis=0,
             tiled=True,
-        ),
-        lax.all_to_all(
-            k_norm.reshape(n_frames, group_pos, width),
-            "frame",
-            split_axis=0,
-            concat_axis=0,
-            tiled=True,
-        ),
-        lax.all_to_all(
-            values.reshape(n_frames, group_pos, width),
-            "frame",
-            split_axis=0,
-            concat_axis=0,
-            tiled=True,
-        ),
-    )
+        ).reshape(frame_tok, width)
+
     anchor = anchor_frame[0]
     k_anchor, v_anchor = (spread(k_norm, "frame", anchor), spread(values, "frame", anchor))
     own_allowed = jnp.concatenate(
@@ -86,19 +81,485 @@
         own_allowed,
     )
     temporal = attend(
-        q_pencil.reshape(frame_tok, width),
-        k_pencil.reshape(frame_tok, width),
-        v_pencil.reshape(frame_tok, width),
-        expand(temporal_mask[0]),
-    )
-    temporal = temporal.astype(jnp.bfloat16).reshape(n_frames, group_pos, width)
-    returned = lax.all_to_all(temporal, "frame", split_axis=0, concat_axis=0, tiled=True).reshape(
-        frame_tok, width
-    )
+        regroup(q_norm), regroup(k_norm), regroup(values), expand(temporal_mask[0])
+    ).astype(jnp.bfloat16)
+    returned = regroup(temporal)
     return (spatial + returned.astype(jnp.float32)).astype(jnp.bfloat16)
 
 
+ROWS = 16
+MASK_ROW = 12
+
+
+def dot_t(a, b):
+    return lax.dot_general(a, b, (((1,), (1,)), ((), ())), preferred_element_type=jnp.float32)
+
+
+def weigh(weights, vals):
+    ones = jnp.ones(vals.shape, vals.dtype)
+    both = jnp.dot(
+        weights.astype(jnp.bfloat16),
+        jnp.concatenate([vals, ones], axis=1),
+        preferred_element_type=jnp.float32,
+    )
+    return both[:, :HD], both[:, HD:]
+
+
+def blocked_scores(query, keys, flag, i):
+    scores = dot_t(query, keys)
+    near = scores[:, i * BLOCK : (i + 1) * BLOCK]
+    away = scores[:, (1 - i) * BLOCK : (2 - i) * BLOCK] + flag
+    return jnp.concatenate([near, away] if i == 0 else [away, near], axis=1)
+
+
+def scaled(rows, column, gain):
+    return (rows.astype(jnp.float32) * column * gain).astype(jnp.bfloat16)
+
+
+def first_kernel(n, pos, q_ref, k_ref, v_ref, sum_ref, out_ref, held, cut, sems, v_sems):
+    tok = q_ref.shape[0]
+    chunks = sems.shape[1]
+    parts = tok // pos
+    step = tok // chunks
+    copies = []
+    for t, ref in enumerate((q_ref, k_ref)):
+        for c in range(chunks):
+            rows = pl.ds(c * step, step)
+            copies.append(pltpu.make_async_copy(ref.at[rows], held.at[t, rows], sems.at[t, c]))
+    loads, stores = [], []
+    for d in range(n):
+        heads = ((d, 0, tok, 0), (n + d // parts, d % parts * pos, pos, tok))
+        for j, (head, row, rows, at) in enumerate(heads):
+            loads.append(
+                pltpu.make_async_copy(
+                    v_ref.at[pl.ds(row, rows), pl.ds(head * HD, HD)],
+                    cut.at[d, pl.ds(at, rows)],
+                    v_sems.at[j, d],
+                )
+            )
+        stores.append(pltpu.make_async_copy(cut.at[d], out_ref.at[d], v_sems.at[2, d]))
+    for copy in copies + loads:
+        copy.start()
+    rows = []
+    for t in range(2):
+        parts = []
+        for c in range(chunks):
+            copies[t * chunks + c].wait()
+            total = None
+            for h in range(q_ref.shape[1] // HD):
+                part = held[t, c * step : (c + 1) * step, h * HD : (h + 1) * HD]
+                part = part.astype(jnp.float32)
+                total = part * part if total is None else total + part * part
+            parts.append(total)
+        rows.append(jnp.sum(jnp.concatenate(parts, axis=0).T, axis=0, keepdims=True))
+    sum_ref[...] = jnp.concatenate(rows + [jnp.zeros((6, tok), jnp.float32)], axis=0)
+    for copy in loads:
+        copy.wait()
+    for copy in stores:
+        copy.start()
+    for copy in stores:
+        copy.wait()
+
+
+def copy_kernel(in_ref, out_ref):
+    out_ref[...] = in_ref[...]
+
+
+def own_kernel(n, pos, *refs):
+    args, blocks, own_ref = refs[:11], refs[11 : 11 + n], refs[11 + n]
+    ins, held, extra, own, sums, gains, masks, in_sems, out_sems = refs[12 + n :]
+    q_ref, k_ref, v_ref = args[:3]
+    tok = q_ref.shape[0]
+    heads = q_ref.shape[1] // HD
+    parts = tok // pos
+    me = lax.axis_index("frame")
+    order = [n + e for e in range(heads - n)] + [me ^ s for s in range(n)]
+
+    def cols(h):
+        return pl.ds(pl.multiple_of(h * HD, HD), HD)
+
+    small = []
+    for j in range(4):
+        small.append(pltpu.make_async_copy(args[3 + j], sums.at[j], in_sems.at[3 * heads + j]))
+    for j in range(2):
+        at = in_sems.at[3 * heads + 4 + j]
+        small.append(pltpu.make_async_copy(args[7 + j], gains.at[j], at))
+        at = in_sems.at[3 * heads + 6 + j]
+        small.append(pltpu.make_async_copy(args[9 + j], masks.at[j], at))
+    loads = [
+        pltpu.make_async_copy(ref.at[:, cols(h)], ins.at[t, x], in_sems.at[3 * x + t])
+        for x, h in enumerate(order)
+        for t, ref in enumerate((q_ref, k_ref, v_ref))
+    ]
+    for copy in small + loads:
+        copy.start()
+    for copy in small:
+        copy.wait()
+    inv = lax.rsqrt((sums[0] + sums[1] + sums[2] + sums[3]) / D + 1e-06).T
+    inv_q = jnp.broadcast_to(inv[:, 0:1] * (LOG2E / float(HD) ** 0.5), (tok, HD))
+    inv_k = jnp.broadcast_to(inv[:, 1:2], (tok, HD))
+    flags = [jnp.where(masks[0, i, 1 - i] == 1, 0.0, NEG) for i in range(2)]
+    lane = lax.broadcasted_iota(jnp.int32, (BLOCK, HD), 1)
+    lses = [jnp.zeros((BLOCK, HD), jnp.float32) for _ in range(tok // BLOCK)]
+    stores = []
+    for x, h in enumerate(order):
+        if x in (0, heads // 2):
+            for copy in loads[3 * x : 3 * (x + heads // 2)]:
+                copy.wait()
+        query = scaled(ins[0, x], inv_q, gains[0, pl.ds(h, 1), :])
+        keys = scaled(ins[1, x], inv_k, gains[1, pl.ds(h, 1), :])
+        vals = ins[2, x]
+        for t, array in enumerate((query, keys)):
+            if x < heads - n:
+                extra[x, t] = array
+            else:
+                s = x - (heads - n)
+                held[s, t * tok : (t + 1) * tok, :] = array
+                at = 2 * tok + t * pos
+                rows = pl.ds(pl.multiple_of((me ^ s) % parts * pos, pos), pos)
+                held[s, at : at + pos, :] = extra[(me ^ s) // parts, t, rows, :]
+        if x >= heads - n:
+            rows = pl.ds(0, 2 * (tok + pos))
+            stores.append(
+                pltpu.make_async_copy(held.at[s, rows], blocks[s].at[rows], out_sems.at[x])
+            )
+            stores[-1].start()
+        for i in range(tok // BLOCK):
+            rows = slice(i * BLOCK, (i + 1) * BLOCK)
+            scores = blocked_scores(query[rows], keys, flags[i], i)
+            top = jnp.max(scores, axis=1, keepdims=True)
+            out, weight = weigh(jnp.exp2(scores - top), vals)
+            own[x, rows, :] = out / weight
+            lses[i] = jnp.where(lane == x, top + jnp.log2(weight), lses[i])
+        stores.append(
+            pltpu.make_async_copy(own.at[x], own_ref.at[:, cols(h)], out_sems.at[heads + x])
+        )
+        stores[-1].start()
+    pieces = []
+    for lse in lses:
+        rest = lse.T[:ROWS]
+        split = []
+        for _ in range(3):
+            split.append(rest.astype(jnp.bfloat16).astype(jnp.float32))
+            rest = rest - split[-1]
+        pieces.append(split)
+    pad = jnp.zeros((ROWS - 1 - MASK_ROW, HD), jnp.float32)
+    lane = lax.broadcasted_iota(jnp.int32, (1, HD), 1)
+    mask = jnp.where(lane == 0, masks[1, 0, 1], masks[1, 1, 0])
+    mask = (mask == 1).astype(jnp.float32)
+    at = 2 * (tok + pos)
+    for s in range(n):
+        late = (me ^ s) // parts == 1
+        rows = []
+        for split in pieces:
+            rows += [piece[s + heads - n : s + heads - n + 1, :] for piece in split]
+        for split in pieces:
+            rows += [jnp.where(late, piece[1:2, :], piece[0:1, :]) for piece in split]
+        side = jnp.concatenate(rows + [mask, pad], axis=0)
+        held[s, at : at + ROWS, :] = side.astype(jnp.bfloat16)
+        rows = pl.ds(at, ROWS)
+        stores.append(
+            pltpu.make_async_copy(held.at[s, rows], blocks[s].at[rows], out_sems.at[2 * heads + s])
+        )
+        stores[-1].start()
+    for copy in stores:
+        copy.wait()
+
+
+def pencil(n, query, keys, vals, lse, anchor_keys, anchor_vals, flags, put):
+    keep = []
+    for i in range(query.shape[0] // BLOCK):
+        rows = slice(i * BLOCK, (i + 1) * BLOCK)
+        scores = blocked_scores(query[rows], keys, flags[i], i)
+        top = jnp.max(scores, axis=1, keepdims=True)
+        out, total = weigh(jnp.exp2(scores - top), vals)
+        temporal = out / total
+        scores = dot_t(query[rows], anchor_keys)
+        top = jnp.maximum(jnp.max(scores, axis=1, keepdims=True), lse[rows])
+        own = jnp.exp2(lse[rows] - top)
+        out, total = weigh(jnp.exp2(scores - top), anchor_vals)
+        scale = 1.0 / (total + own)
+        result = (temporal + out * scale).astype(jnp.bfloat16)
+        keep.append(own * scale)
+        gp = query.shape[0] // n
+        for j in range(BLOCK // gp):
+            put(i * (BLOCK // gp) + j, result[j * gp : (j + 1) * gp])
+    return jnp.concatenate(keep, axis=0)
+
+
+def add_side(side, keep, gp, first):
+    n = side.shape[0]
+    lane = lax.broadcasted_iota(jnp.int32, side.shape, 2)
+    keep = keep.reshape(n, gp, HD)
+    for g in range(gp // ROWS):
+        side = jnp.where(lane == first + g, keep[:, g * ROWS : (g + 1) * ROWS, :], side)
+    return side
+
+
+def read_side(blocks, at, which, mask_ref):
+    rows, masks = [], []
+    for block in blocks:
+        side = block[at : at + ROWS, :].astype(jnp.float32)
+        for half in range(2):
+            first = 6 * which + 3 * half
+            rows.append(
+                side[first : first + 1] + side[first + 1 : first + 2] + side[first + 2 : first + 3]
+            )
+        masks.append(side[MASK_ROW : MASK_ROW + 1])
+    mask_ref[...] = jnp.concatenate(masks, axis=0)
+    rows.append(jnp.zeros((HD - len(rows), HD), jnp.float32))
+    return jnp.concatenate(rows, axis=0).T
+
+
+def pencil_flags(mask_ref, row, upper):
+    mask = mask_ref[pl.ds(row, 1), :]
+    flags = [jnp.where(mask[:, i : i + 1] == 1.0, 0.0, NEG) for i in range(2)]
+    return [jnp.where(upper, flags[1 - i], flags[i]) for i in range(2)]
+
+
+def whole_kernel(n, tok, pos, at_ref, *refs):
+    v_ref, blocks, outs, side_ref = refs[0], refs[1 : n + 1], refs[n + 1 : 2 * n + 1], refs[2 * n + 1]
+    held_ref, mask_ref = refs[2 * n + 2 :]
+    gp = tok // n
+    me = lax.axis_index("frame")
+    for s in range(n):
+
+        @pl.when(at_ref[0] == me ^ s)
+        def _():
+            held_ref[...] = blocks[s][tok : 2 * tok, :]
+
+    ka, va = held_ref[...], v_ref[at_ref[0], :tok, :]
+    lses = read_side(blocks, 2 * (tok + pos), 0, mask_ref)
+    upper = me >= n // 2
+    side = jnp.zeros((n, ROWS, HD), jnp.float32)
+    for g in range(n):
+
+        def rows(at):
+            return jnp.concatenate(
+                [block[at + g * gp : at + (g + 1) * gp, :] for block in blocks], axis=0
+            )
+
+        def put(s, result):
+            outs[s][g * gp : (g + 1) * gp, :] = result
+
+        vals = [v_ref[me ^ s, g * gp : (g + 1) * gp, :] for s in range(n)]
+        half, first = g * gp // BLOCK, g * gp % BLOCK
+        lse = [lses[first : first + gp, 2 * s + half : 2 * s + half + 1] for s in range(n)]
+        keep = pencil(
+            n,
+            rows(0),
+            rows(tok),
+            jnp.concatenate(vals, axis=0),
+            jnp.concatenate(lse, axis=0),
+            ka,
+            va,
+            pencil_flags(mask_ref, g ^ me, upper),
+            put,
+        )
+        side = add_side(side, keep, gp, g * gp // ROWS)
+    side_ref[...] = side
+
+
+def part_kernel(n, tok, pos, *refs):
+    v_ref, refs = refs[0], refs[1:]
+    blocks, held = refs[:n], refs[n : n + 4]
+    done, came_ref = refs[n + 4 : 2 * n + 4], refs[2 * n + 4]
+    outs = refs[2 * n + 5 : 3 * n + 5]
+    lse_ref, mask_ref = refs[3 * n + 5 :]
+    gp = tok // n
+    me = lax.axis_index("frame")
+    quarter = me % (tok // pos)
+    per_block = BLOCK // pos
+    for s in range(n):
+        outs[s][:tok, :] = done[s][...]
+    ka = jnp.concatenate([a[:pos, :] for a in held], axis=0)
+    va = jnp.concatenate([a[pos:, :] for a in held], axis=0)
+    lse_ref[...] = read_side(blocks, 2 * (tok + pos), 1, mask_ref)
+    upper = me >= n // 2
+    late = quarter >= per_block
+    side = came_ref[...]
+    for u in range(pos // gp):
+
+        def rows(at):
+            return jnp.concatenate(
+                [block[at + u * gp : at + (u + 1) * gp, :] for block in blocks], axis=0
+            )
+
+        def put(s, result):
+            outs[s][tok + u * gp : tok + (u + 1) * gp, :] = result
+
+        at = tok + u * gp
+        vals = [v_ref[me ^ s, at : at + gp, :] for s in range(n)]
+        first = pl.multiple_of(quarter % per_block * pos + u * gp, gp)
+        lses = lse_ref[pl.ds(first, gp), :]
+        lse = [
+            jnp.where(late, lses[:, 2 * s + 1 : 2 * s + 2], lses[:, 2 * s : 2 * s + 1])
+            for s in range(n)
+        ]
+        keep = pencil(
+            n,
+            rows(2 * tok),
+            rows(2 * tok + pos),
+            jnp.concatenate(vals, axis=0),
+            jnp.concatenate(lse, axis=0),
+            ka,
+            va,
+            pencil_flags(mask_ref, (quarter * (pos // gp) + u) ^ me, upper),
+            put,
+        )
+        side = add_side(side, keep, gp, (tok + u * gp) // ROWS)
+    for s in range(n):
+        outs[s][tok + pos : tok + pos + ROWS, :] = side[s].astype(jnp.bfloat16)
+
+
+def join_kernel(n, pos, own_ref, *refs):
+    back, out_ref = refs[:n], refs[n]
+    tok = own_ref.shape[0]
+    parts = tok // pos
+    me = lax.axis_index("frame")
+    for s in range(n):
+        d = me ^ s
+        side = back[s][tok + pos : tok + pos + ROWS, :].astype(jnp.float32)
+        row = pl.multiple_of(d % parts * pos, pos)
+        for head, rows, at in ((d, pl.ds(0, tok), 0), (n + d // parts, pl.ds(row, pos), tok)):
+            cols = pl.ds(pl.multiple_of(head * HD, HD), HD)
+            keep = [side[:, g : g + 1] for g in range(at // ROWS, (at + rows.size) // ROWS)]
+            keep = jnp.concatenate(keep, axis=0)
+            got = back[s][at : at + rows.size, :].astype(jnp.float32)
+            out_ref[rows, cols] = (own_ref[rows, cols] * keep + got).astype(jnp.bfloat16)
+
+
+def call(kernel, out_shape, *args, vmem=40, **more):
+    return pl.pallas_call(
+        kernel,
+        out_shape=out_shape,
+        compiler_params=pltpu.CompilerParams(vmem_limit_bytes=vmem * 1024 * 1024),
+        **more,
+    )(*args)
+
+
+def pairwise(array, axis, step):
+    size = lax.axis_size(axis)
+    return lax.ppermute(array, axis, [(i, i ^ step) for i in range(size)])
+
+
+def swap_blocks(blocks):
+    n = len(blocks)
+    got = {0: blocks[0]}
+    wide = sorted(range(n // 2, n), key=lambda s: (s % 2, s))
+    for s in wide + [1, 2]:
+        got[s] = pairwise(blocks[s], "frame", s)
+    for s in range(3, n // 2):
+        block, _ = lax.optimization_barrier((blocks[s], got[s - 1]))
+        got[s] = pairwise(block, "frame", s)
+    return [got[s] for s in range(n)]
+
+
+def local_heads(
+    q_raw, k_raw, values, q_gain, k_gain, spatial_mask, temporal_mask, anchor_frame
+):
+    tok, width = q_raw.shape
+    n = lax.axis_size("frame")
+    n_mp = lax.axis_size("mp")
+    heads = width // HD
+    parts = n // (heads - n)
+    pos = tok // parts
+    me = lax.axis_index("frame")
+    shape = jax.ShapeDtypeStruct
+    vm = pl.BlockSpec(memory_space=pltpu.VMEM)
+    sm = pl.BlockSpec(memory_space=pltpu.SMEM)
+    hbm = pl.BlockSpec(memory_space=pltpu.HBM)
+    dma = pltpu.SemaphoreType.DMA
+    bf16, f32 = jnp.bfloat16, jnp.float32
+
+    sums, v_blocks = call(
+        functools.partial(first_kernel, n, pos),
+        (shape((8, tok), f32), shape((n, tok + pos, HD), bf16)),
+        q_raw,
+        k_raw,
+        values,
+        in_specs=[hbm] * 3,
+        out_specs=(vm, hbm),
+        scratch_shapes=[
+            pltpu.VMEM((2, tok, width), bf16),
+            pltpu.VMEM((n, tok + pos, HD), bf16),
+            dma((2, 4)),
+            dma((3, n)),
+        ],
+        vmem=60,
+    )
+    v_far = lax.all_to_all(v_blocks, "frame", split_axis=0, concat_axis=0, tiled=True)
+    all_sums = [sums] + [pairwise(sums, "mp", step) for step in range(1, n_mp)]
+    rows = 2 * (tok + pos) + ROWS
+    *sent, own = call(
+        functools.partial(own_kernel, n, pos),
+        [shape((rows, HD), bf16)] * n + [shape((tok, width), f32)],
+        q_raw,
+        k_raw,
+        values,
+        *all_sums,
+        q_gain.reshape(heads, HD),
+        k_gain.reshape(heads, HD),
+        spatial_mask[0],
+        temporal_mask[0],
+        in_specs=[hbm] * 11,
+        out_specs=[hbm] * (n + 1),
+        scratch_shapes=[
+            pltpu.VMEM((3, heads, tok, HD), bf16),
+            pltpu.VMEM((n, rows, HD), bf16),
+            pltpu.VMEM((heads - n, 2, tok, HD), bf16),
+            pltpu.VMEM((heads, tok, HD), f32),
+            pltpu.VMEM((4, 8, tok), f32),
+            pltpu.VMEM((2, heads, HD), f32),
+            pltpu.SMEM((2, 2, 2), jnp.int32),
+            dma((3 * heads + 8,)),
+            dma((2 * heads + n,)),
+        ],
+        vmem=60,
+    )
+    far = swap_blocks(sent)
+
+    anchor = anchor_frame[0]
+    part = slice(2 * tok + pos, 2 * (tok + pos))
+    mine = far[0][part]
+    for s in range(1, n):
+        mine = jnp.where(anchor == me ^ s, far[s][part], mine)
+    v_mine = lax.dynamic_slice(v_far, (anchor, tok, 0), (1, pos, HD))[0]
+    mine = jnp.concatenate([mine, v_mine], axis=0)
+    held = [mine] + [pairwise(mine, "frame", step) for step in range(1, parts)]
+    *done, weights = call(
+        functools.partial(whole_kernel, n, tok, pos),
+        [shape((tok, HD), bf16)] * n + [shape((n, ROWS, HD), f32)],
+        anchor_frame,
+        v_far,
+        *far,
+        in_specs=[sm] + [vm] * (n + 1),
+        scratch_shapes=[pltpu.VMEM((tok, HD), bf16), pltpu.VMEM((n, HD), f32)],
+    )
+    result = call(
+        functools.partial(part_kernel, n, tok, pos),
+        [shape((tok + pos + ROWS, HD), bf16)] * n,
+        v_far,
+        *far,
+        *held,
+        *done,
+        weights,
+        scratch_shapes=[pltpu.VMEM((HD, HD), f32), pltpu.VMEM((n, HD), f32)],
+    )
+    back = swap_blocks(result)
+    return call(
+        functools.partial(join_kernel, n, pos), shape((tok, width), bf16), own, *back
+    )
+
+
 def solution(mesh):
+    n = mesh.shape["frame"]
+
+    def local(*args):
+        tok, width = args[0].shape
+        fits = n == 8 and mesh.shape["mp"] == 4 and width == 10 * HD and tok == 2 * BLOCK
+        return local_heads(*args) if fits else local_general(*args)
+
     return jax.shard_map(
         local,
         mesh=mesh,

time: 201 us -> 85.5 us (0.43)
  matrix products: 50.3 us -> 0 us
  waiting for transfers between devices: 79.8 us -> 30.4 us
  starting transfers between devices: 17.9 us -> 37.7 us
  local copies, waits for them, and re-layouts: 17.7 us -> 1.53 us
  Pallas kernels: 0 us -> 14 us
  between operations: 14.3 us -> 0.79 us
  other arithmetic: 10.7 us -> 0.74 us
  blocking collectives: 8.37 us -> 0 us
    dot_general x40 -> x0, matrix products: 50.3 us -> none  [the longest x20 36 us: one_head(): return jnp.dot(probs, head_v, preferred_element_type=jnp.float32)]
    all_to_all x4 -> x1, waiting for transfers between devices: 45 us -> 0.01 us  [local_heads(): lax.all_to_all(v_blocks, 'frame', split_axis=0, concat_axis=0, tiled=True)]
    psum x1 -> x0, waiting for transfers between devices: 34.8 us -> none  [spread(): return lax.psum(kept, axis)]
    ppermute x0 -> x20, starting transfers between devices: none -> 30.5 us  [pairwise(): return lax.ppermute(array, axis, [(i, i ^ step) for i in range(size)])]
    ppermute x0 -> x20, waiting for transfers between devices: none -> 30.4 us  [pairwise(): return lax.ppermute(array, axis, [(i, i ^ step) for i in range(size)])]
    pallas_call x0 -> x5, Pallas kernels: none -> 14 us  [call(): pl.pallas_call(kernel, out_shape=out_shape, compiler_params=pltpu.Compile...]
    all_to_all x4 -> x1, starting transfers between devices: 17.9 us -> 7.27 us  [local_heads(): lax.all_to_all(v_blocks, 'frame', split_axis=0, concat_axis=0, tiled=True)]
    psum x1 -> x0, blocking collectives: 8.37 us -> none  [local(): lax.psum((jnp.sum(q_float * q_float, axis=1), jnp.sum(k_float * k_float,...]
  transfers between devices with their start and end apart: 5 -> 21, of which waited for: 4 -> 9; matrix products, arithmetic and copies ran while one was open for 35% -> 1% of each run, Pallas kernels for 0% -> 9%
where the time goes in v4:
time: 85.5 us; the launch traced here: 85.1 us
  starting transfers between devices  37.7 us (44%)
  waiting for transfers between devices  30.4 us (36%)
  Pallas kernels  14 us (16%)
  local copies, waits for them, and re-layouts  1.53 us (2%)
    ppermute x20, starting transfers between devices, pairwise(): return lax.ppermute(array, axis, [(i, i ^ step) for i in range(size)])  30.5 us
    ppermute x20, waiting for transfers between devices, pairwise(): return lax.ppermute(array, axis, [(i, i ^ step) for i in range(size)])  30.4 us
    pallas_call x5, Pallas kernels, call(): pl.pallas_call(kernel, out_shape=out_shape, compiler_params=pltpu.Compile...  14 us
    all_to_all x1, starting transfers between devices, local_heads(): lax.all_to_all(v_blocks, 'frame', split_axis=0, concat_axis=0, tiled=True)  7.27 us
  transfers between devices with their start and end apart: 21, of which 9 were waited for; matrix products, arithmetic and copies ran while one was open for 1% of the time, Pallas kernels for 9%

profile of v4, /device:TPU:0, one launch (start us, length us, event | category | flops | bytes accessed | tf_op | source)
XLA Modules:
  0.0 85.1 jit_solution(15651638879917819645)
XLA Ops:
  0.0 3.4 %shard_map.82 = (f32[8,256]{1,0:T(8,128)}, bf16[8,320,128]{2,1,0:T(8,128)(2,1)}) custom-call(bf16[256,1280]{1,0:T(8,128)(2,1)} %refs_0_.1, bf16[256,1280]{1,0:T(8,128)(2,1)} %refs_1_.1, bf16[256,1280]{1,0:T(8,128)(2,1)} %refs_2_.1), custom_call_target="tpu_custom_call" | custom-call | tf_op jit(solution)/shard_map/pallas_call | solution.py:433
  3.5 7.3 %all-to-all-start = ((bf16[8,320,128]{2,1,0:T(8,128)(2,1)}), bf16[8,320,128]{2,1,0:T(8,128)(2,1)S(1)}, u32[]{:S(2)}, u32[]{:S(2)}) async-start(bf16[8,320,128]{2,1,0:T(8,128)(2,1)} %get-tuple-element.37), calls=%async_computation | async-start | bytes 1310720 | tf_op jit(solution)/shard_map/all_to_all | solution.py:491
  12.7 1.2 %collective-permute-done.2.refs_6_ = f32[8,256]{1,0:T(8,128)S(1)} collective-permute-done((f32[8,256]{1,0:T(8,128)S(1)}, f32[8,256]{1,0:T(8,128)S(1)}, u32[]{:S(2)}, u32[]{:S(2)}) %collective-permute-start.2) | collective-permute-done | bytes 8224 | tf_op jit(solution)/shard_map/ppermute | solution.py:443
  13.9 1.3 %collective-permute-done.1.refs_5_ = f32[8,256]{1,0:T(8,128)S(1)} collective-permute-done((f32[8,256]{1,0:T(8,128)S(1)}, f32[8,256]{1,0:T(8,128)S(1)}, u32[]{:S(2)}, u32[]{:S(2)}) %collective-permute-start.1) | collective-permute-done | bytes 8224 | tf_op jit(solution)/shard_map/ppermute | solution.py:443
  15.8 4.2 %shard_map.83 = (bf16[656,128]{1,0:T(8,128)(2,1)}, bf16[656,128]{1,0:T(8,128)(2,1)}, bf16[656,128]{1,0:T(8,128)(2,1)}, bf16[656,128]{1,0:T(8,128)(2,1)}, bf16[65...) custom-call(bf16[256,1280]{1,0:T(8,128)(2,1)} %refs_0_.1, ...), custom_call_target="tpu_custom_call" | custom-call | tf_op jit(solution)/shard_map/pallas_call | solution.py:433
  20.0 1.7 %collective-permute-start.4 = (bf16[656,128]{1,0:T(8,128)(2,1)}, bf16[656,128]{1,0:T(8,128)(2,1)S(1)}, u32[]{:S(2)}, u32[]{:S(2)}) collective-permute-start(bf16[656,128]{1,0:T(8,128)(2,1)} %get-tuple-element.40), channel_id=1, source_target_pairs={{0,8},{4,12},{8,0},{12,4},{16,24},{20,28},{24,16},{28,20},{1,9},{5... | collective-permute-start | bytes 503816 | tf_op jit(solution)/shard_map/ppermute | solution.py:443
  21.7 1.4 %collective-permute-start.3 = (bf16[656,128]{1,0:T(8,128)(2,1)}, bf16[656,128]{1,0:T(8,128)(2,1)S(1)}, u32[]{:S(2)}, u32[]{:S(2)}) collective-permute-start(bf16[656,128]{1,0:T(8,128)(2,1)} %get-tuple-element.39), channel_id=1, source_target_pairs={{0,4},{4,0},{8,12},{12,8},{16,20},{20,16},{24,28},{28,24},{1,5},{5... | collective-permute-start | bytes 503816 | tf_op jit(solution)/shard_map/ppermute | solution.py:443
  23.2 2.4 %collective-permute-start.6 = (bf16[656,128]{1,0:T(8,128)(2,1)}, bf16[656,128]{1,0:T(8,128)(2,1)S(1)}, u32[]{:S(2)}, u32[]{:S(2)}) collective-permute-start(bf16[656,128]{1,0:T(8,128)(2,1)} %get-tuple-element.43), channel_id=1, source_target_pairs={{0,16},{4,20},{8,24},{12,28},{16,0},{20,4},{24,8},{28,12},{1,17},{... | collective-permute-start | bytes 503816 | tf_op jit(solution)/shard_map/ppermute | solution.py:443
  26.1 2.4 %collective-permute-start.8 = (bf16[656,128]{1,0:T(8,128)(2,1)}, bf16[656,128]{1,0:T(8,128)(2,1)S(1)}, u32[]{:S(2)}, u32[]{:S(2)}) collective-permute-start(bf16[656,128]{1,0:T(8,128)(2,1)} %get-tuple-element.45), channel_id=1, source_target_pairs={{0,24},{4,28},{8,16},{12,20},{16,8},{20,12},{24,0},{28,4},{1,25},{... | collective-permute-start | bytes 503816 | tf_op jit(solution)/shard_map/ppermute | solution.py:443
  28.5 1.8 %collective-permute-done.4.refs_3_ = bf16[656,128]{1,0:T(8,128)(2,1)S(1)} collective-permute-done((bf16[656,128]{1,0:T(8,128)(2,1)}, bf16[656,128]{1,0:T(8,128)(2,1)S(1)}, u32[]{:S(2)}, u32[]{:S(2)}) %collective-permute-start.4) | collective-permute-done | bytes 167968 | tf_op jit(solution)/shard_map/ppermute | solution.py:443
  30.3 3.5 %collective-permute-start.9 = (bf16[656,128]{1,0:T(8,128)(2,1)}, bf16[656,128]{1,0:T(8,128)(2,1)S(1)}, u32[]{:S(2)}, u32[]{:S(2)}) collective-permute-start(bf16[656,128]{1,0:T(8,128)(2,1)} %get-tuple-element.46), channel_id=1, source_target_pairs={{0,28},{4,24},{8,20},{12,16},{16,12},{20,8},{24,4},{28,0},{1,29},{... | collective-permute-start | bytes 503816 | tf_op jit(solution)/shard_map/ppermute | solution.py:443
  34.5 12.9 %collective-permute-done.6.refs_5_ = bf16[656,128]{1,0:T(8,128)(2,1)S(1)} collective-permute-done((bf16[656,128]{1,0:T(8,128)(2,1)}, bf16[656,128]{1,0:T(8,128)(2,1)S(1)}, u32[]{:S(2)}, u32[]{:S(2)}) %collective-permute-start.6) | collective-permute-done | bytes 167968 | tf_op jit(solution)/shard_map/ppermute | solution.py:443
  47.4 4.2 %collective-permute-done.7.refs_6_ = bf16[656,128]{1,0:T(8,128)(2,1)S(1)} collective-permute-done((bf16[656,128]{1,0:T(8,128)(2,1)}, bf16[656,128]{1,0:T(8,128)(2,1)S(1)}, u32[]{:S(2)}, u32[]{:S(2)}) %collective-permute-start.7) | collective-permute-done | bytes 167968 | tf_op jit(solution)/shard_map/ppermute | solution.py:443
  51.7 2.0 %collective-permute-done.5.refs_4_ = bf16[656,128]{1,0:T(8,128)(2,1)S(1)} collective-permute-done((bf16[656,128]{1,0:T(8,128)(2,1)}, bf16[656,128]{1,0:T(8,128)(2,1)S(1)}, u32[]{:S(2)}, u32[]{:S(2)}) %collective-permute-start.5) | collective-permute-done | bytes 167968 | tf_op jit(solution)/shard_map/ppermute | solution.py:443
  54.4 4.8 %collective-permute-start.12 = (bf16[128,128]{1,0:T(8,128)(2,1)S(1)}, bf16[128,128]{1,0:T(8,128)(2,1)S(1)}, u32[]{:S(2)}, u32[]{:S(2)}) collective-permute-start(bf16[128,128]{1,0:T(8,128)(2,1)S(1)} %pad_maximum_fusion.refs_9_), channel_id=1, source_target_pairs={{0,12},{4,8},{8,4},{12,0},{16,28},{20,24},{24,20},{28,16},{1,13},{... | collective-permute-start | bytes 98312 | tf_op jit(solution)/shard_map/ppermute | solution.py:443
  59.3 1.4 %collective-permute-start.10 = (bf16[128,128]{1,0:T(8,128)(2,1)S(1)}, bf16[128,128]{1,0:T(8,128)(2,1)S(1)}, u32[]{:S(2)}, u32[]{:S(2)}) collective-permute-start(bf16[128,128]{1,0:T(8,128)(2,1)S(1)} %pad_maximum_fusion.refs_9_), channel_id=1, source_target_pairs={{0,4},{4,0},{8,12},{12,8},{16,20},{20,16},{24,28},{28,24},{1,5},{5... | collective-permute-start | bytes 98312 | tf_op jit(solution)/shard_map/ppermute | solution.py:443
  61.6 3.6 %shard_map.84 = (bf16[256,128]{1,0:T(8,128)(2,1)S(1)}, bf16[256,128]{1,0:T(8,128)(2,1)S(1)}, bf16[256,128]{1,0:T(8,128)(2,1)S(1)}, bf16[256,128]{1,0:T(8,128)(2,...) custom-call(s32[1]{0:T(128)} %copy.9.at_ref, ...), custom_call_target="tpu_custom_call" | custom-call | tf_op jit(solution)/shard_map/pallas_call | solution.py:433
  66.2 2.1 %collective-permute-start.14 = (bf16[336,128]{1,0:T(8,128)(2,1)S(1)}, bf16[336,128]{1,0:T(8,128)(2,1)S(1)}, u32[]{:S(2)}, u32[]{:S(2)}) collective-permute-start(bf16[336,128]{1,0:T(8,128)(2,1)S(1)} %get-tuple-element.58), channel_id=1, source_target_pairs={{0,8},{4,12},{8,0},{12,4},{16,24},{20,28},{24,16},{28,20},{1,9},{5... | collective-permute-start | bytes 258056 | tf_op jit(solution)/shard_map/ppermute | solution.py:443
  69.0 3.8 %collective-permute-start.17 = (bf16[336,128]{1,0:T(8,128)(2,1)S(1)}, bf16[336,128]{1,0:T(8,128)(2,1)S(1)}, u32[]{:S(2)}, u32[]{:S(2)}) collective-permute-start(bf16[336,128]{1,0:T(8,128)(2,1)S(1)} %get-tuple-element.62), channel_id=1, source_target_pairs={{0,20},{4,16},{8,28},{12,24},{16,4},{20,0},{24,12},{28,8},{1,21},{... | collective-permute-start | bytes 258056 | tf_op jit(solution)/shard_map/ppermute | solution.py:443
  72.7 1.5 %collective-permute-start.18 = (bf16[336,128]{1,0:T(8,128)(2,1)S(1)}, bf16[336,128]{1,0:T(8,128)(2,1)S(1)}, u32[]{:S(2)}, u32[]{:S(2)}) collective-permute-start(bf16[336,128]{1,0:T(8,128)(2,1)S(1)} %get-tuple-element.63), channel_id=1, source_target_pairs={{0,24},{4,28},{8,16},{12,20},{16,8},{20,12},{24,0},{28,4},{1,25},{... | collective-permute-start | bytes 258056 | tf_op jit(solution)/shard_map/ppermute | solution.py:443
  74.2 2.4 %collective-permute-start.19 = (bf16[336,128]{1,0:T(8,128)(2,1)S(1)}, bf16[336,128]{1,0:T(8,128)(2,1)S(1)}, u32[]{:S(2)}, u32[]{:S(2)}) collective-permute-start(bf16[336,128]{1,0:T(8,128)(2,1)S(1)} %get-tuple-element.64), channel_id=1, source_target_pairs={{0,28},{4,24},{8,20},{12,16},{16,12},{20,8},{24,4},{28,0},{1,29},{... | collective-permute-start | bytes 258056 | tf_op jit(solution)/shard_map/ppermute | solution.py:443
  76.6 4.8 %collective-permute-done.16.refs_4_ = bf16[336,128]{1,0:T(8,128)(2,1)S(1)} collective-permute-done((bf16[336,128]{1,0:T(8,128)(2,1)S(1)}, bf16[336,128]{1,0:T(8,128)(2,1)S(1)}, u32[]{:S(2)}, u32[]{:S(2)}) %collective-permute-start.16) | collective-permute-done | bytes 86048 | tf_op jit(solution)/shard_map/ppermute | solution.py:443
  81.3 1.8 %collective-permute-done.17.refs_5_ = bf16[336,128]{1,0:T(8,128)(2,1)S(1)} collective-permute-done((bf16[336,128]{1,0:T(8,128)(2,1)S(1)}, bf16[336,128]{1,0:T(8,128)(2,1)S(1)}, u32[]{:S(2)}, u32[]{:S(2)}) %collective-permute-start.17) | collective-permute-done | bytes 86048 | tf_op jit(solution)/shard_map/ppermute | solution.py:443
  83.4 1.7 %shard_map.86 = bf16[256,1280]{1,0:T(8,128)(2,1)} custom-call(f32[256,1280]{1,0:T(8,128)S(1)} %copy-done, bf16[336,128]{1,0:T(8,128)(2,1)S(1)} %get-tuple-element.56.refs_0_, bf16[336,128]{1,0:T(8,128)(2,1)S(1)} %collective-permute-done.13.refs_1_, bf16[336,128]{1,0:T(8,128)(2,1)S(1)} %collective-permute-done.14.refs_2_, ...), custom_call_target="tpu_custom_call" | custom-call | tf_op jit(solution)/shard_map/pallas_call | solution.py:433
  (38 shorter events, 6.8 us)
Async XLA Ops:
  3.5 7.3 %copy-start.2 = (f32[8,256]{1,0:T(8,128)S(1)}, f32[8,256]{1,0:T(8,128)}, u32[]{:S(2)}) copy-start(f32[8,256]{1,0:T(8,128)} %get-tuple-element.35.refs_3_) | copy-start | bytes 24580
  3.5 50.9 %all-to-all-start = ((bf16[8,320,128]{2,1,0:T(8,128)(2,1)}), bf16[8,320,128]{2,1,0:T(8,128)(2,1)S(1)}, u32[]{:S(2)}, u32[]{:S(2)}) async-start(bf16[8,320,128]{2,1,0:T(8,128)(2,1)} %get-tuple-element.37), calls=%async_computation | async-start | bytes 1310720 | tf_op jit(solution)/shard_map/all_to_all | solution.py:491
  10.7 3.2 %collective-permute-start.2 = (f32[8,256]{1,0:T(8,128)S(1)}, f32[8,256]{1,0:T(8,128)S(1)}, u32[]{:S(2)}, u32[]{:S(2)}) collective-permute-start(f32[8,256]{1,0:T(8,128)S(1)} %copy-done.2), channel_id=1, source_target_pairs={{0,3},{1,2},{2,1},{3,0},{4,7},{5,6},{6,5},{7,4},{8,11},{9,10},{10,... | collective-permute-start | bytes 24584 | tf_op jit(solution)/shard_map/ppermute | solution.py:443
  11.5 3.7 %collective-permute-start.1 = (f32[8,256]{1,0:T(8,128)S(1)}, f32[8,256]{1,0:T(8,128)S(1)}, u32[]{:S(2)}, u32[]{:S(2)}) collective-permute-start(f32[8,256]{1,0:T(8,128)S(1)} %copy-done.2), channel_id=1, source_target_pairs={{0,2},{1,3},{2,0},{3,1},{4,6},{5,7},{6,4},{7,5},{8,10},{9,11},{10,... | collective-permute-start | bytes 24584 | tf_op jit(solution)/shard_map/ppermute | solution.py:443
  12.4 2.8 %collective-permute-start = (f32[8,256]{1,0:T(8,128)S(1)}, f32[8,256]{1,0:T(8,128)S(1)}, u32[]{:S(2)}, u32[]{:S(2)}) collective-permute-start(f32[8,256]{1,0:T(8,128)S(1)} %copy-done.2), channel_id=1, source_target_pairs={{0,1},{1,0},{2,3},{3,2},{4,5},{5,4},{6,7},{7,6},{8,9},{9,8},{10,11... | collective-permute-start | bytes 24584 | tf_op jit(solution)/shard_map/ppermute | solution.py:443
  13.9 1.3 %copy-start.3 = (f32[8,256]{1,0:T(8,128)}, f32[8,256]{1,0:T(8,128)S(1)}, u32[]{:S(2)}) copy-start(f32[8,256]{1,0:T(8,128)S(1)} %collective-permute-done.2.refs_6_) | copy-start | bytes 24580
  20.0 10.2 %collective-permute-start.4 = (bf16[656,128]{1,0:T(8,128)(2,1)}, bf16[656,128]{1,0:T(8,128)(2,1)S(1)}, u32[]{:S(2)}, u32[]{:S(2)}) collective-permute-start(bf16[656,128]{1,0:T(8,128)(2,1)} %get-tuple-element.40), channel_id=1, source_target_pairs={{0,8},{4,12},{8,0},{12,4},{16,24},{20,28},{24,16},{28,20},{1,9},{5... | collective-permute-start | bytes 503816 | tf_op jit(solution)/shard_map/ppermute | solution.py:443
  21.7 12.1 %collective-permute-start.3 = (bf16[656,128]{1,0:T(8,128)(2,1)}, bf16[656,128]{1,0:T(8,128)(2,1)S(1)}, u32[]{:S(2)}, u32[]{:S(2)}) collective-permute-start(bf16[656,128]{1,0:T(8,128)(2,1)} %get-tuple-element.39), channel_id=1, source_target_pairs={{0,4},{4,0},{8,12},{12,8},{16,20},{20,16},{24,28},{28,24},{1,5},{5... | collective-permute-start | bytes 503816 | tf_op jit(solution)/shard_map/ppermute | solution.py:443
  23.2 24.3 %collective-permute-start.6 = (bf16[656,128]{1,0:T(8,128)(2,1)}, bf16[656,128]{1,0:T(8,128)(2,1)S(1)}, u32[]{:S(2)}, u32[]{:S(2)}) collective-permute-start(bf16[656,128]{1,0:T(8,128)(2,1)} %get-tuple-element.43), channel_id=1, source_target_pairs={{0,16},{4,20},{8,24},{12,28},{16,0},{20,4},{24,8},{28,12},{1,17},{... | collective-permute-start | bytes 503816 | tf_op jit(solution)/shard_map/ppermute | solution.py:443
  25.6 26.1 %collective-permute-start.7 = (bf16[656,128]{1,0:T(8,128)(2,1)}, bf16[656,128]{1,0:T(8,128)(2,1)S(1)}, u32[]{:S(2)}, u32[]{:S(2)}) collective-permute-start(bf16[656,128]{1,0:T(8,128)(2,1)} %get-tuple-element.44), channel_id=1, source_target_pairs={{0,20},{4,16},{8,28},{12,24},{16,4},{20,0},{24,12},{28,8},{1,21},{... | collective-permute-start | bytes 503816 | tf_op jit(solution)/shard_map/ppermute | solution.py:443
  26.1 25.5 %collective-permute-start.8 = (bf16[656,128]{1,0:T(8,128)(2,1)}, bf16[656,128]{1,0:T(8,128)(2,1)S(1)}, u32[]{:S(2)}, u32[]{:S(2)}) collective-permute-start(bf16[656,128]{1,0:T(8,128)(2,1)} %get-tuple-element.45), channel_id=1, source_target_pairs={{0,24},{4,28},{8,16},{12,20},{16,8},{20,12},{24,0},{28,4},{1,25},{... | collective-permute-start | bytes 503816 | tf_op jit(solution)/shard_map/ppermute | solution.py:443
  30.3 21.4 %collective-permute-start.9 = (bf16[656,128]{1,0:T(8,128)(2,1)}, bf16[656,128]{1,0:T(8,128)(2,1)S(1)}, u32[]{:S(2)}, u32[]{:S(2)}) collective-permute-start(bf16[656,128]{1,0:T(8,128)(2,1)} %get-tuple-element.46), channel_id=1, source_target_pairs={{0,28},{4,24},{8,20},{12,16},{16,12},{20,8},{24,4},{28,0},{1,29},{... | collective-permute-start | bytes 503816 | tf_op jit(solution)/shard_map/ppermute | solution.py:443
  33.8 19.8 %collective-permute-start.5 = (bf16[656,128]{1,0:T(8,128)(2,1)}, bf16[656,128]{1,0:T(8,128)(2,1)S(1)}, u32[]{:S(2)}, u32[]{:S(2)}) collective-permute-start(bf16[656,128]{1,0:T(8,128)(2,1)} %get-tuple-element.42), channel_id=1, source_target_pairs={{0,12},{4,8},{8,4},{12,0},{16,28},{20,24},{24,20},{28,16},{1,13},{... | collective-permute-start | bytes 503816 | tf_op jit(solution)/shard_map/ppermute | solution.py:443
  54.4 10.7 %collective-permute-start.12 = (bf16[128,128]{1,0:T(8,128)(2,1)S(1)}, bf16[128,128]{1,0:T(8,128)(2,1)S(1)}, u32[]{:S(2)}, u32[]{:S(2)}) collective-permute-start(bf16[128,128]{1,0:T(8,128)(2,1)S(1)} %pad_maximum_fusion.refs_9_), channel_id=1, source_target_pairs={{0,12},{4,8},{8,4},{12,0},{16,28},{20,24},{24,20},{28,16},{1,13},{... | collective-permute-start | bytes 98312 | tf_op jit(solution)/shard_map/ppermute | solution.py:443
  59.2 6.0 %collective-permute-start.11 = (bf16[128,128]{1,0:T(8,128)(2,1)S(1)}, bf16[128,128]{1,0:T(8,128)(2,1)S(1)}, u32[]{:S(2)}, u32[]{:S(2)}) collective-permute-start(bf16[128,128]{1,0:T(8,128)(2,1)S(1)} %pad_maximum_fusion.refs_9_), channel_id=1, source_target_pairs={{0,8},{4,12},{8,0},{12,4},{16,24},{20,28},{24,16},{28,20},{1,9},{5... | collective-permute-start | bytes 98312 | tf_op jit(solution)/shard_map/ppermute | solution.py:443
  59.3 5.9 %collective-permute-start.10 = (bf16[128,128]{1,0:T(8,128)(2,1)S(1)}, bf16[128,128]{1,0:T(8,128)(2,1)S(1)}, u32[]{:S(2)}, u32[]{:S(2)}) collective-permute-start(bf16[128,128]{1,0:T(8,128)(2,1)S(1)} %pad_maximum_fusion.refs_9_), channel_id=1, source_target_pairs={{0,4},{4,0},{8,12},{12,8},{16,20},{20,16},{24,28},{28,24},{1,5},{5... | collective-permute-start | bytes 98312 | tf_op jit(solution)/shard_map/ppermute | solution.py:443
  65.2 18.2 %copy-start = (f32[256,1280]{1,0:T(8,128)S(1)}, f32[256,1280]{1,0:T(8,128)}, u32[]{:S(2)}) copy-start(f32[256,1280]{1,0:T(8,128)} %get-tuple-element.36.own_ref) | copy-start | bytes 3932164
  66.2 7.9 %collective-permute-start.14 = (bf16[336,128]{1,0:T(8,128)(2,1)S(1)}, bf16[336,128]{1,0:T(8,128)(2,1)S(1)}, u32[]{:S(2)}, u32[]{:S(2)}) collective-permute-start(bf16[336,128]{1,0:T(8,128)(2,1)S(1)} %get-tuple-element.58), channel_id=1, source_target_pairs={{0,8},{4,12},{8,0},{12,4},{16,24},{20,28},{24,16},{28,20},{1,9},{5... | collective-permute-start | bytes 258056 | tf_op jit(solution)/shard_map/ppermute | solution.py:443
  68.3 8.2 %collective-permute-start.13 = (bf16[336,128]{1,0:T(8,128)(2,1)S(1)}, bf16[336,128]{1,0:T(8,128)(2,1)S(1)}, u32[]{:S(2)}, u32[]{:S(2)}) collective-permute-start(bf16[336,128]{1,0:T(8,128)(2,1)S(1)} %get-tuple-element.57), channel_id=1, source_target_pairs={{0,4},{4,0},{8,12},{12,8},{16,20},{20,16},{24,28},{28,24},{1,5},{5... | collective-permute-start | bytes 258056 | tf_op jit(solution)/shard_map/ppermute | solution.py:443
  68.9 12.4 %collective-permute-start.16 = (bf16[336,128]{1,0:T(8,128)(2,1)S(1)}, bf16[336,128]{1,0:T(8,128)(2,1)S(1)}, u32[]{:S(2)}, u32[]{:S(2)}) collective-permute-start(bf16[336,128]{1,0:T(8,128)(2,1)S(1)} %get-tuple-element.61), channel_id=1, source_target_pairs={{0,16},{4,20},{8,24},{12,28},{16,0},{20,4},{24,8},{28,12},{1,17},{... | collective-permute-start | bytes 258056 | tf_op jit(solution)/shard_map/ppermute | solution.py:443
  69.0 14.2 %collective-permute-start.17 = (bf16[336,128]{1,0:T(8,128)(2,1)S(1)}, bf16[336,128]{1,0:T(8,128)(2,1)S(1)}, u32[]{:S(2)}, u32[]{:S(2)}) collective-permute-start(bf16[336,128]{1,0:T(8,128)(2,1)S(1)} %get-tuple-element.62), channel_id=1, source_target_pairs={{0,20},{4,16},{8,28},{12,24},{16,4},{20,0},{24,12},{28,8},{1,21},{... | collective-permute-start | bytes 258056 | tf_op jit(solution)/shard_map/ppermute | solution.py:443
  72.7 10.4 %collective-permute-start.18 = (bf16[336,128]{1,0:T(8,128)(2,1)S(1)}, bf16[336,128]{1,0:T(8,128)(2,1)S(1)}, u32[]{:S(2)}, u32[]{:S(2)}) collective-permute-start(bf16[336,128]{1,0:T(8,128)(2,1)S(1)} %get-tuple-element.63), channel_id=1, source_target_pairs={{0,24},{4,28},{8,16},{12,20},{16,8},{20,12},{24,0},{28,4},{1,25},{... | collective-permute-start | bytes 258056 | tf_op jit(solution)/shard_map/ppermute | solution.py:443
  74.2 9.0 %collective-permute-start.19 = (bf16[336,128]{1,0:T(8,128)(2,1)S(1)}, bf16[336,128]{1,0:T(8,128)(2,1)S(1)}, u32[]{:S(2)}, u32[]{:S(2)}) collective-permute-start(bf16[336,128]{1,0:T(8,128)(2,1)S(1)} %get-tuple-element.64), channel_id=1, source_target_pairs={{0,28},{4,24},{8,20},{12,16},{16,12},{20,8},{24,4},{28,0},{1,29},{... | collective-permute-start | bytes 258056 | tf_op jit(solution)/shard_map/ppermute | solution.py:443
  76.6 6.9 %collective-permute-start.15 = (bf16[336,128]{1,0:T(8,128)(2,1)S(1)}, bf16[336,128]{1,0:T(8,128)(2,1)S(1)}, u32[]{:S(2)}, u32[]{:S(2)}) collective-permute-start(bf16[336,128]{1,0:T(8,128)(2,1)S(1)} %get-tuple-element.60), channel_id=1, source_target_pairs={{0,12},{4,8},{8,4},{12,0},{16,28},{20,24},{24,20},{28,16},{1,13},{... | collective-permute-start | bytes 258056 | tf_op jit(solution)/shard_map/ppermute | solution.py:443
  (3 other events, 2.1 us)

commit v5 on v4

--- a/solution.py
+++ b/solution.py
@@ -88,7 +88,9 @@
 
 
 ROWS = 16
-MASK_ROW = 12
+LSE_ROW = 6
+NORM_ROW = 9
+MASK_ROW = 15
 
 
 def dot_t(a, b):
@@ -128,16 +130,21 @@
             copies.append(pltpu.make_async_copy(ref.at[rows], held.at[t, rows], sems.at[t, c]))
     loads, stores = [], []
     for d in range(n):
-        heads = ((d, 0, tok, 0), (n + d // parts, d % parts * pos, pos, tok))
-        for j, (head, row, rows, at) in enumerate(heads):
+        row = d % parts * pos
+        pieces = (
+            (v_ref, d, 0, tok, 0),
+            (v_ref, n + d // parts, row, pos, tok),
+            (k_ref, n + d // parts, row, pos, tok + pos),
+        )
+        for j, (ref, head, row, rows, at) in enumerate(pieces):
             loads.append(
                 pltpu.make_async_copy(
-                    v_ref.at[pl.ds(row, rows), pl.ds(head * HD, HD)],
+                    ref.at[pl.ds(row, rows), pl.ds(head * HD, HD)],
                     cut.at[d, pl.ds(at, rows)],
                     v_sems.at[j, d],
                 )
             )
-        stores.append(pltpu.make_async_copy(cut.at[d], out_ref.at[d], v_sems.at[2, d]))
+        stores.append(pltpu.make_async_copy(cut.at[d], out_ref.at[d], v_sems.at[3, d]))
     for copy in copies + loads:
         copy.start()
     rows = []
@@ -195,7 +202,9 @@
         copy.start()
     for copy in small:
         copy.wait()
-    inv = lax.rsqrt((sums[0] + sums[1] + sums[2] + sums[3]) / D + 1e-06).T
+    inv = lax.rsqrt((sums[0] + sums[1] + sums[2] + sums[3]) / D + 1e-06)
+    inv_row = inv[1:2, :]
+    inv = inv.T
     inv_q = jnp.broadcast_to(inv[:, 0:1] * (LOG2E / float(HD) ** 0.5), (tok, HD))
     inv_k = jnp.broadcast_to(inv[:, 1:2], (tok, HD))
     flags = [jnp.where(masks[0, i, 1 - i] == 1, 0.0, NEG) for i in range(2)]
@@ -209,17 +218,15 @@
         query = scaled(ins[0, x], inv_q, gains[0, pl.ds(h, 1), :])
         keys = scaled(ins[1, x], inv_k, gains[1, pl.ds(h, 1), :])
         vals = ins[2, x]
-        for t, array in enumerate((query, keys)):
-            if x < heads - n:
-                extra[x, t] = array
-            else:
-                s = x - (heads - n)
-                held[s, t * tok : (t + 1) * tok, :] = array
-                at = 2 * tok + t * pos
-                rows = pl.ds(pl.multiple_of((me ^ s) % parts * pos, pos), pos)
-                held[s, at : at + pos, :] = extra[(me ^ s) // parts, t, rows, :]
-        if x >= heads - n:
-            rows = pl.ds(0, 2 * (tok + pos))
+        if x < heads - n:
+            extra[x] = query
+        else:
+            s = x - (heads - n)
+            held[s, :tok, :] = query
+            held[s, tok : 2 * tok, :] = keys
+            rows = pl.ds(pl.multiple_of((me ^ s) % parts * pos, pos), pos)
+            held[s, 2 * tok : 2 * tok + pos, :] = extra[(me ^ s) // parts, rows, :]
+            rows = pl.ds(0, 2 * tok + pos)
             stores.append(
                 pltpu.make_async_copy(held.at[s, rows], blocks[s].at[rows], out_sems.at[x])
             )
@@ -235,28 +242,28 @@
             pltpu.make_async_copy(own.at[x], own_ref.at[:, cols(h)], out_sems.at[heads + x])
         )
         stores[-1].start()
-    pieces = []
-    for lse in lses:
-        rest = lse.T[:ROWS]
-        split = []
+    def split(rest):
+        parts = []
         for _ in range(3):
-            split.append(rest.astype(jnp.bfloat16).astype(jnp.float32))
-            rest = rest - split[-1]
-        pieces.append(split)
-    pad = jnp.zeros((ROWS - 1 - MASK_ROW, HD), jnp.float32)
+            parts.append(rest.astype(jnp.bfloat16).astype(jnp.float32))
+            rest = rest - parts[-1]
+        return parts
+
+    lses = [split(lse.T[:ROWS]) for lse in lses]
+    norms = [split(inv_row[:, i * BLOCK : (i + 1) * BLOCK]) for i in range(tok // BLOCK)]
     lane = lax.broadcasted_iota(jnp.int32, (1, HD), 1)
     mask = jnp.where(lane == 0, masks[1, 0, 1], masks[1, 1, 0])
-    mask = (mask == 1).astype(jnp.float32)
-    at = 2 * (tok + pos)
+    tail = norms[0] + norms[1] + [(mask == 1).astype(jnp.float32)]
+    at = 2 * tok + pos
     for s in range(n):
+        first = heads - n + s
+        rows = [piece[first : first + 1, :] for half in lses for piece in half]
         late = (me ^ s) // parts == 1
-        rows = []
-        for split in pieces:
-            rows += [piece[s + heads - n : s + heads - n + 1, :] for piece in split]
-        for split in pieces:
-            rows += [jnp.where(late, piece[1:2, :], piece[0:1, :]) for piece in split]
-        side = jnp.concatenate(rows + [mask, pad], axis=0)
-        held[s, at : at + ROWS, :] = side.astype(jnp.bfloat16)
+        upper = (me ^ s) % parts * pos >= BLOCK
+        for low, high in zip(*lses):
+            piece = jnp.where(upper, high, low)
+            rows.append(jnp.where(late, piece[1:2, :], piece[0:1, :]))
+        held[s, at : at + ROWS, :] = jnp.concatenate(rows + tail, axis=0).astype(jnp.bfloat16)
         rows = pl.ds(at, ROWS)
         stores.append(
             pltpu.make_async_copy(held.at[s, rows], blocks[s].at[rows], out_sems.at[2 * heads + s])
@@ -296,19 +303,22 @@
     return side
 
 
-def read_side(blocks, at, which, mask_ref):
-    rows, masks = [], []
+def read_side(blocks, at, col_ref, mask_ref):
+    whole, part, norm, masks = [], [], [], []
     for block in blocks:
         side = block[at : at + ROWS, :].astype(jnp.float32)
-        for half in range(2):
-            first = 6 * which + 3 * half
-            rows.append(
-                side[first : first + 1] + side[first + 1 : first + 2] + side[first + 2 : first + 3]
-            )
+
+        def joined(first):
+            return side[first : first + 1] + side[first + 1 : first + 2] + side[first + 2 : first + 3]
+
+        whole += [joined(0), joined(3)]
+        part.append(joined(LSE_ROW))
+        norm += [joined(NORM_ROW), joined(NORM_ROW + 3)]
         masks.append(side[MASK_ROW : MASK_ROW + 1])
     mask_ref[...] = jnp.concatenate(masks, axis=0)
+    rows = whole + part + norm
     rows.append(jnp.zeros((HD - len(rows), HD), jnp.float32))
-    return jnp.concatenate(rows, axis=0).T
+    col_ref[...] = jnp.concatenate(rows, axis=0).T
 
 
 def pencil_flags(mask_ref, row, upper):
@@ -317,97 +327,87 @@
     return [jnp.where(upper, flags[1 - i], flags[i]) for i in range(2)]
 
 
-def whole_kernel(n, tok, pos, at_ref, *refs):
-    v_ref, blocks, outs, side_ref = refs[0], refs[1 : n + 1], refs[n + 1 : 2 * n + 1], refs[2 * n + 1]
-    held_ref, mask_ref = refs[2 * n + 2 :]
+def run_pencil(n, gp, mask_ref, query, keys, vals, lse, ka, va, row, outs, at, side):
+    me = lax.axis_index("frame")
+
+    def put(s, result):
+        outs[s][at : at + gp, :] = result
+
+    flags = pencil_flags(mask_ref, row ^ me, me >= n // 2)
+    lse = jnp.concatenate(lse, axis=0)
+    keep = pencil(n, query, keys, vals, lse, ka, va, flags, put)
+    return add_side(side, keep, gp, at // ROWS)
+
+
+def stack_rows(blocks, at, gp):
+    return jnp.concatenate([block[at : at + gp, :] for block in blocks], axis=0)
+
+
+def whole_kernel(n, tok, pos, at_ref, v_ref, *refs):
+    blocks, outs, side_ref = refs[:n], refs[n : 2 * n], refs[2 * n]
+    col_ref, mask_ref, key_ref = refs[2 * n + 1 :]
     gp = tok // n
     me = lax.axis_index("frame")
+    anchor = at_ref[0]
     for s in range(n):
 
-        @pl.when(at_ref[0] == me ^ s)
+        @pl.when(anchor == me ^ s)
         def _():
-            held_ref[...] = blocks[s][tok : 2 * tok, :]
-
-    ka, va = held_ref[...], v_ref[at_ref[0], :tok, :]
-    lses = read_side(blocks, 2 * (tok + pos), 0, mask_ref)
-    upper = me >= n // 2
+            key_ref[...] = blocks[s][tok : 2 * tok, :]
+
+    read_side(blocks, 2 * tok + pos, col_ref, mask_ref)
+    ka, va = key_ref[...], v_ref[anchor, :tok, :]
+    values = [v_ref.at[me ^ s] for s in range(n)]
     side = jnp.zeros((n, ROWS, HD), jnp.float32)
     for g in range(n):
-
-        def rows(at):
-            return jnp.concatenate(
-                [block[at + g * gp : at + (g + 1) * gp, :] for block in blocks], axis=0
-            )
-
-        def put(s, result):
-            outs[s][g * gp : (g + 1) * gp, :] = result
-
-        vals = [v_ref[me ^ s, g * gp : (g + 1) * gp, :] for s in range(n)]
-        half, first = g * gp // BLOCK, g * gp % BLOCK
-        lse = [lses[first : first + gp, 2 * s + half : 2 * s + half + 1] for s in range(n)]
-        keep = pencil(
-            n,
-            rows(0),
-            rows(tok),
-            jnp.concatenate(vals, axis=0),
-            jnp.concatenate(lse, axis=0),
-            ka,
-            va,
-            pencil_flags(mask_ref, g ^ me, upper),
-            put,
+        half, first, at = g * gp // BLOCK, g * gp % BLOCK, g * gp
+        lse = [col_ref[first : first + gp, 2 * s + half : 2 * s + half + 1] for s in range(n)]
+        query, keys = stack_rows(blocks, at, gp), stack_rows(blocks, tok + at, gp)
+        vals = stack_rows(values, at, gp)
+        side = run_pencil(
+            n, gp, mask_ref, query, keys, vals, lse, ka, va, g, outs, at, side
         )
-        side = add_side(side, keep, gp, g * gp // ROWS)
     side_ref[...] = side
 
 
-def part_kernel(n, tok, pos, *refs):
-    v_ref, refs = refs[0], refs[1:]
-    blocks, held = refs[:n], refs[n : n + 4]
-    done, came_ref = refs[n + 4 : 2 * n + 4], refs[2 * n + 4]
-    outs = refs[2 * n + 5 : 3 * n + 5]
-    lse_ref, mask_ref = refs[3 * n + 5 :]
+def part_kernel(n, tok, pos, at_ref, gain_ref, held_ref, v_ref, *refs):
+    blocks, done, (came_ref, col_ref, mask_ref) = refs[:n], refs[n : 2 * n], refs[2 * n : 2 * n + 3]
+    outs = refs[2 * n + 3 :]
     gp = tok // n
+    parts = tok // pos
     me = lax.axis_index("frame")
-    quarter = me % (tok // pos)
-    per_block = BLOCK // pos
+    anchor = at_ref[0]
+    quarter = me % parts
+    gain = jnp.where(me // parts == 1, gain_ref[n + 1 : n + 2, :], gain_ref[n : n + 1, :])
+    late = quarter * pos >= BLOCK
     for s in range(n):
         outs[s][:tok, :] = done[s][...]
-    ka = jnp.concatenate([a[:pos, :] for a in held], axis=0)
-    va = jnp.concatenate([a[pos:, :] for a in held], axis=0)
-    lse_ref[...] = read_side(blocks, 2 * (tok + pos), 1, mask_ref)
-    upper = me >= n // 2
-    late = quarter >= per_block
+    norm = []
+    for half in range(tok // BLOCK):
+        norm.append(jnp.zeros((BLOCK, 1), jnp.float32))
+        for s in range(n):
+            lane = 3 * n + 2 * s + half
+            norm[-1] = jnp.where(anchor == me ^ s, col_ref[:, lane : lane + 1], norm[-1])
+    va = jnp.concatenate([held_ref[j, :pos, :] for j in range(parts)], axis=0)
+    ka = jnp.concatenate([held_ref[j, pos:, :] for j in range(parts)], axis=0)
+    ka = scaled(ka, jnp.concatenate(norm, axis=0), gain)
+    values = [v_ref.at[me ^ s] for s in range(n)]
     side = came_ref[...]
     for u in range(pos // gp):
-
-        def rows(at):
-            return jnp.concatenate(
-                [block[at + u * gp : at + (u + 1) * gp, :] for block in blocks], axis=0
-            )
-
-        def put(s, result):
-            outs[s][tok + u * gp : tok + (u + 1) * gp, :] = result
-
+        first = pl.multiple_of(quarter * pos % BLOCK + u * gp, gp)
+        cols = col_ref[pl.ds(first, gp), :]
+        lse, norm = [], []
+        for s in range(n):
+            lse.append(cols[:, 2 * n + s : 2 * n + s + 1])
+            lane = 3 * n + 2 * s
+            norm.append(jnp.where(late, cols[:, lane + 1 : lane + 2], cols[:, lane : lane + 1]))
         at = tok + u * gp
-        vals = [v_ref[me ^ s, at : at + gp, :] for s in range(n)]
-        first = pl.multiple_of(quarter % per_block * pos + u * gp, gp)
-        lses = lse_ref[pl.ds(first, gp), :]
-        lse = [
-            jnp.where(late, lses[:, 2 * s + 1 : 2 * s + 2], lses[:, 2 * s : 2 * s + 1])
-            for s in range(n)
-        ]
-        keep = pencil(
-            n,
-            rows(2 * tok),
-            rows(2 * tok + pos),
-            jnp.concatenate(vals, axis=0),
-            jnp.concatenate(lse, axis=0),
-            ka,
-            va,
-            pencil_flags(mask_ref, (quarter * (pos // gp) + u) ^ me, upper),
-            put,
+        query, vals = stack_rows(blocks, tok + at, gp), stack_rows(values, at, gp)
+        keys = scaled(stack_rows(values, at + pos, gp), jnp.concatenate(norm, axis=0), gain)
+        row = quarter * (pos // gp) + u
+        side = run_pencil(
+            n, gp, mask_ref, query, keys, vals, lse, ka, va, row, outs, at, side
         )
-        side = add_side(side, keep, gp, (tok + u * gp) // ROWS)
     for s in range(n):
         outs[s][tok + pos : tok + pos + ROWS, :] = side[s].astype(jnp.bfloat16)
 
@@ -474,7 +474,7 @@
 
     sums, v_blocks = call(
         functools.partial(first_kernel, n, pos),
-        (shape((8, tok), f32), shape((n, tok + pos, HD), bf16)),
+        (shape((8, tok), f32), shape((n, tok + 2 * pos, HD), bf16)),
         q_raw,
         k_raw,
         values,
@@ -482,15 +482,15 @@
         out_specs=(vm, hbm),
         scratch_shapes=[
             pltpu.VMEM((2, tok, width), bf16),
-            pltpu.VMEM((n, tok + pos, HD), bf16),
+            pltpu.VMEM((n, tok + 2 * pos, HD), bf16),
             dma((2, 4)),
-            dma((3, n)),
+            dma((4, n)),
         ],
         vmem=60,
     )
+    all_sums = [sums] + [pairwise(sums, "mp", step) for step in range(1, n_mp)]
     v_far = lax.all_to_all(v_blocks, "frame", split_axis=0, concat_axis=0, tiled=True)
-    all_sums = [sums] + [pairwise(sums, "mp", step) for step in range(1, n_mp)]
-    rows = 2 * (tok + pos) + ROWS
+    rows = 2 * tok + pos + ROWS
     *sent, own = call(
         functools.partial(own_kernel, n, pos),
         [shape((rows, HD), bf16)] * n + [shape((tok, width), f32)],
@@ -507,7 +507,7 @@
         scratch_shapes=[
             pltpu.VMEM((3, heads, tok, HD), bf16),
             pltpu.VMEM((n, rows, HD), bf16),
-            pltpu.VMEM((heads - n, 2, tok, HD), bf16),
+            pltpu.VMEM((heads - n, tok, HD), bf16),
             pltpu.VMEM((heads, tok, HD), f32),
             pltpu.VMEM((4, 8, tok), f32),
             pltpu.VMEM((2, heads, HD), f32),
@@ -518,33 +518,47 @@
         vmem=60,
     )
     far = swap_blocks(sent)
+    block, v_far = lax.optimization_barrier((sent[0], v_far))
+    far[0] = call(copy_kernel, shape((rows, HD), bf16), block, vmem=8)
 
     anchor = anchor_frame[0]
-    part = slice(2 * tok + pos, 2 * (tok + pos))
-    mine = far[0][part]
-    for s in range(1, n):
-        mine = jnp.where(anchor == me ^ s, far[s][part], mine)
-    v_mine = lax.dynamic_slice(v_far, (anchor, tok, 0), (1, pos, HD))[0]
-    mine = jnp.concatenate([mine, v_mine], axis=0)
-    held = [mine] + [pairwise(mine, "frame", step) for step in range(1, parts)]
-    *done, weights = call(
+    mine = lax.dynamic_slice(v_far, (anchor, tok, 0), (1, 2 * pos, HD))
+    groups = [list(range(first, first + parts)) for first in range(0, n, parts)]
+    held = lax.all_to_all(
+        jnp.broadcast_to(mine, (parts, 2 * pos, HD)),
+        "frame",
+        split_axis=0,
+        concat_axis=0,
+        axis_index_groups=groups,
+        tiled=True,
+    )
+    exps = n * tok * 2 * tok
+    *done, side, columns, masks = call(
         functools.partial(whole_kernel, n, tok, pos),
-        [shape((tok, HD), bf16)] * n + [shape((n, ROWS, HD), f32)],
+        [shape((tok, HD), bf16)] * n
+        + [shape((n, ROWS, HD), f32), shape((HD, HD), f32), shape((n, HD), f32)],
         anchor_frame,
         v_far,
         *far,
         in_specs=[sm] + [vm] * (n + 1),
-        scratch_shapes=[pltpu.VMEM((tok, HD), bf16), pltpu.VMEM((n, HD), f32)],
+        scratch_shapes=[pltpu.VMEM((tok, HD), bf16)],
+        cost_estimate=pl.CostEstimate(
+            flops=6 * exps * HD, bytes_accessed=8 * n * tok * HD, transcendentals=exps
+        ),
     )
     result = call(
         functools.partial(part_kernel, n, tok, pos),
         [shape((tok + pos + ROWS, HD), bf16)] * n,
+        anchor_frame,
+        k_gain.reshape(heads, HD),
+        held,
         v_far,
         *far,
-        *held,
         *done,
-        weights,
-        scratch_shapes=[pltpu.VMEM((HD, HD), f32), pltpu.VMEM((n, HD), f32)],
+        side,
+        columns,
+        masks,
+        in_specs=[sm] + [vm] * (2 * n + 6),
     )
     back = swap_blocks(result)
     return call(

time: 85.5 us -> 82.6 us (0.966)
  waiting for transfers between devices: 30.4 us -> 26.4 us
  Pallas kernels: 14 us -> 15.2 us
    ppermute x20 -> x17, waiting for transfers between devices: 30.4 us -> 13.8 us  [pairwise(): return lax.ppermute(array, axis, [(i, i ^ step) for i in range(size)])]
    all_to_all x1, waiting for transfers between devices: 0.01 us -> 12.6 us  [local_heads(): lax.all_to_all(v_blocks, 'frame', split_axis=0, concat_axis=0, tiled=True)]
    ppermute x20 -> x17, starting transfers between devices: 30.5 us -> 26.1 us  [pairwise(): return lax.ppermute(array, axis, [(i, i ^ step) for i in range(size)])]
    all_to_all x0 -> x1, starting transfers between devices: none -> 4.19 us  [local_heads(): lax.all_to_all(jnp.broadcast_to(mine, (parts, 2 * pos, HD)), 'frame', spl...]
    pallas_call x5 -> x6, Pallas kernels: 14 us -> 15.2 us  [call(): pl.pallas_call(kernel, out_shape=out_shape, compiler_params=pltpu.Compile...]
  transfers between devices with their start and end apart: 21 -> 19, of which waited for: 9 -> 8; matrix products, arithmetic and copies ran while one was open for 1% -> 1% of each run, Pallas kernels for 9% -> 10%
where the time goes in v5:
time: 82.6 us; the launch traced here: 82.1 us
  starting transfers between devices  37.5 us (45%)
  waiting for transfers between devices  26.4 us (32%)
  Pallas kernels  15.2 us (18%)
  local copies, waits for them, and re-layouts  2.19 us (3%)
    ppermute x17, starting transfers between devices, pairwise(): return lax.ppermute(array, axis, [(i, i ^ step) for i in range(size)])  26.1 us
    pallas_call x6, Pallas kernels, call(): pl.pallas_call(kernel, out_shape=out_shape, compiler_params=pltpu.Compile...  15.2 us
    ppermute x17, waiting for transfers between devices, pairwise(): return lax.ppermute(array, axis, [(i, i ^ step) for i in range(size)])  13.8 us
    all_to_all x1, waiting for transfers between devices, local_heads(): lax.all_to_all(v_blocks, 'frame', split_axis=0, concat_axis=0, tiled=True)  12.6 us
    all_to_all x1, starting transfers between devices, local_heads(): lax.all_to_all(v_blocks, 'frame', split_axis=0, concat_axis=0, tiled=True)  7.27 us
    all_to_all x1, starting transfers between devices, local_heads(): lax.all_to_all(jnp.broadcast_to(mine, (parts, 2 * pos, HD)), 'frame', spl...  4.19 us
  transfers between devices with their start and end apart: 19, of which 8 were waited for; matrix products, arithmetic and copies ran while one was open for 1% of the time, Pallas kernels for 10%

profile of v5, /device:TPU:0, one launch (start us, length us, event | category | flops | bytes accessed | tf_op | source)
XLA Modules:
  0.0 82.1 jit_solution(11812640778539521875)
XLA Ops:
  0.0 3.6 %shard_map.82 = (f32[8,256]{1,0:T(8,128)}, bf16[8,384,128]{2,1,0:T(8,128)(2,1)}) custom-call(bf16[256,1280]{1,0:T(8,128)(2,1)} %refs_0_.1, bf16[256,1280]{1,0:T(8,128)(2,1)} %refs_1_.1, bf16[256,1280]{1,0:T(8,128)(2,1)} %refs_2_.1), custom_call_target="tpu_custom_call" | custom-call | tf_op jit(solution)/shard_map/pallas_call | solution.py:433
  3.6 7.3 %all-to-all-start = ((bf16[8,384,128]{2,1,0:T(8,128)(2,1)}), bf16[8,384,128]{2,1,0:T(8,128)(2,1)S(1)}, u32[]{:S(2)}, u32[]{:S(2)}) async-start(bf16[8,384,128]{2,1,0:T(8,128)(2,1)} %get-tuple-element.42), calls=%async_computation | async-start | bytes 1572864 | tf_op jit(solution)/shard_map/all_to_all | solution.py:492
  11.7 0.9 %collective-permute-start.1 = (f32[8,256]{1,0:T(8,128)S(1)}, f32[8,256]{1,0:T(8,128)S(1)}, u32[]{:S(2)}, u32[]{:S(2)}) collective-permute-start(f32[8,256]{1,0:T(8,128)S(1)} %copy-done.3), channel_id=1, source_target_pairs={{0,2},{1,3},{2,0},{3,1},{4,6},{5,7},{6,4},{7,5},{8,10},{9,11},{10,... | collective-permute-start | bytes 24584 | tf_op jit(solution)/shard_map/ppermute | solution.py:443
  12.8 1.2 %collective-permute-done.2.refs_6_ = f32[8,256]{1,0:T(8,128)S(1)} collective-permute-done((f32[8,256]{1,0:T(8,128)S(1)}, f32[8,256]{1,0:T(8,128)S(1)}, u32[]{:S(2)}, u32[]{:S(2)}) %collective-permute-start.2) | collective-permute-done | bytes 8224 | tf_op jit(solution)/shard_map/ppermute | solution.py:443
  14.1 1.3 %collective-permute-done.1.refs_5_ = f32[8,256]{1,0:T(8,128)S(1)} collective-permute-done((f32[8,256]{1,0:T(8,128)S(1)}, f32[8,256]{1,0:T(8,128)S(1)}, u32[]{:S(2)}, u32[]{:S(2)}) %collective-permute-start.1) | collective-permute-done | bytes 8224 | tf_op jit(solution)/shard_map/ppermute | solution.py:443
  16.0 4.2 %shard_map.83 = (bf16[592,128]{1,0:T(8,128)(2,1)}, bf16[592,128]{1,0:T(8,128)(2,1)}, bf16[592,128]{1,0:T(8,128)(2,1)}, bf16[592,128]{1,0:T(8,128)(2,1)}, bf16[59...) custom-call(bf16[256,1280]{1,0:T(8,128)(2,1)} %refs_0_.1, ...), custom_call_target="tpu_custom_call" | custom-call | tf_op jit(solution)/shard_map/pallas_call | solution.py:433
  20.2 1.7 %collective-permute-start.4 = (bf16[592,128]{1,0:T(8,128)(2,1)}, bf16[592,128]{1,0:T(8,128)(2,1)S(1)}, u32[]{:S(2)}, u32[]{:S(2)}) collective-permute-start(bf16[592,128]{1,0:T(8,128)(2,1)} %get-tuple-element.46), channel_id=1, source_target_pairs={{0,8},{4,12},{8,0},{12,4},{16,24},{20,28},{24,16},{28,20},{1,9},{5... | collective-permute-start | bytes 454664 | tf_op jit(solution)/shard_map/ppermute | solution.py:443
  21.9 1.5 %collective-permute-start.3 = (bf16[592,128]{1,0:T(8,128)(2,1)}, bf16[592,128]{1,0:T(8,128)(2,1)S(1)}, u32[]{:S(2)}, u32[]{:S(2)}) collective-permute-start(bf16[592,128]{1,0:T(8,128)(2,1)} %get-tuple-element.45), channel_id=1, source_target_pairs={{0,4},{4,0},{8,12},{12,8},{16,20},{20,16},{24,28},{28,24},{1,5},{5... | collective-permute-start | bytes 454664 | tf_op jit(solution)/shard_map/ppermute | solution.py:443
  24.0 2.4 %collective-permute-start.6 = (bf16[592,128]{1,0:T(8,128)(2,1)}, bf16[592,128]{1,0:T(8,128)(2,1)S(1)}, u32[]{:S(2)}, u32[]{:S(2)}) collective-permute-start(bf16[592,128]{1,0:T(8,128)(2,1)} %get-tuple-element.49), channel_id=1, source_target_pairs={{0,16},{4,20},{8,24},{12,28},{16,0},{20,4},{24,8},{28,12},{1,17},{... | collective-permute-start | bytes 454664 | tf_op jit(solution)/shard_map/ppermute | solution.py:443
  27.0 2.3 %collective-permute-start.8 = (bf16[592,128]{1,0:T(8,128)(2,1)}, bf16[592,128]{1,0:T(8,128)(2,1)S(1)}, u32[]{:S(2)}, u32[]{:S(2)}) collective-permute-start(bf16[592,128]{1,0:T(8,128)(2,1)} %get-tuple-element.51), channel_id=1, source_target_pairs={{0,24},{4,28},{8,16},{12,20},{16,8},{20,12},{24,0},{28,4},{1,25},{... | collective-permute-start | bytes 454664 | tf_op jit(solution)/shard_map/ppermute | solution.py:443
  29.3 3.6 %collective-permute-start.9 = (bf16[592,128]{1,0:T(8,128)(2,1)}, bf16[592,128]{1,0:T(8,128)(2,1)S(1)}, u32[]{:S(2)}, u32[]{:S(2)}) collective-permute-start(bf16[592,128]{1,0:T(8,128)(2,1)} %get-tuple-element.52), channel_id=1, source_target_pairs={{0,28},{4,24},{8,20},{12,16},{16,12},{20,8},{24,4},{28,0},{1,29},{... | collective-permute-start | bytes 454664 | tf_op jit(solution)/shard_map/ppermute | solution.py:443
  33.0 12.6 %all-to-all-done.v_ref = bf16[8,384,128]{2,1,0:T(8,128)(2,1)S(1)} async-done(((bf16[8,384,128]{2,1,0:T(8,128)(2,1)}), bf16[8,384,128]{2,1,0:T(8,128)(2,1)S(1)}, u32[]{:S(2)}, u32[]{:S(2)}) %all-to-all-start) | async-done | bytes 786464 | tf_op jit(solution)/shard_map/all_to_all | solution.py:492
  46.2 4.2 %all-to-all-start.1 = ((bf16[4,128,128]{2,1,0:T(8,128)(2,1)}), bf16[4,128,128]{2,1,0:T(8,128)(2,1)S(1)}, u32[]{:S(2)}, u32[]{:S(2)}) async-start(bf16[4,128,128]{2,1,0:T(8,128)(2,1)} %broadcast_in_dim.8), calls=%async_computation.1 | async-start | bytes 262144 | tf_op jit(solution)/shard_map/all_to_all | solution.py:527
  51.4 1.2 %collective-permute-done.7.refs_5_ = bf16[592,128]{1,0:T(8,128)(2,1)S(1)} collective-permute-done((bf16[592,128]{1,0:T(8,128)(2,1)}, bf16[592,128]{1,0:T(8,128)(2,1)S(1)}, u32[]{:S(2)}, u32[]{:S(2)}) %collective-permute-start.7) | collective-permute-done | bytes 151584 | tf_op jit(solution)/shard_map/ppermute | solution.py:443
  52.6 2.3 %collective-permute-done.5.refs_3_ = bf16[592,128]{1,0:T(8,128)(2,1)S(1)} collective-permute-done((bf16[592,128]{1,0:T(8,128)(2,1)}, bf16[592,128]{1,0:T(8,128)(2,1)S(1)}, u32[]{:S(2)}, u32[]{:S(2)}) %collective-permute-start.5) | collective-permute-done | bytes 151584 | tf_op jit(solution)/shard_map/ppermute | solution.py:443
  54.8 3.6 %shard_map.85 = (bf16[256,128]{1,0:T(8,128)(2,1)S(1)}, bf16[256,128]{1,0:T(8,128)(2,1)S(1)}, bf16[256,128]{1,0:T(8,128)(2,1)S(1)}, bf16[256,128]{1,0:T(8,128)(2,...) custom-call(s32[1]{0:T(128)} %copy.9.at_ref, ...), custom_call_target="tpu_custom_call" | custom-call | flops 805306368 | bytes 2097152 | tf_op jit(solution)/shard_map/pallas_call | solution.py:433
  58.5 2.1 %shard_map.86 = (bf16[336,128]{1,0:T(8,128)(2,1)S(1)}, bf16[336,128]{1,0:T(8,128)(2,1)S(1)}, bf16[336,128]{1,0:T(8,128)(2,1)S(1)}, bf16[336,128]{1,0:T(8,128)(2,...) custom-call(s32[1]{0:T(128)} %copy.9.at_ref, ...), custom_call_target="tpu_custom_call" | custom-call | tf_op jit(solution)/shard_map/pallas_call | solution.py:433
  60.6 3.9 %collective-permute-start.11 = (bf16[336,128]{1,0:T(8,128)(2,1)S(1)}, bf16[336,128]{1,0:T(8,128)(2,1)S(1)}, u32[]{:S(2)}, u32[]{:S(2)}) collective-permute-start(bf16[336,128]{1,0:T(8,128)(2,1)S(1)} %get-tuple-element.66), channel_id=1, source_target_pairs={{0,8},{4,12},{8,0},{12,4},{16,24},{20,28},{24,16},{28,20},{1,9},{5... | collective-permute-start | bytes 258056 | tf_op jit(solution)/shard_map/ppermute | solution.py:443
  65.2 3.7 %collective-permute-start.14 = (bf16[336,128]{1,0:T(8,128)(2,1)S(1)}, bf16[336,128]{1,0:T(8,128)(2,1)S(1)}, u32[]{:S(2)}, u32[]{:S(2)}) collective-permute-start(bf16[336,128]{1,0:T(8,128)(2,1)S(1)} %get-tuple-element.70), channel_id=1, source_target_pairs={{0,20},{4,16},{8,28},{12,24},{16,4},{20,0},{24,12},{28,8},{1,21},{... | collective-permute-start | bytes 258056 | tf_op jit(solution)/shard_map/ppermute | solution.py:443
  68.9 1.7 %collective-permute-start.15 = (bf16[336,128]{1,0:T(8,128)(2,1)S(1)}, bf16[336,128]{1,0:T(8,128)(2,1)S(1)}, u32[]{:S(2)}, u32[]{:S(2)}) collective-permute-start(bf16[336,128]{1,0:T(8,128)(2,1)S(1)} %get-tuple-element.71), channel_id=1, source_target_pairs={{0,24},{4,28},{8,16},{12,20},{16,8},{20,12},{24,0},{28,4},{1,25},{... | collective-permute-start | bytes 258056 | tf_op jit(solution)/shard_map/ppermute | solution.py:443
  70.6 2.0 %collective-permute-start.16 = (bf16[336,128]{1,0:T(8,128)(2,1)S(1)}, bf16[336,128]{1,0:T(8,128)(2,1)S(1)}, u32[]{:S(2)}, u32[]{:S(2)}) collective-permute-start(bf16[336,128]{1,0:T(8,128)(2,1)S(1)} %get-tuple-element.72), channel_id=1, source_target_pairs={{0,28},{4,24},{8,20},{12,16},{16,12},{20,8},{24,4},{28,0},{1,29},{... | collective-permute-start | bytes 258056 | tf_op jit(solution)/shard_map/ppermute | solution.py:443
  72.7 5.1 %collective-permute-done.13.refs_4_ = bf16[336,128]{1,0:T(8,128)(2,1)S(1)} collective-permute-done((bf16[336,128]{1,0:T(8,128)(2,1)S(1)}, bf16[336,128]{1,0:T(8,128)(2,1)S(1)}, u32[]{:S(2)}, u32[]{:S(2)}) %collective-permute-start.13) | collective-permute-done | bytes 86048 | tf_op jit(solution)/shard_map/ppermute | solution.py:443
  77.8 2.5 %collective-permute-done.14.refs_5_ = bf16[336,128]{1,0:T(8,128)(2,1)S(1)} collective-permute-done((bf16[336,128]{1,0:T(8,128)(2,1)S(1)}, bf16[336,128]{1,0:T(8,128)(2,1)S(1)}, u32[]{:S(2)}, u32[]{:S(2)}) %collective-permute-start.14) | collective-permute-done | bytes 86048 | tf_op jit(solution)/shard_map/ppermute | solution.py:443
  80.5 1.7 %shard_map.87 = bf16[256,1280]{1,0:T(8,128)(2,1)} custom-call(f32[256,1280]{1,0:T(8,128)S(1)} %copy-done, bf16[336,128]{1,0:T(8,128)(2,1)S(1)} %get-tuple-element.64.refs_0_, bf16[336,128]{1,0:T(8,128)(2,1)S(1)} %collective-permute-done.10.refs_1_, bf16[336,128]{1,0:T(8,128)(2,1)S(1)} %collective-permute-done.11.refs_2_, ...), custom_call_target="tpu_custom_call" | custom-call | tf_op jit(solution)/shard_map/pallas_call | solution.py:433
  (36 shorter events, 4.7 us)
Async XLA Ops:
  3.6 7.3 %copy-start.3 = (f32[8,256]{1,0:T(8,128)S(1)}, f32[8,256]{1,0:T(8,128)}, u32[]{:S(2)}) copy-start(f32[8,256]{1,0:T(8,128)} %get-tuple-element.39.refs_3_) | copy-start | bytes 24580
  3.6 41.9 %all-to-all-start = ((bf16[8,384,128]{2,1,0:T(8,128)(2,1)}), bf16[8,384,128]{2,1,0:T(8,128)(2,1)S(1)}, u32[]{:S(2)}, u32[]{:S(2)}) async-start(bf16[8,384,128]{2,1,0:T(8,128)(2,1)} %get-tuple-element.42), calls=%async_computation | async-start | bytes 1572864 | tf_op jit(solution)/shard_map/all_to_all | solution.py:492
  10.9 3.2 %collective-permute-start.2 = (f32[8,256]{1,0:T(8,128)S(1)}, f32[8,256]{1,0:T(8,128)S(1)}, u32[]{:S(2)}, u32[]{:S(2)}) collective-permute-start(f32[8,256]{1,0:T(8,128)S(1)} %copy-done.3), channel_id=1, source_target_pairs={{0,3},{1,2},{2,1},{3,0},{4,7},{5,6},{6,5},{7,4},{8,11},{9,10},{10,... | collective-permute-start | bytes 24584 | tf_op jit(solution)/shard_map/ppermute | solution.py:443
  11.7 3.7 %collective-permute-start.1 = (f32[8,256]{1,0:T(8,128)S(1)}, f32[8,256]{1,0:T(8,128)S(1)}, u32[]{:S(2)}, u32[]{:S(2)}) collective-permute-start(f32[8,256]{1,0:T(8,128)S(1)} %copy-done.3), channel_id=1, source_target_pairs={{0,2},{1,3},{2,0},{3,1},{4,6},{5,7},{6,4},{7,5},{8,10},{9,11},{10,... | collective-permute-start | bytes 24584 | tf_op jit(solution)/shard_map/ppermute | solution.py:443
  12.6 2.8 %collective-permute-start = (f32[8,256]{1,0:T(8,128)S(1)}, f32[8,256]{1,0:T(8,128)S(1)}, u32[]{:S(2)}, u32[]{:S(2)}) collective-permute-start(f32[8,256]{1,0:T(8,128)S(1)} %copy-done.3), channel_id=1, source_target_pairs={{0,1},{1,0},{2,3},{3,2},{4,5},{5,4},{6,7},{7,6},{8,9},{9,8},{10,11... | collective-permute-start | bytes 24584 | tf_op jit(solution)/shard_map/ppermute | solution.py:443
  14.1 1.3 %copy-start.4 = (f32[8,256]{1,0:T(8,128)}, f32[8,256]{1,0:T(8,128)S(1)}, u32[]{:S(2)}) copy-start(f32[8,256]{1,0:T(8,128)S(1)} %collective-permute-done.2.refs_6_) | copy-start | bytes 24580
  20.2 9.1 %collective-permute-start.4 = (bf16[592,128]{1,0:T(8,128)(2,1)}, bf16[592,128]{1,0:T(8,128)(2,1)S(1)}, u32[]{:S(2)}, u32[]{:S(2)}) collective-permute-start(bf16[592,128]{1,0:T(8,128)(2,1)} %get-tuple-element.46), channel_id=1, source_target_pairs={{0,8},{4,12},{8,0},{12,4},{16,24},{20,28},{24,16},{28,20},{1,9},{5... | collective-permute-start | bytes 454664 | tf_op jit(solution)/shard_map/ppermute | solution.py:443
  21.9 23.7 %collective-permute-start.3 = (bf16[592,128]{1,0:T(8,128)(2,1)}, bf16[592,128]{1,0:T(8,128)(2,1)S(1)}, u32[]{:S(2)}, u32[]{:S(2)}) collective-permute-start(bf16[592,128]{1,0:T(8,128)(2,1)} %get-tuple-element.45), channel_id=1, source_target_pairs={{0,4},{4,0},{8,12},{12,8},{16,20},{20,16},{24,28},{28,24},{1,5},{5... | collective-permute-start | bytes 454664 | tf_op jit(solution)/shard_map/ppermute | solution.py:443
  24.0 27.4 %collective-permute-start.6 = (bf16[592,128]{1,0:T(8,128)(2,1)}, bf16[592,128]{1,0:T(8,128)(2,1)S(1)}, u32[]{:S(2)}, u32[]{:S(2)}) collective-permute-start(bf16[592,128]{1,0:T(8,128)(2,1)} %get-tuple-element.49), channel_id=1, source_target_pairs={{0,16},{4,20},{8,24},{12,28},{16,0},{20,4},{24,8},{28,12},{1,17},{... | collective-permute-start | bytes 454664 | tf_op jit(solution)/shard_map/ppermute | solution.py:443
  26.4 26.2 %collective-permute-start.7 = (bf16[592,128]{1,0:T(8,128)(2,1)}, bf16[592,128]{1,0:T(8,128)(2,1)S(1)}, u32[]{:S(2)}, u32[]{:S(2)}) collective-permute-start(bf16[592,128]{1,0:T(8,128)(2,1)} %get-tuple-element.50), channel_id=1, source_target_pairs={{0,20},{4,16},{8,28},{12,24},{16,4},{20,0},{24,12},{28,8},{1,21},{... | collective-permute-start | bytes 454664 | tf_op jit(solution)/shard_map/ppermute | solution.py:443
  27.0 25.6 %collective-permute-start.8 = (bf16[592,128]{1,0:T(8,128)(2,1)}, bf16[592,128]{1,0:T(8,128)(2,1)S(1)}, u32[]{:S(2)}, u32[]{:S(2)}) collective-permute-start(bf16[592,128]{1,0:T(8,128)(2,1)} %get-tuple-element.51), channel_id=1, source_target_pairs={{0,24},{4,28},{8,16},{12,20},{16,8},{20,12},{24,0},{28,4},{1,25},{... | collective-permute-start | bytes 454664 | tf_op jit(solution)/shard_map/ppermute | solution.py:443
  29.3 23.2 %collective-permute-start.9 = (bf16[592,128]{1,0:T(8,128)(2,1)}, bf16[592,128]{1,0:T(8,128)(2,1)S(1)}, u32[]{:S(2)}, u32[]{:S(2)}) collective-permute-start(bf16[592,128]{1,0:T(8,128)(2,1)} %get-tuple-element.52), channel_id=1, source_target_pairs={{0,28},{4,24},{8,20},{12,16},{16,12},{20,8},{24,4},{28,0},{1,29},{... | collective-permute-start | bytes 454664 | tf_op jit(solution)/shard_map/ppermute | solution.py:443
  45.6 9.3 %collective-permute-start.5 = (bf16[592,128]{1,0:T(8,128)(2,1)}, bf16[592,128]{1,0:T(8,128)(2,1)S(1)}, u32[]{:S(2)}, u32[]{:S(2)}) collective-permute-start(bf16[592,128]{1,0:T(8,128)(2,1)} %get-tuple-element.48), channel_id=1, source_target_pairs={{0,12},{4,8},{8,4},{12,0},{16,28},{20,24},{24,20},{28,16},{1,13},{... | collective-permute-start | bytes 454664 | tf_op jit(solution)/shard_map/ppermute | solution.py:443
  46.2 12.2 %all-to-all-start.1 = ((bf16[4,128,128]{2,1,0:T(8,128)(2,1)}), bf16[4,128,128]{2,1,0:T(8,128)(2,1)S(1)}, u32[]{:S(2)}, u32[]{:S(2)}) async-start(bf16[4,128,128]{2,1,0:T(8,128)(2,1)} %broadcast_in_dim.8), calls=%async_computation.1 | async-start | bytes 262144 | tf_op jit(solution)/shard_map/all_to_all | solution.py:527
  50.4 0.9 %copy-start.1 = (bf16[592,128]{1,0:T(8,128)(2,1)S(1)}, bf16[592,128]{1,0:T(8,128)(2,1)}, u32[]{:S(2)}) copy-start(bf16[592,128]{1,0:T(8,128)(2,1)} %get-tuple-element.44.in_ref) | copy-start | bytes 454660
  51.4 7.1 %copy-start.2 = (f32[1280]{0:T(1024)S(1)}, f32[1280]{0:T(1024)}, u32[]{:S(2)}) copy-start(f32[1280]{0:T(1024)} %param.12) | copy-start | bytes 15364
  58.5 22.0 %copy-start = (f32[256,1280]{1,0:T(8,128)S(1)}, f32[256,1280]{1,0:T(8,128)}, u32[]{:S(2)}) copy-start(f32[256,1280]{1,0:T(8,128)} %get-tuple-element.40.own_ref) | copy-start | bytes 3932164
  60.6 10.0 %collective-permute-start.11 = (bf16[336,128]{1,0:T(8,128)(2,1)S(1)}, bf16[336,128]{1,0:T(8,128)(2,1)S(1)}, u32[]{:S(2)}, u32[]{:S(2)}) collective-permute-start(bf16[336,128]{1,0:T(8,128)(2,1)S(1)} %get-tuple-element.66), channel_id=1, source_target_pairs={{0,8},{4,12},{8,0},{12,4},{16,24},{20,28},{24,16},{28,20},{1,9},{5... | collective-permute-start | bytes 258056 | tf_op jit(solution)/shard_map/ppermute | solution.py:443
  64.5 8.2 %collective-permute-start.10 = (bf16[336,128]{1,0:T(8,128)(2,1)S(1)}, bf16[336,128]{1,0:T(8,128)(2,1)S(1)}, u32[]{:S(2)}, u32[]{:S(2)}) collective-permute-start(bf16[336,128]{1,0:T(8,128)(2,1)S(1)} %get-tuple-element.65), channel_id=1, source_target_pairs={{0,4},{4,0},{8,12},{12,8},{16,20},{20,16},{24,28},{28,24},{1,5},{5... | collective-permute-start | bytes 258056 | tf_op jit(solution)/shard_map/ppermute | solution.py:443
  65.0 12.8 %collective-permute-start.13 = (bf16[336,128]{1,0:T(8,128)(2,1)S(1)}, bf16[336,128]{1,0:T(8,128)(2,1)S(1)}, u32[]{:S(2)}, u32[]{:S(2)}) collective-permute-start(bf16[336,128]{1,0:T(8,128)(2,1)S(1)} %get-tuple-element.69), channel_id=1, source_target_pairs={{0,16},{4,20},{8,24},{12,28},{16,0},{20,4},{24,8},{28,12},{1,17},{... | collective-permute-start | bytes 258056 | tf_op jit(solution)/shard_map/ppermute | solution.py:443
  65.2 15.1 %collective-permute-start.14 = (bf16[336,128]{1,0:T(8,128)(2,1)S(1)}, bf16[336,128]{1,0:T(8,128)(2,1)S(1)}, u32[]{:S(2)}, u32[]{:S(2)}) collective-permute-start(bf16[336,128]{1,0:T(8,128)(2,1)S(1)} %get-tuple-element.70), channel_id=1, source_target_pairs={{0,20},{4,16},{8,28},{12,24},{16,4},{20,0},{24,12},{28,8},{1,21},{... | collective-permute-start | bytes 258056 | tf_op jit(solution)/shard_map/ppermute | solution.py:443
  68.9 11.4 %collective-permute-start.15 = (bf16[336,128]{1,0:T(8,128)(2,1)S(1)}, bf16[336,128]{1,0:T(8,128)(2,1)S(1)}, u32[]{:S(2)}, u32[]{:S(2)}) collective-permute-start(bf16[336,128]{1,0:T(8,128)(2,1)S(1)} %get-tuple-element.71), channel_id=1, source_target_pairs={{0,24},{4,28},{8,16},{12,20},{16,8},{20,12},{24,0},{28,4},{1,25},{... | collective-permute-start | bytes 258056 | tf_op jit(solution)/shard_map/ppermute | solution.py:443
  70.6 9.7 %collective-permute-start.16 = (bf16[336,128]{1,0:T(8,128)(2,1)S(1)}, bf16[336,128]{1,0:T(8,128)(2,1)S(1)}, u32[]{:S(2)}, u32[]{:S(2)}) collective-permute-start(bf16[336,128]{1,0:T(8,128)(2,1)S(1)} %get-tuple-element.72), channel_id=1, source_target_pairs={{0,28},{4,24},{8,20},{12,16},{16,12},{20,8},{24,4},{28,0},{1,29},{... | collective-permute-start | bytes 258056 | tf_op jit(solution)/shard_map/ppermute | solution.py:443
  72.7 7.8 %collective-permute-start.12 = (bf16[336,128]{1,0:T(8,128)(2,1)S(1)}, bf16[336,128]{1,0:T(8,128)(2,1)S(1)}, u32[]{:S(2)}, u32[]{:S(2)}) collective-permute-start(bf16[336,128]{1,0:T(8,128)(2,1)S(1)} %get-tuple-element.68), channel_id=1, source_target_pairs={{0,12},{4,8},{8,4},{12,0},{16,28},{20,24},{24,20},{28,16},{1,13},{... | collective-permute-start | bytes 258056 | tf_op jit(solution)/shard_map/ppermute | solution.py:443
  (2 other events, 1.2 us)

commit v6 on v5

--- a/solution.py
+++ b/solution.py
@@ -91,6 +91,7 @@
 LSE_ROW = 6
 NORM_ROW = 9
 MASK_ROW = 15
+ONES = 8
 
 
 def dot_t(a, b):
@@ -118,16 +119,9 @@
     return (rows.astype(jnp.float32) * column * gain).astype(jnp.bfloat16)
 
 
-def first_kernel(n, pos, q_ref, k_ref, v_ref, sum_ref, out_ref, held, cut, sems, v_sems):
-    tok = q_ref.shape[0]
-    chunks = sems.shape[1]
+def cut_kernel(n, pos, k_ref, v_ref, out_ref, cut, sems):
+    tok = k_ref.shape[0]
     parts = tok // pos
-    step = tok // chunks
-    copies = []
-    for t, ref in enumerate((q_ref, k_ref)):
-        for c in range(chunks):
-            rows = pl.ds(c * step, step)
-            copies.append(pltpu.make_async_copy(ref.at[rows], held.at[t, rows], sems.at[t, c]))
     loads, stores = [], []
     for d in range(n):
         row = d % parts * pos
@@ -141,11 +135,29 @@
                 pltpu.make_async_copy(
                     ref.at[pl.ds(row, rows), pl.ds(head * HD, HD)],
                     cut.at[d, pl.ds(at, rows)],
-                    v_sems.at[j, d],
+                    sems.at[j, d],
                 )
             )
-        stores.append(pltpu.make_async_copy(cut.at[d], out_ref.at[d], v_sems.at[3, d]))
-    for copy in copies + loads:
+            loads[-1].start()
+        stores.append(pltpu.make_async_copy(cut.at[d], out_ref.at[d], sems.at[3, d]))
+    for d in range(n):
+        for copy in loads[3 * d : 3 * d + 3]:
+            copy.wait()
+        stores[d].start()
+    for copy in stores:
+        copy.wait()
+
+
+def squares_kernel(q_ref, k_ref, out_ref, held, sems):
+    tok = q_ref.shape[0]
+    chunks = sems.shape[1]
+    step = tok // chunks
+    copies = []
+    for t, ref in enumerate((q_ref, k_ref)):
+        for c in range(chunks):
+            rows = pl.ds(c * step, step)
+            copies.append(pltpu.make_async_copy(ref.at[rows], held.at[t, rows], sems.at[t, c]))
+    for copy in copies:
         copy.start()
     rows = []
     for t in range(2):
@@ -159,13 +171,7 @@
                 total = part * part if total is None else total + part * part
             parts.append(total)
         rows.append(jnp.sum(jnp.concatenate(parts, axis=0).T, axis=0, keepdims=True))
-    sum_ref[...] = jnp.concatenate(rows + [jnp.zeros((6, tok), jnp.float32)], axis=0)
-    for copy in loads:
-        copy.wait()
-    for copy in stores:
-        copy.start()
-    for copy in stores:
-        copy.wait()
+    out_ref[...] = jnp.concatenate(rows + [jnp.zeros((6, tok), jnp.float32)], axis=0)
 
 
 def copy_kernel(in_ref, out_ref):
@@ -273,143 +279,194 @@
         copy.wait()
 
 
-def pencil(n, query, keys, vals, lse, anchor_keys, anchor_vals, flags, put):
-    keep = []
-    for i in range(query.shape[0] // BLOCK):
-        rows = slice(i * BLOCK, (i + 1) * BLOCK)
-        scores = blocked_scores(query[rows], keys, flags[i], i)
-        top = jnp.max(scores, axis=1, keepdims=True)
-        out, total = weigh(jnp.exp2(scores - top), vals)
-        temporal = out / total
-        scores = dot_t(query[rows], anchor_keys)
-        top = jnp.maximum(jnp.max(scores, axis=1, keepdims=True), lse[rows])
-        own = jnp.exp2(lse[rows] - top)
-        out, total = weigh(jnp.exp2(scores - top), anchor_vals)
-        scale = 1.0 / (total + own)
-        result = (temporal + out * scale).astype(jnp.bfloat16)
-        keep.append(own * scale)
-        gp = query.shape[0] // n
-        for j in range(BLOCK // gp):
-            put(i * (BLOCK // gp) + j, result[j * gp : (j + 1) * gp])
-    return jnp.concatenate(keep, axis=0)
-
-
-def add_side(side, keep, gp, first):
-    n = side.shape[0]
-    lane = lax.broadcasted_iota(jnp.int32, side.shape, 2)
-    keep = keep.reshape(n, gp, HD)
-    for g in range(gp // ROWS):
-        side = jnp.where(lane == first + g, keep[:, g * ROWS : (g + 1) * ROWS, :], side)
-    return side
-
-
-def read_side(blocks, at, col_ref, mask_ref):
-    whole, part, norm, masks = [], [], [], []
+def inverse(value):
+    guess = pl.reciprocal(value, approx=True)
+    return guess * (2.0 - value * guess)
+
+
+def turned(vals):
+    return jnp.concatenate([vals.T, jnp.ones((ONES, vals.shape[0]), vals.dtype)], axis=0)
+
+
+def turn_kernel(n, tok, pos, at_ref, v_ref, out_ref):
+    gp = tok // n
+    me = lax.axis_index("frame")
+    for g in range((tok + pos) // gp):
+        rows = [v_ref[me ^ s, g * gp : (g + 1) * gp, :] for s in range(n)]
+        out_ref[g] = turned(jnp.concatenate(rows, axis=0))
+    out_ref[(tok + pos) // gp] = turned(v_ref[at_ref[0], :tok, :])
+
+
+def attend_tiles(tiles):
+    scores = [(dot_t(t[1], t[0]), dot_t(t[3], t[0])) for t in tiles]
+    weights = []
+    for t, (paired, anchored) in zip(tiles, scores):
+        lse, flag, i = t[5:]
+        near = paired[i * BLOCK : (i + 1) * BLOCK]
+        away = paired[(1 - i) * BLOCK : (2 - i) * BLOCK] + flag
+        top = jnp.maximum(
+            jnp.max(near, axis=0, keepdims=True), jnp.max(away, axis=0, keepdims=True)
+        )
+        both = [jnp.exp2(near - top), jnp.exp2(away - top)]
+        both = jnp.concatenate(both if i == 0 else both[::-1], axis=0)
+        top = jnp.maximum(jnp.max(anchored, axis=0, keepdims=True), lse)
+        own = jnp.exp2(lse - top)
+        anchored = jnp.exp2(anchored - top)
+        weights.append((both.astype(jnp.bfloat16), anchored.astype(jnp.bfloat16), own))
+    sums = [
+        (
+            jnp.dot(t[2], both, preferred_element_type=jnp.float32),
+            jnp.dot(t[4], anchored, preferred_element_type=jnp.float32),
+            own,
+        )
+        for t, (both, anchored, own) in zip(tiles, weights)
+    ]
+    results = []
+    for paired, anchored, own in sums:
+        scale = inverse(anchored[HD : HD + 1] + own)
+        result = paired[:HD] * inverse(paired[HD : HD + 1]) + anchored[:HD] * scale
+        results.append((result.T.astype(jnp.bfloat16), own * scale))
+    return results
+
+
+def spin(rows, parts):
+    parts %= HD // rows[1]
+    return rows[0] if parts == 0 else pltpu.roll(rows[0], parts * rows[1], 1)
+
+
+def gather_lanes(rows, place, gp):
+    lane = lax.broadcasted_iota(jnp.int32, (1, HD), 1) // gp
+    out = None
+    for j in range(rows.shape[0]):
+        row = spin((rows, gp), j - place)[j : j + 1]
+        out = row if out is None else jnp.where(lane == j, row, out)
+    return out
+
+
+def scatter_lanes(kept, row, place, gp):
+    lane = lax.broadcasted_iota(jnp.int32, (1, HD), 1) // gp
+    for j in range(len(kept)):
+        kept[j] = jnp.where(lane == place, spin((row, gp), place - j), kept[j])
+
+
+def side_rows(blocks, at, first):
+    rows = []
     for block in blocks:
         side = block[at : at + ROWS, :].astype(jnp.float32)
-
-        def joined(first):
-            return side[first : first + 1] + side[first + 1 : first + 2] + side[first + 2 : first + 3]
-
-        whole += [joined(0), joined(3)]
-        part.append(joined(LSE_ROW))
-        norm += [joined(NORM_ROW), joined(NORM_ROW + 3)]
-        masks.append(side[MASK_ROW : MASK_ROW + 1])
-    mask_ref[...] = jnp.concatenate(masks, axis=0)
-    rows = whole + part + norm
-    rows.append(jnp.zeros((HD - len(rows), HD), jnp.float32))
-    col_ref[...] = jnp.concatenate(rows, axis=0).T
-
-
-def pencil_flags(mask_ref, row, upper):
-    mask = mask_ref[pl.ds(row, 1), :]
-    flags = [jnp.where(mask[:, i : i + 1] == 1.0, 0.0, NEG) for i in range(2)]
-    return [jnp.where(upper, flags[1 - i], flags[i]) for i in range(2)]
-
-
-def run_pencil(n, gp, mask_ref, query, keys, vals, lse, ka, va, row, outs, at, side):
-    me = lax.axis_index("frame")
-
-    def put(s, result):
-        outs[s][at : at + gp, :] = result
-
-    flags = pencil_flags(mask_ref, row ^ me, me >= n // 2)
-    lse = jnp.concatenate(lse, axis=0)
-    keep = pencil(n, query, keys, vals, lse, ka, va, flags, put)
-    return add_side(side, keep, gp, at // ROWS)
+        rows.append(side[first : first + 1] + side[first + 1 : first + 2] + side[first + 2 : first + 3])
+    return jnp.concatenate(rows, axis=0)
+
+
+def keep_flags(n, blocks, at, flag_ref):
+    masks = [block[at : at + ROWS, :].astype(jnp.float32)[MASK_ROW:] for block in blocks]
+    masks = jnp.concatenate(masks, axis=0)
+    flags = [jnp.broadcast_to(masks[:, i : i + 1], (n, HD)) for i in range(2)]
+    flags = [jnp.where(flag == 1.0, 0.0, NEG) for flag in flags]
+    upper = lax.axis_index("frame") >= n // 2
+    for i in range(2):
+        flag_ref[i] = jnp.where(upper, flags[1 - i], flags[i])
 
 
 def stack_rows(blocks, at, gp):
     return jnp.concatenate([block[at : at + gp, :] for block in blocks], axis=0)
 
 
-def whole_kernel(n, tok, pos, at_ref, v_ref, *refs):
+def whole_kernel(n, tok, pos, at_ref, vt_ref, *refs):
     blocks, outs, side_ref = refs[:n], refs[n : 2 * n], refs[2 * n]
-    col_ref, mask_ref, key_ref = refs[2 * n + 1 :]
+    key_ref, flag_ref = refs[2 * n + 1 :]
     gp = tok // n
+    per = n // 2
     me = lax.axis_index("frame")
-    anchor = at_ref[0]
     for s in range(n):
 
-        @pl.when(anchor == me ^ s)
+        @pl.when(at_ref[0] == me ^ s)
         def _():
             key_ref[...] = blocks[s][tok : 2 * tok, :]
 
-    read_side(blocks, 2 * tok + pos, col_ref, mask_ref)
-    ka, va = key_ref[...], v_ref[anchor, :tok, :]
-    values = [v_ref.at[me ^ s] for s in range(n)]
-    side = jnp.zeros((n, ROWS, HD), jnp.float32)
-    for g in range(n):
-        half, first, at = g * gp // BLOCK, g * gp % BLOCK, g * gp
-        lse = [col_ref[first : first + gp, 2 * s + half : 2 * s + half + 1] for s in range(n)]
-        query, keys = stack_rows(blocks, at, gp), stack_rows(blocks, tok + at, gp)
-        vals = stack_rows(values, at, gp)
-        side = run_pencil(
-            n, gp, mask_ref, query, keys, vals, lse, ka, va, g, outs, at, side
-        )
-    side_ref[...] = side
-
-
-def part_kernel(n, tok, pos, at_ref, gain_ref, held_ref, v_ref, *refs):
-    blocks, done, (came_ref, col_ref, mask_ref) = refs[:n], refs[n : 2 * n], refs[2 * n : 2 * n + 3]
-    outs = refs[2 * n + 3 :]
+    at_side = 2 * tok + pos
+    keep_flags(n, blocks, at_side, flag_ref)
+    ka, va = key_ref[...], vt_ref[(tok + pos) // gp]
+    halves = [blocks[:per], blocks[per:]]
+    lses = [[side_rows(half, at_side, 3 * b) for b in range(2)] for half in halves]
+    kept = [[[jnp.zeros((1, HD), jnp.float32)] * per for _ in range(2)] for _ in range(2)]
+    across = BLOCK // gp
+    together = 2
+    for g0 in range(0, n, together):
+        tiles, places = [], []
+        for g in range(g0, g0 + together):
+            keys = stack_rows(blocks, tok + g * gp, gp)
+            for i, half in enumerate(halves):
+                query = stack_rows(half, g * gp, gp)
+                lse = gather_lanes(lses[i][g // across], g % across, gp)
+                flag = flag_ref[i, pl.ds(g ^ me, 1), :]
+                tiles.append((query, keys, vt_ref[g], ka, va, lse, flag, i))
+                places.append((g, i))
+        for (g, i), (result, keep) in zip(places, attend_tiles(tiles)):
+            for j in range(per):
+                outs[i * per + j][g * gp : (g + 1) * gp, :] = result[j * gp : (j + 1) * gp]
+            scatter_lanes(kept[i][g // across], keep, g % across, gp)
+    rows = [kept[s // per][b][s % per] for s in range(n) for b in range(2)]
+    side_ref[...] = jnp.concatenate(rows, axis=0)
+
+
+def part_kernel(n, tok, pos, at_ref, gain_ref, held_ref, vt_ref, v_ref, *refs):
+    blocks, done, came_ref = refs[:n], refs[n : 2 * n], refs[2 * n]
+    outs, flag_ref, col_ref = refs[2 * n + 1 : 3 * n + 1], refs[3 * n + 1], refs[3 * n + 2]
     gp = tok // n
+    per = n // 2
     parts = tok // pos
     me = lax.axis_index("frame")
     anchor = at_ref[0]
     quarter = me % parts
+    odd = quarter * pos % BLOCK != 0
+    late = quarter * pos >= BLOCK
     gain = jnp.where(me // parts == 1, gain_ref[n + 1 : n + 2, :], gain_ref[n : n + 1, :])
-    late = quarter * pos >= BLOCK
-    for s in range(n):
-        outs[s][:tok, :] = done[s][...]
-    norm = []
-    for half in range(tok // BLOCK):
-        norm.append(jnp.zeros((BLOCK, 1), jnp.float32))
-        for s in range(n):
-            lane = 3 * n + 2 * s + half
-            norm[-1] = jnp.where(anchor == me ^ s, col_ref[:, lane : lane + 1], norm[-1])
-    va = jnp.concatenate([held_ref[j, :pos, :] for j in range(parts)], axis=0)
+    at_side = 2 * tok + pos
+    keep_flags(n, blocks, at_side, flag_ref)
+    norms = [side_rows(blocks, at_side, NORM_ROW + 3 * b) for b in range(2)]
+    rows = [jnp.where(late, norms[1], norms[0])]
+    for norm in norms:
+        row = norm[0:1]
+        for s in range(1, n):
+            row = jnp.where(anchor == me ^ s, norm[s : s + 1], row)
+        rows.append(row)
+    rows.append(jnp.zeros((HD - n - 2, HD), jnp.float32))
+    col_ref[...] = jnp.concatenate(rows, axis=0).T
+    va = turned(jnp.concatenate([held_ref[j, :pos, :] for j in range(parts)], axis=0))
     ka = jnp.concatenate([held_ref[j, pos:, :] for j in range(parts)], axis=0)
-    ka = scaled(ka, jnp.concatenate(norm, axis=0), gain)
-    values = [v_ref.at[me ^ s] for s in range(n)]
-    side = came_ref[...]
+    norm = jnp.concatenate([col_ref[:, n + b : n + b + 1] for b in range(2)], axis=0)
+    ka = scaled(ka, norm, gain)
+    halves = [blocks[:per], blocks[per:]]
+    lses = []
+    for half in halves:
+        lse = side_rows(half, at_side, LSE_ROW)
+        lses.append(jnp.where(odd, pltpu.roll(lse, HD - pos, 1), lse))
+    kept = [[jnp.zeros((1, HD), jnp.float32)] * per for _ in range(2)]
+    tiles, places = [], []
     for u in range(pos // gp):
         first = pl.multiple_of(quarter * pos % BLOCK + u * gp, gp)
         cols = col_ref[pl.ds(first, gp), :]
-        lse, norm = [], []
-        for s in range(n):
-            lse.append(cols[:, 2 * n + s : 2 * n + s + 1])
-            lane = 3 * n + 2 * s
-            norm.append(jnp.where(late, cols[:, lane + 1 : lane + 2], cols[:, lane : lane + 1]))
-        at = tok + u * gp
-        query, vals = stack_rows(blocks, tok + at, gp), stack_rows(values, at, gp)
-        keys = scaled(stack_rows(values, at + pos, gp), jnp.concatenate(norm, axis=0), gain)
-        row = quarter * (pos // gp) + u
-        side = run_pencil(
-            n, gp, mask_ref, query, keys, vals, lse, ka, va, row, outs, at, side
-        )
+        norm = jnp.concatenate([cols[:, s : s + 1] for s in range(n)], axis=0)
+        at = tok + pos + u * gp
+        keys = jnp.concatenate([v_ref[me ^ s, at : at + gp, :] for s in range(n)], axis=0)
+        keys = scaled(keys, norm, gain)
+        for i, half in enumerate(halves):
+            query = stack_rows(half, 2 * tok + u * gp, gp)
+            lse = gather_lanes(lses[i], u, gp)
+            flag = flag_ref[i, pl.ds((quarter * (pos // gp) + u) ^ me, 1), :]
+            tiles.append((query, keys, vt_ref[n + u], ka, va, lse, flag, i))
+            places.append((tok + u * gp, u, i))
     for s in range(n):
-        outs[s][tok + pos : tok + pos + ROWS, :] = side[s].astype(jnp.bfloat16)
+        outs[s][:tok, :] = done[s][...]
+    for (at, u, i), (result, keep) in zip(places, attend_tiles(tiles)):
+        for j in range(per):
+            outs[i * per + j][at : at + gp, :] = result[j * gp : (j + 1) * gp]
+        scatter_lanes(kept[i], keep, u, gp)
+    pad = jnp.zeros((ROWS - 3, HD), jnp.float32)
+    for s in range(n):
+        rows = [came_ref[2 * s : 2 * s + 2, :], kept[s // per][s % per], pad]
+        rows = jnp.concatenate(rows, axis=0)
+        outs[s][tok + pos : tok + pos + ROWS, :] = rows.astype(jnp.bfloat16)
 
 
 def join_kernel(n, pos, own_ref, *refs):
@@ -417,16 +474,26 @@
     tok = own_ref.shape[0]
     parts = tok // pos
     me = lax.axis_index("frame")
+    at_side = tok + pos
+    sides = jnp.concatenate([block[at_side : at_side + ROWS, :] for block in back], axis=0).T
+    sub = lax.broadcasted_iota(jnp.int32, (n * ROWS, HD), 0)
+
+    def spread_lanes(row):
+        pick = (sub == row).astype(jnp.bfloat16)
+        return jnp.dot(sides, pick, preferred_element_type=jnp.float32)
+
     for s in range(n):
         d = me ^ s
-        side = back[s][tok + pos : tok + pos + ROWS, :].astype(jnp.float32)
-        row = pl.multiple_of(d % parts * pos, pos)
-        for head, rows, at in ((d, pl.ds(0, tok), 0), (n + d // parts, pl.ds(row, pos), tok)):
-            cols = pl.ds(pl.multiple_of(head * HD, HD), HD)
-            keep = [side[:, g : g + 1] for g in range(at // ROWS, (at + rows.size) // ROWS)]
-            keep = jnp.concatenate(keep, axis=0)
-            got = back[s][at : at + rows.size, :].astype(jnp.float32)
-            out_ref[rows, cols] = (own_ref[rows, cols] * keep + got).astype(jnp.bfloat16)
+        keeps = [spread_lanes(s * ROWS + r) for r in range(3)]
+        whole = pl.ds(pl.multiple_of(d * HD, HD), HD)
+        for b in range(tok // BLOCK):
+            rows = slice(b * BLOCK, (b + 1) * BLOCK)
+            got = back[s][rows, :].astype(jnp.float32)
+            out_ref[rows, whole] = (own_ref[rows, whole] * keeps[b] + got).astype(jnp.bfloat16)
+        part = pl.ds(pl.multiple_of((n + d // parts) * HD, HD), HD)
+        rows = pl.ds(pl.multiple_of(d % parts * pos, pos), pos)
+        got = back[s][tok : tok + pos, :].astype(jnp.float32)
+        out_ref[rows, part] = (own_ref[rows, part] * keeps[2][:pos] + got).astype(jnp.bfloat16)
 
 
 def call(kernel, out_shape, *args, vmem=40, **more):
@@ -472,20 +539,24 @@
     dma = pltpu.SemaphoreType.DMA
     bf16, f32 = jnp.bfloat16, jnp.float32
 
-    sums, v_blocks = call(
-        functools.partial(first_kernel, n, pos),
-        (shape((8, tok), f32), shape((n, tok + 2 * pos, HD), bf16)),
+    v_blocks = call(
+        functools.partial(cut_kernel, n, pos),
+        shape((n, tok + 2 * pos, HD), bf16),
+        k_raw,
+        values,
+        in_specs=[hbm] * 2,
+        out_specs=hbm,
+        scratch_shapes=[pltpu.VMEM((n, tok + 2 * pos, HD), bf16), dma((4, n))],
+        vmem=60,
+    )
+    q_raw, k_raw, values, v_blocks = lax.optimization_barrier((q_raw, k_raw, values, v_blocks))
+    sums = call(
+        squares_kernel,
+        shape((8, tok), f32),
         q_raw,
         k_raw,
-        values,
-        in_specs=[hbm] * 3,
-        out_specs=(vm, hbm),
-        scratch_shapes=[
-            pltpu.VMEM((2, tok, width), bf16),
-            pltpu.VMEM((n, tok + 2 * pos, HD), bf16),
-            dma((2, 4)),
-            dma((4, n)),
-        ],
+        in_specs=[hbm] * 2,
+        scratch_shapes=[pltpu.VMEM((2, tok, width), bf16), dma((2, 4))],
         vmem=60,
     )
     all_sums = [sums] + [pairwise(sums, "mp", step) for step in range(1, n_mp)]
@@ -532,16 +603,23 @@
         axis_index_groups=groups,
         tiled=True,
     )
-    exps = n * tok * 2 * tok
-    *done, side, columns, masks = call(
-        functools.partial(whole_kernel, n, tok, pos),
-        [shape((tok, HD), bf16)] * n
-        + [shape((n, ROWS, HD), f32), shape((HD, HD), f32), shape((n, HD), f32)],
+    pencils = (tok + pos) // (tok // n)
+    vt = call(
+        functools.partial(turn_kernel, n, tok, pos),
+        shape((pencils + 1, HD + ONES, tok), bf16),
         anchor_frame,
         v_far,
+        in_specs=[sm, vm],
+    )
+    exps = n * tok * 2 * tok
+    *done, side = call(
+        functools.partial(whole_kernel, n, tok, pos),
+        [shape((tok, HD), bf16)] * n + [shape((2 * n, HD), f32)],
+        anchor_frame,
+        vt,
         *far,
         in_specs=[sm] + [vm] * (n + 1),
-        scratch_shapes=[pltpu.VMEM((tok, HD), bf16)],
+        scratch_shapes=[pltpu.VMEM((tok, HD), bf16), pltpu.VMEM((2, n, HD), f32)],
         cost_estimate=pl.CostEstimate(
             flops=6 * exps * HD, bytes_accessed=8 * n * tok * HD, transcendentals=exps
         ),
@@ -552,13 +630,13 @@
         anchor_frame,
         k_gain.reshape(heads, HD),
         held,
+        vt,
         v_far,
         *far,
         *done,
         side,
-        columns,
-        masks,
-        in_specs=[sm] + [vm] * (2 * n + 6),
+        in_specs=[sm] + [vm] * (2 * n + 5),
+        scratch_shapes=[pltpu.VMEM((2, n, HD), f32), pltpu.VMEM((HD, HD), f32)],
     )
     back = swap_blocks(result)
     return call(

time: 82.6 us -> 77.9 us (0.943)
  Pallas kernels: 15.2 us -> 12.9 us
  waiting for transfers between devices: 26.4 us -> 24.9 us
  local copies, waits for them, and re-layouts: 2.19 us -> 1.29 us
    all_to_all x1, waiting for transfers between devices: 12.6 us -> 9.68 us  [local_heads(): lax.all_to_all(v_blocks, 'frame', split_axis=0, concat_axis=0, tiled=True)]
    pallas_call x6 -> x8, Pallas kernels: 15.2 us -> 12.9 us  [call(): pl.pallas_call(kernel, out_shape=out_shape, compiler_params=pltpu.Compile...]
    ppermute x17, waiting for transfers between devices: 13.8 us -> 15.3 us  [pairwise(): return lax.ppermute(array, axis, [(i, i ^ step) for i in range(size)])]
    unnamed x14 -> x12, local copies, waits for them, and re-layouts: 1.53 us -> 0.62 us
  transfers between devices with their start and end apart: 19 -> 19, of which waited for: 8 -> 9; matrix products, arithmetic and copies ran while one was open for 1% -> 1% of each run, Pallas kernels for 10% -> 11%
where the time goes in v6:
time: 77.9 us; the launch traced here: 77.5 us
  starting transfers between devices  37.6 us (48%)
  waiting for transfers between devices  24.9 us (32%)
  Pallas kernels  12.9 us (17%)
  local copies, waits for them, and re-layouts  1.29 us (2%)
    ppermute x17, starting transfers between devices, pairwise(): return lax.ppermute(array, axis, [(i, i ^ step) for i in range(size)])  26.2 us
    ppermute x17, waiting for transfers between devices, pairwise(): return lax.ppermute(array, axis, [(i, i ^ step) for i in range(size)])  15.3 us
    pallas_call x8, Pallas kernels, call(): pl.pallas_call(kernel, out_shape=out_shape, compiler_params=pltpu.Compile...  12.9 us
    all_to_all x1, waiting for transfers between devices, local_heads(): lax.all_to_all(v_blocks, 'frame', split_axis=0, concat_axis=0, tiled=True)  9.68 us
    all_to_all x1, starting transfers between devices, local_heads(): lax.all_to_all(v_blocks, 'frame', split_axis=0, concat_axis=0, tiled=True)  7.27 us
    all_to_all x1, starting transfers between devices, local_heads(): lax.all_to_all(jnp.broadcast_to(mine, (parts, 2 * pos, HD)), 'frame', spl...  4.19 us
  transfers between devices with their start and end apart: 19, of which 9 were waited for; matrix products, arithmetic and copies ran while one was open for 1% of the time, Pallas kernels for 11%

profile of v6, /device:TPU:0, one launch (start us, length us, event | category | flops | bytes accessed | tf_op | source)
XLA Modules:
  0.0 77.5 jit_solution(12783316135901169714)
XLA Ops:
  0.0 2.1 %shard_map.82 = bf16[8,384,128]{2,1,0:T(8,128)(2,1)} custom-call(bf16[256,1280]{1,0:T(8,128)(2,1)} %refs_1_, bf16[256,1280]{1,0:T(8,128)(2,1)} %refs_2_), custom_call_target="tpu_custom_call" | custom-call | tf_op jit(solution)/shard_map/pallas_call | solution.py:500
  2.1 7.3 %all-to-all-start = ((bf16[8,384,128]{2,1,0:T(8,128)(2,1)}), bf16[8,384,128]{2,1,0:T(8,128)(2,1)S(1)}, u32[]{:S(2)}, u32[]{:S(2)}) async-start(bf16[8,384,128]{2,1,0:T(8,128)(2,1)} %shard_map.82), calls=%async_computation | async-start | bytes 1572864 | tf_op jit(solution)/shard_map/all_to_all | solution.py:563
  9.4 2.2 %shard_map.83.refs_3_ = f32[8,256]{1,0:T(8,128)} custom-call(bf16[256,1280]{1,0:T(8,128)(2,1)} %refs_0_, bf16[256,1280]{1,0:T(8,128)(2,1)} %refs_1_), custom_call_target="tpu_custom_call" | custom-call | tf_op jit(solution)/shard_map/pallas_call | solution.py:500
  13.5 1.4 %collective-permute-done.2.refs_6_ = f32[8,256]{1,0:T(8,128)S(1)} collective-permute-done((f32[8,256]{1,0:T(8,128)}, f32[8,256]{1,0:T(8,128)S(1)}, u32[]{:S(2)}, u32[]{:S(2)}) %collective-permute-start.2) | collective-permute-done | bytes 8224 | tf_op jit(solution)/shard_map/ppermute | solution.py:510
  14.9 1.3 %collective-permute-done.1.refs_5_ = f32[8,256]{1,0:T(8,128)S(1)} collective-permute-done((f32[8,256]{1,0:T(8,128)}, f32[8,256]{1,0:T(8,128)S(1)}, u32[]{:S(2)}, u32[]{:S(2)}) %collective-permute-start.1) | collective-permute-done | bytes 8224 | tf_op jit(solution)/shard_map/ppermute | solution.py:510
  16.9 4.2 %shard_map.84 = (bf16[592,128]{1,0:T(8,128)(2,1)}, bf16[592,128]{1,0:T(8,128)(2,1)}, bf16[592,128]{1,0:T(8,128)(2,1)}, bf16[592,128]{1,0:T(8,128)(2,1)}, bf16[59...) custom-call(bf16[256,1280]{1,0:T(8,128)(2,1)} %refs_0_, ...), custom_call_target="tpu_custom_call" | custom-call | tf_op jit(solution)/shard_map/pallas_call | solution.py:500
  21.1 1.7 %collective-permute-start.4 = (bf16[592,128]{1,0:T(8,128)(2,1)}, bf16[592,128]{1,0:T(8,128)(2,1)S(1)}, u32[]{:S(2)}, u32[]{:S(2)}) collective-permute-start(bf16[592,128]{1,0:T(8,128)(2,1)} %get-tuple-element.48), channel_id=1, source_target_pairs={{0,8},{4,12},{8,0},{12,4},{16,24},{20,28},{24,16},{28,20},{1,9},{5... | collective-permute-start | bytes 454664 | tf_op jit(solution)/shard_map/ppermute | solution.py:510
  22.8 1.4 %collective-permute-start.3 = (bf16[592,128]{1,0:T(8,128)(2,1)}, bf16[592,128]{1,0:T(8,128)(2,1)S(1)}, u32[]{:S(2)}, u32[]{:S(2)}) collective-permute-start(bf16[592,128]{1,0:T(8,128)(2,1)} %get-tuple-element.47), channel_id=1, source_target_pairs={{0,4},{4,0},{8,12},{12,8},{16,20},{20,16},{24,28},{28,24},{1,5},{5... | collective-permute-start | bytes 454664 | tf_op jit(solution)/shard_map/ppermute | solution.py:510
  24.9 2.5 %collective-permute-start.6 = (bf16[592,128]{1,0:T(8,128)(2,1)}, bf16[592,128]{1,0:T(8,128)(2,1)S(1)}, u32[]{:S(2)}, u32[]{:S(2)}) collective-permute-start(bf16[592,128]{1,0:T(8,128)(2,1)} %get-tuple-element.51), channel_id=1, source_target_pairs={{0,16},{4,20},{8,24},{12,28},{16,0},{20,4},{24,8},{28,12},{1,17},{... | collective-permute-start | bytes 454664 | tf_op jit(solution)/shard_map/ppermute | solution.py:510
  27.9 2.4 %collective-permute-start.8 = (bf16[592,128]{1,0:T(8,128)(2,1)}, bf16[592,128]{1,0:T(8,128)(2,1)S(1)}, u32[]{:S(2)}, u32[]{:S(2)}) collective-permute-start(bf16[592,128]{1,0:T(8,128)(2,1)} %get-tuple-element.53), channel_id=1, source_target_pairs={{0,24},{4,28},{8,16},{12,20},{16,8},{20,12},{24,0},{28,4},{1,25},{... | collective-permute-start | bytes 454664 | tf_op jit(solution)/shard_map/ppermute | solution.py:510
  30.6 3.5 %collective-permute-start.9 = (bf16[592,128]{1,0:T(8,128)(2,1)}, bf16[592,128]{1,0:T(8,128)(2,1)S(1)}, u32[]{:S(2)}, u32[]{:S(2)}) collective-permute-start(bf16[592,128]{1,0:T(8,128)(2,1)} %get-tuple-element.54), channel_id=1, source_target_pairs={{0,28},{4,24},{8,20},{12,16},{16,12},{20,8},{24,4},{28,0},{1,29},{... | collective-permute-start | bytes 454664 | tf_op jit(solution)/shard_map/ppermute | solution.py:510
  34.1 9.7 %all-to-all-done.v_ref = bf16[8,384,128]{2,1,0:T(8,128)(2,1)S(1)} async-done(((bf16[8,384,128]{2,1,0:T(8,128)(2,1)}), bf16[8,384,128]{2,1,0:T(8,128)(2,1)S(1)}, u32[]{:S(2)}, u32[]{:S(2)}) %all-to-all-start) | async-done | bytes 786464 | tf_op jit(solution)/shard_map/all_to_all | solution.py:563
  44.5 4.2 %all-to-all-start.1 = ((bf16[4,128,128]{2,1,0:T(8,128)(2,1)}), bf16[4,128,128]{2,1,0:T(8,128)(2,1)S(1)}, u32[]{:S(2)}, u32[]{:S(2)}) async-start(bf16[4,128,128]{2,1,0:T(8,128)(2,1)} %broadcast_in_dim.8), calls=%async_computation.1 | async-start | bytes 262144 | tf_op jit(solution)/shard_map/all_to_all | solution.py:598
  49.0 2.0 %collective-permute-done.7.refs_5_ = bf16[592,128]{1,0:T(8,128)(2,1)S(1)} collective-permute-done((bf16[592,128]{1,0:T(8,128)(2,1)}, bf16[592,128]{1,0:T(8,128)(2,1)S(1)}, u32[]{:S(2)}, u32[]{:S(2)}) %collective-permute-start.7) | collective-permute-done | bytes 151584 | tf_op jit(solution)/shard_map/ppermute | solution.py:510
  51.0 2.3 %collective-permute-done.5.refs_3_ = bf16[592,128]{1,0:T(8,128)(2,1)S(1)} collective-permute-done((bf16[592,128]{1,0:T(8,128)(2,1)}, bf16[592,128]{1,0:T(8,128)(2,1)S(1)}, u32[]{:S(2)}, u32[]{:S(2)}) %collective-permute-start.5) | collective-permute-done | bytes 151584 | tf_op jit(solution)/shard_map/ppermute | solution.py:510
  53.3 1.9 %shard_map.87 = (bf16[256,128]{1,0:T(8,128)(2,1)S(1)}, bf16[256,128]{1,0:T(8,128)(2,1)S(1)}, bf16[256,128]{1,0:T(8,128)(2,1)S(1)}, bf16[256,128]{1,0:T(8,128)(2,...) custom-call(s32[1]{0:T(128)} %copy.9.at_ref, ...), custom_call_target="tpu_custom_call" | custom-call | flops 805306368 | bytes 2097152 | tf_op jit(solution)/shard_map/pallas_call | solution.py:500
  55.2 1.0 %shard_map.88 = (bf16[336,128]{1,0:T(8,128)(2,1)S(1)}, bf16[336,128]{1,0:T(8,128)(2,1)S(1)}, bf16[336,128]{1,0:T(8,128)(2,1)S(1)}, bf16[336,128]{1,0:T(8,128)(2,...) custom-call(s32[1]{0:T(128)} %copy.9.at_ref, ...), custom_call_target="tpu_custom_call" | custom-call | tf_op jit(solution)/shard_map/pallas_call | solution.py:500
  56.2 3.8 %collective-permute-start.11 = (bf16[336,128]{1,0:T(8,128)(2,1)S(1)}, bf16[336,128]{1,0:T(8,128)(2,1)S(1)}, u32[]{:S(2)}, u32[]{:S(2)}) collective-permute-start(bf16[336,128]{1,0:T(8,128)(2,1)S(1)} %get-tuple-element.66), channel_id=1, source_target_pairs={{0,8},{4,12},{8,0},{12,4},{16,24},{20,28},{24,16},{28,20},{1,9},{5... | collective-permute-start | bytes 258056 | tf_op jit(solution)/shard_map/ppermute | solution.py:510
  60.7 3.7 %collective-permute-start.14 = (bf16[336,128]{1,0:T(8,128)(2,1)S(1)}, bf16[336,128]{1,0:T(8,128)(2,1)S(1)}, u32[]{:S(2)}, u32[]{:S(2)}) collective-permute-start(bf16[336,128]{1,0:T(8,128)(2,1)S(1)} %get-tuple-element.70), channel_id=1, source_target_pairs={{0,20},{4,16},{8,28},{12,24},{16,4},{20,0},{24,12},{28,8},{1,21},{... | collective-permute-start | bytes 258056 | tf_op jit(solution)/shard_map/ppermute | solution.py:510
  64.5 1.4 %collective-permute-start.15 = (bf16[336,128]{1,0:T(8,128)(2,1)S(1)}, bf16[336,128]{1,0:T(8,128)(2,1)S(1)}, u32[]{:S(2)}, u32[]{:S(2)}) collective-permute-start(bf16[336,128]{1,0:T(8,128)(2,1)S(1)} %get-tuple-element.71), channel_id=1, source_target_pairs={{0,24},{4,28},{8,16},{12,20},{16,8},{20,12},{24,0},{28,4},{1,25},{... | collective-permute-start | bytes 258056 | tf_op jit(solution)/shard_map/ppermute | solution.py:510
  65.9 2.5 %collective-permute-start.16 = (bf16[336,128]{1,0:T(8,128)(2,1)S(1)}, bf16[336,128]{1,0:T(8,128)(2,1)S(1)}, u32[]{:S(2)}, u32[]{:S(2)}) collective-permute-start(bf16[336,128]{1,0:T(8,128)(2,1)S(1)} %get-tuple-element.72), channel_id=1, source_target_pairs={{0,28},{4,24},{8,20},{12,16},{16,12},{20,8},{24,4},{28,0},{1,29},{... | collective-permute-start | bytes 258056 | tf_op jit(solution)/shard_map/ppermute | solution.py:510
  68.4 4.8 %collective-permute-done.13.refs_4_ = bf16[336,128]{1,0:T(8,128)(2,1)S(1)} collective-permute-done((bf16[336,128]{1,0:T(8,128)(2,1)S(1)}, bf16[336,128]{1,0:T(8,128)(2,1)S(1)}, u32[]{:S(2)}, u32[]{:S(2)}) %collective-permute-start.13) | collective-permute-done | bytes 86048 | tf_op jit(solution)/shard_map/ppermute | solution.py:510
  73.2 2.5 %collective-permute-done.14.refs_5_ = bf16[336,128]{1,0:T(8,128)(2,1)S(1)} collective-permute-done((bf16[336,128]{1,0:T(8,128)(2,1)S(1)}, bf16[336,128]{1,0:T(8,128)(2,1)S(1)}, u32[]{:S(2)}, u32[]{:S(2)}) %collective-permute-start.14) | collective-permute-done | bytes 86048 | tf_op jit(solution)/shard_map/ppermute | solution.py:510
  76.2 1.2 %shard_map.89 = bf16[256,1280]{1,0:T(8,128)(2,1)} custom-call(f32[256,1280]{1,0:T(8,128)S(1)} %copy-done, bf16[336,128]{1,0:T(8,128)(2,1)S(1)} %get-tuple-element.64.refs_0_, bf16[336,128]{1,0:T(8,128)(2,1)S(1)} %collective-permute-done.10.refs_1_, bf16[336,128]{1,0:T(8,128)(2,1)S(1)} %collective-permute-done.11.refs_2_, ...), custom_call_target="tpu_custom_call" | custom-call | tf_op jit(solution)/shard_map/pallas_call | solution.py:500
  (36 shorter events, 5.5 us)
Async XLA Ops:
  2.1 41.7 %all-to-all-start = ((bf16[8,384,128]{2,1,0:T(8,128)(2,1)}), bf16[8,384,128]{2,1,0:T(8,128)(2,1)S(1)}, u32[]{:S(2)}, u32[]{:S(2)}) async-start(bf16[8,384,128]{2,1,0:T(8,128)(2,1)} %shard_map.82), calls=%async_computation | async-start | bytes 1572864 | tf_op jit(solution)/shard_map/all_to_all | solution.py:563
  11.6 3.4 %collective-permute-start.2 = (f32[8,256]{1,0:T(8,128)}, f32[8,256]{1,0:T(8,128)S(1)}, u32[]{:S(2)}, u32[]{:S(2)}) collective-permute-start(f32[8,256]{1,0:T(8,128)} %shard_map.83.refs_3_), channel_id=1, source_target_pairs={{0,3},{1,2},{2,1},{3,0},{4,7},{5,6},{6,5},{7,4},{8,11},{9,10},{10,... | collective-permute-start | bytes 24584 | tf_op jit(solution)/shard_map/ppermute | solution.py:510
  12.3 3.9 %collective-permute-start.1 = (f32[8,256]{1,0:T(8,128)}, f32[8,256]{1,0:T(8,128)S(1)}, u32[]{:S(2)}, u32[]{:S(2)}) collective-permute-start(f32[8,256]{1,0:T(8,128)} %shard_map.83.refs_3_), channel_id=1, source_target_pairs={{0,2},{1,3},{2,0},{3,1},{4,6},{5,7},{6,4},{7,5},{8,10},{9,11},{10,... | collective-permute-start | bytes 24584 | tf_op jit(solution)/shard_map/ppermute | solution.py:510
  13.2 3.0 %collective-permute-start = (f32[8,256]{1,0:T(8,128)}, f32[8,256]{1,0:T(8,128)S(1)}, u32[]{:S(2)}, u32[]{:S(2)}) collective-permute-start(f32[8,256]{1,0:T(8,128)} %shard_map.83.refs_3_), channel_id=1, source_target_pairs={{0,1},{1,0},{2,3},{3,2},{4,5},{5,4},{6,7},{7,6},{8,9},{9,8},{10,11... | collective-permute-start | bytes 24584 | tf_op jit(solution)/shard_map/ppermute | solution.py:510
  14.9 1.3 %copy-start.3 = (f32[8,256]{1,0:T(8,128)}, f32[8,256]{1,0:T(8,128)S(1)}, u32[]{:S(2)}) copy-start(f32[8,256]{1,0:T(8,128)S(1)} %collective-permute-done.2.refs_6_) | copy-start | bytes 24580
  16.2 0.6 copy-start.5
  21.1 27.9 %copy-start.1 = (bf16[592,128]{1,0:T(8,128)(2,1)S(1)}, bf16[592,128]{1,0:T(8,128)(2,1)}, u32[]{:S(2)}) copy-start(bf16[592,128]{1,0:T(8,128)(2,1)} %get-tuple-element.46.in_ref) | copy-start | bytes 454660
  21.1 9.5 %collective-permute-start.4 = (bf16[592,128]{1,0:T(8,128)(2,1)}, bf16[592,128]{1,0:T(8,128)(2,1)S(1)}, u32[]{:S(2)}, u32[]{:S(2)}) collective-permute-start(bf16[592,128]{1,0:T(8,128)(2,1)} %get-tuple-element.48), channel_id=1, source_target_pairs={{0,8},{4,12},{8,0},{12,4},{16,24},{20,28},{24,16},{28,20},{1,9},{5... | collective-permute-start | bytes 454664 | tf_op jit(solution)/shard_map/ppermute | solution.py:510
  22.8 21.0 %collective-permute-start.3 = (bf16[592,128]{1,0:T(8,128)(2,1)}, bf16[592,128]{1,0:T(8,128)(2,1)S(1)}, u32[]{:S(2)}, u32[]{:S(2)}) collective-permute-start(bf16[592,128]{1,0:T(8,128)(2,1)} %get-tuple-element.47), channel_id=1, source_target_pairs={{0,4},{4,0},{8,12},{12,8},{16,20},{20,16},{24,28},{28,24},{1,5},{5... | collective-permute-start | bytes 454664 | tf_op jit(solution)/shard_map/ppermute | solution.py:510
  24.9 24.1 %collective-permute-start.6 = (bf16[592,128]{1,0:T(8,128)(2,1)}, bf16[592,128]{1,0:T(8,128)(2,1)S(1)}, u32[]{:S(2)}, u32[]{:S(2)}) collective-permute-start(bf16[592,128]{1,0:T(8,128)(2,1)} %get-tuple-element.51), channel_id=1, source_target_pairs={{0,16},{4,20},{8,24},{12,28},{16,0},{20,4},{24,8},{28,12},{1,17},{... | collective-permute-start | bytes 454664 | tf_op jit(solution)/shard_map/ppermute | solution.py:510
  27.4 23.6 %collective-permute-start.7 = (bf16[592,128]{1,0:T(8,128)(2,1)}, bf16[592,128]{1,0:T(8,128)(2,1)S(1)}, u32[]{:S(2)}, u32[]{:S(2)}) collective-permute-start(bf16[592,128]{1,0:T(8,128)(2,1)} %get-tuple-element.52), channel_id=1, source_target_pairs={{0,20},{4,16},{8,28},{12,24},{16,4},{20,0},{24,12},{28,8},{1,21},{... | collective-permute-start | bytes 454664 | tf_op jit(solution)/shard_map/ppermute | solution.py:510
  27.9 23.1 %collective-permute-start.8 = (bf16[592,128]{1,0:T(8,128)(2,1)}, bf16[592,128]{1,0:T(8,128)(2,1)S(1)}, u32[]{:S(2)}, u32[]{:S(2)}) collective-permute-start(bf16[592,128]{1,0:T(8,128)(2,1)} %get-tuple-element.53), channel_id=1, source_target_pairs={{0,24},{4,28},{8,16},{12,20},{16,8},{20,12},{24,0},{28,4},{1,25},{... | collective-permute-start | bytes 454664 | tf_op jit(solution)/shard_map/ppermute | solution.py:510
  30.6 20.4 %collective-permute-start.9 = (bf16[592,128]{1,0:T(8,128)(2,1)}, bf16[592,128]{1,0:T(8,128)(2,1)S(1)}, u32[]{:S(2)}, u32[]{:S(2)}) collective-permute-start(bf16[592,128]{1,0:T(8,128)(2,1)} %get-tuple-element.54), channel_id=1, source_target_pairs={{0,28},{4,24},{8,20},{12,16},{16,12},{20,8},{24,4},{28,0},{1,29},{... | collective-permute-start | bytes 454664 | tf_op jit(solution)/shard_map/ppermute | solution.py:510
  43.8 9.5 %collective-permute-start.5 = (bf16[592,128]{1,0:T(8,128)(2,1)}, bf16[592,128]{1,0:T(8,128)(2,1)S(1)}, u32[]{:S(2)}, u32[]{:S(2)}) collective-permute-start(bf16[592,128]{1,0:T(8,128)(2,1)} %get-tuple-element.50), channel_id=1, source_target_pairs={{0,12},{4,8},{8,4},{12,0},{16,28},{20,24},{24,20},{28,16},{1,13},{... | collective-permute-start | bytes 454664 | tf_op jit(solution)/shard_map/ppermute | solution.py:510
  44.5 10.7 %all-to-all-start.1 = ((bf16[4,128,128]{2,1,0:T(8,128)(2,1)}), bf16[4,128,128]{2,1,0:T(8,128)(2,1)S(1)}, u32[]{:S(2)}, u32[]{:S(2)}) async-start(bf16[4,128,128]{2,1,0:T(8,128)(2,1)} %broadcast_in_dim.8), calls=%async_computation.1 | async-start | bytes 262144 | tf_op jit(solution)/shard_map/all_to_all | solution.py:598
  48.9 6.3 %copy-start.2 = (f32[1280]{0:T(1024)S(1)}, f32[1280]{0:T(1024)}, u32[]{:S(2)}) copy-start(f32[1280]{0:T(1024)} %param.12) | copy-start | bytes 15364
  55.2 21.0 %copy-start = (f32[256,1280]{1,0:T(8,128)S(1)}, f32[256,1280]{1,0:T(8,128)}, u32[]{:S(2)}) copy-start(f32[256,1280]{1,0:T(8,128)} %get-tuple-element.42.own_ref) | copy-start | bytes 3932164
  56.2 9.6 %collective-permute-start.11 = (bf16[336,128]{1,0:T(8,128)(2,1)S(1)}, bf16[336,128]{1,0:T(8,128)(2,1)S(1)}, u32[]{:S(2)}, u32[]{:S(2)}) collective-permute-start(bf16[336,128]{1,0:T(8,128)(2,1)S(1)} %get-tuple-element.66), channel_id=1, source_target_pairs={{0,8},{4,12},{8,0},{12,4},{16,24},{20,28},{24,16},{28,20},{1,9},{5... | collective-permute-start | bytes 258056 | tf_op jit(solution)/shard_map/ppermute | solution.py:510
  60.1 8.3 %collective-permute-start.10 = (bf16[336,128]{1,0:T(8,128)(2,1)S(1)}, bf16[336,128]{1,0:T(8,128)(2,1)S(1)}, u32[]{:S(2)}, u32[]{:S(2)}) collective-permute-start(bf16[336,128]{1,0:T(8,128)(2,1)S(1)} %get-tuple-element.65), channel_id=1, source_target_pairs={{0,4},{4,0},{8,12},{12,8},{16,20},{20,16},{24,28},{28,24},{1,5},{5... | collective-permute-start | bytes 258056 | tf_op jit(solution)/shard_map/ppermute | solution.py:510
  60.7 12.4 %collective-permute-start.13 = (bf16[336,128]{1,0:T(8,128)(2,1)S(1)}, bf16[336,128]{1,0:T(8,128)(2,1)S(1)}, u32[]{:S(2)}, u32[]{:S(2)}) collective-permute-start(bf16[336,128]{1,0:T(8,128)(2,1)S(1)} %get-tuple-element.69), channel_id=1, source_target_pairs={{0,16},{4,20},{8,24},{12,28},{16,0},{20,4},{24,8},{28,12},{1,17},{... | collective-permute-start | bytes 258056 | tf_op jit(solution)/shard_map/ppermute | solution.py:510
  60.7 15.0 %collective-permute-start.14 = (bf16[336,128]{1,0:T(8,128)(2,1)S(1)}, bf16[336,128]{1,0:T(8,128)(2,1)S(1)}, u32[]{:S(2)}, u32[]{:S(2)}) collective-permute-start(bf16[336,128]{1,0:T(8,128)(2,1)S(1)} %get-tuple-element.70), channel_id=1, source_target_pairs={{0,20},{4,16},{8,28},{12,24},{16,4},{20,0},{24,12},{28,8},{1,21},{... | collective-permute-start | bytes 258056 | tf_op jit(solution)/shard_map/ppermute | solution.py:510
  64.5 11.2 %collective-permute-start.15 = (bf16[336,128]{1,0:T(8,128)(2,1)S(1)}, bf16[336,128]{1,0:T(8,128)(2,1)S(1)}, u32[]{:S(2)}, u32[]{:S(2)}) collective-permute-start(bf16[336,128]{1,0:T(8,128)(2,1)S(1)} %get-tuple-element.71), channel_id=1, source_target_pairs={{0,24},{4,28},{8,16},{12,20},{16,8},{20,12},{24,0},{28,4},{1,25},{... | collective-permute-start | bytes 258056 | tf_op jit(solution)/shard_map/ppermute | solution.py:510
  65.9 9.8 %collective-permute-start.16 = (bf16[336,128]{1,0:T(8,128)(2,1)S(1)}, bf16[336,128]{1,0:T(8,128)(2,1)S(1)}, u32[]{:S(2)}, u32[]{:S(2)}) collective-permute-start(bf16[336,128]{1,0:T(8,128)(2,1)S(1)} %get-tuple-element.72), channel_id=1, source_target_pairs={{0,28},{4,24},{8,20},{12,16},{16,12},{20,8},{24,4},{28,0},{1,29},{... | collective-permute-start | bytes 258056 | tf_op jit(solution)/shard_map/ppermute | solution.py:510
  68.4 7.9 %collective-permute-start.12 = (bf16[336,128]{1,0:T(8,128)(2,1)S(1)}, bf16[336,128]{1,0:T(8,128)(2,1)S(1)}, u32[]{:S(2)}, u32[]{:S(2)}) collective-permute-start(bf16[336,128]{1,0:T(8,128)(2,1)S(1)} %get-tuple-element.68), channel_id=1, source_target_pairs={{0,12},{4,8},{8,4},{12,0},{16,28},{20,24},{24,20},{28,16},{1,13},{... | collective-permute-start | bytes 258056 | tf_op jit(solution)/shard_map/ppermute | solution.py:510
  (1 other events, 0.6 us)

commit v7 on v6

--- a/solution.py
+++ b/solution.py
@@ -279,6 +279,14 @@
         copy.wait()
 
 
+FAR_ORDER = (0, 1, 2, 3, 4, 5, 6, 7)
+BACK_ORDER = (0, 1, 2, 3, 4, 5, 6, 7)
+
+
+def by_step(refs, order):
+    return [refs[order.index(s)] for s in range(len(order))]
+
+
 def inverse(value):
     guess = pl.reciprocal(value, approx=True)
     return guess * (2.0 - value * guess)
@@ -372,7 +380,7 @@
 
 
 def whole_kernel(n, tok, pos, at_ref, vt_ref, *refs):
-    blocks, outs, side_ref = refs[:n], refs[n : 2 * n], refs[2 * n]
+    blocks, outs, side_ref = by_step(refs[:n], FAR_ORDER), refs[n : 2 * n], refs[2 * n]
     key_ref, flag_ref = refs[2 * n + 1 :]
     gp = tok // n
     per = n // 2
@@ -390,7 +398,7 @@
     lses = [[side_rows(half, at_side, 3 * b) for b in range(2)] for half in halves]
     kept = [[[jnp.zeros((1, HD), jnp.float32)] * per for _ in range(2)] for _ in range(2)]
     across = BLOCK // gp
-    together = 2
+    together = 4
     for g0 in range(0, n, together):
         tiles, places = [], []
         for g in range(g0, g0 + together):
@@ -410,7 +418,7 @@
 
 
 def part_kernel(n, tok, pos, at_ref, gain_ref, held_ref, vt_ref, v_ref, *refs):
-    blocks, done, came_ref = refs[:n], refs[n : 2 * n], refs[2 * n]
+    blocks, done, came_ref = by_step(refs[:n], FAR_ORDER), refs[n : 2 * n], refs[2 * n]
     outs, flag_ref, col_ref = refs[2 * n + 1 : 3 * n + 1], refs[3 * n + 1], refs[3 * n + 2]
     gp = tok // n
     per = n // 2
@@ -470,7 +478,8 @@
 
 
 def join_kernel(n, pos, own_ref, *refs):
-    back, out_ref = refs[:n], refs[n]
+    back, out_ref = by_step(refs[:n], BACK_ORDER), refs[n]
+    held, sems = refs[n + 1 :]
     tok = own_ref.shape[0]
     parts = tok // pos
     me = lax.axis_index("frame")
@@ -482,6 +491,7 @@
         pick = (sub == row).astype(jnp.bfloat16)
         return jnp.dot(sides, pick, preferred_element_type=jnp.float32)
 
+    copies = []
     for s in range(n):
         d = me ^ s
         keeps = [spread_lanes(s * ROWS + r) for r in range(3)]
@@ -489,11 +499,22 @@
         for b in range(tok // BLOCK):
             rows = slice(b * BLOCK, (b + 1) * BLOCK)
             got = back[s][rows, :].astype(jnp.float32)
-            out_ref[rows, whole] = (own_ref[rows, whole] * keeps[b] + got).astype(jnp.bfloat16)
+            held[s, rows, :] = (own_ref[rows, whole] * keeps[b] + got).astype(jnp.bfloat16)
+        copies.append(pltpu.make_async_copy(held.at[s], out_ref.at[:, whole], sems.at[0, s]))
+        copies[-1].start()
         part = pl.ds(pl.multiple_of((n + d // parts) * HD, HD), HD)
         rows = pl.ds(pl.multiple_of(d % parts * pos, pos), pos)
         got = back[s][tok : tok + pos, :].astype(jnp.float32)
-        out_ref[rows, part] = (own_ref[rows, part] * keeps[2][:pos] + got).astype(jnp.bfloat16)
+        got = own_ref[rows, part] * keeps[2][:pos] + got
+        held[n + s // parts, s % parts * pos : (s % parts + 1) * pos, :] = got.astype(jnp.bfloat16)
+        copies.append(
+            pltpu.make_async_copy(
+                held.at[n + s // parts, pl.ds(s % parts * pos, pos)], out_ref.at[rows, part], sems.at[1, s]
+            )
+        )
+        copies[-1].start()
+    for copy in copies:
+        copy.wait()
 
 
 def call(kernel, out_shape, *args, vmem=40, **more):
@@ -510,16 +531,14 @@
     return lax.ppermute(array, axis, [(i, i ^ step) for i in range(size)])
 
 
-def swap_blocks(blocks):
-    n = len(blocks)
+def swap_blocks(blocks, order, chain):
     got = {0: blocks[0]}
-    wide = sorted(range(n // 2, n), key=lambda s: (s % 2, s))
-    for s in wide + [1, 2]:
-        got[s] = pairwise(blocks[s], "frame", s)
-    for s in range(3, n // 2):
-        block, _ = lax.optimization_barrier((blocks[s], got[s - 1]))
+    for s in order:
+        block = blocks[s]
+        if s in chain:
+            block, _ = lax.optimization_barrier((block, got[chain[s]]))
         got[s] = pairwise(block, "frame", s)
-    return [got[s] for s in range(n)]
+    return [got[s] for s in range(len(blocks))]
 
 
 def local_heads(
@@ -588,8 +607,8 @@
         ],
         vmem=60,
     )
-    far = swap_blocks(sent)
-    block, v_far = lax.optimization_barrier((sent[0], v_far))
+    far = swap_blocks(sent, (4, 6, 5, 7, 1, 2, 3), {3: 2})
+    block, v_far, *_ = lax.optimization_barrier((sent[0], v_far, far[1], far[2]))
     far[0] = call(copy_kernel, shape((rows, HD), bf16), block, vmem=8)
 
     anchor = anchor_frame[0]
@@ -617,7 +636,7 @@
         [shape((tok, HD), bf16)] * n + [shape((2 * n, HD), f32)],
         anchor_frame,
         vt,
-        *far,
+        *[far[s] for s in FAR_ORDER],
         in_specs=[sm] + [vm] * (n + 1),
         scratch_shapes=[pltpu.VMEM((tok, HD), bf16), pltpu.VMEM((2, n, HD), f32)],
         cost_estimate=pl.CostEstimate(
@@ -632,15 +651,21 @@
         held,
         vt,
         v_far,
-        *far,
+        *[far[s] for s in FAR_ORDER],
         *done,
         side,
         in_specs=[sm] + [vm] * (2 * n + 5),
         scratch_shapes=[pltpu.VMEM((2, n, HD), f32), pltpu.VMEM((HD, HD), f32)],
     )
-    back = swap_blocks(result)
+    back = swap_blocks(result, (4, 6, 5, 7, 1, 2, 3), {2: 4, 3: 6})
     return call(
-        functools.partial(join_kernel, n, pos), shape((tok, width), bf16), own, *back
+        functools.partial(join_kernel, n, pos),
+        shape((tok, width), bf16),
+        own,
+        *[back[s] for s in BACK_ORDER],
+        in_specs=[vm] * (n + 1),
+        out_specs=hbm,
+        scratch_shapes=[pltpu.VMEM((n + 2, tok, HD), bf16), dma((2, n))],
     )
 
 

time: 77.9 us -> 77.3 us (level)
  starting transfers between devices: 37.6 us -> 36.8 us
    ppermute x17, waiting for transfers between devices: 15.3 us -> 16.2 us  [pairwise(): return lax.ppermute(array, axis, [(i, i ^ step) for i in range(size)])]
    all_to_all x1, starting transfers between devices: 4.19 us -> 3.32 us  [local_heads(): lax.all_to_all(jnp.broadcast_to(mine, (parts, 2 * pos, HD)), 'frame', spl...]
  transfers between devices with their start and end apart: 19 -> 19, of which waited for: 9 -> 10; matrix products, arithmetic and copies ran while one was open for 1% -> 1% of each run, Pallas kernels for 11% -> 11%
where the time goes in v7:
time: 77.3 us; the launch traced here: 76.8 us
  starting transfers between devices  36.8 us (48%)
  waiting for transfers between devices  25.4 us (33%)
  Pallas kernels  12.6 us (16%)
  local copies, waits for them, and re-layouts  1.29 us (2%)
  between operations  0.78 us (1%)
    ppermute x17, starting transfers between devices, pairwise(): return lax.ppermute(array, axis, [(i, i ^ step) for i in range(size)])  26.2 us
    ppermute x17, waiting for transfers between devices, pairwise(): return lax.ppermute(array, axis, [(i, i ^ step) for i in range(size)])  16.2 us
    pallas_call x8, Pallas kernels, call(): pl.pallas_call(kernel, out_shape=out_shape, compiler_params=pltpu.Compile...  12.6 us
    all_to_all x1, waiting for transfers between devices, local_heads(): lax.all_to_all(v_blocks, 'frame', split_axis=0, concat_axis=0, tiled=True)  9.23 us
    all_to_all x1, starting transfers between devices, local_heads(): lax.all_to_all(v_blocks, 'frame', split_axis=0, concat_axis=0, tiled=True)  7.27 us
    all_to_all x1, starting transfers between devices, local_heads(): lax.all_to_all(jnp.broadcast_to(mine, (parts, 2 * pos, HD)), 'frame', spl...  3.32 us
  transfers between devices with their start and end apart: 19, of which 10 were waited for; matrix products, arithmetic and copies ran while one was open for 1% of the time, Pallas kernels for 11%

profile of v7, /device:TPU:0, one launch (start us, length us, event | category | flops | bytes accessed | tf_op | source)
XLA Modules:
  0.0 76.8 jit_solution(12636146874398884345)
XLA Ops:
  0.0 2.1 %shard_map.82 = bf16[8,384,128]{2,1,0:T(8,128)(2,1)} custom-call(bf16[256,1280]{1,0:T(8,128)(2,1)} %refs_1_, bf16[256,1280]{1,0:T(8,128)(2,1)} %refs_2_), custom_call_target="tpu_custom_call" | custom-call | tf_op jit(solution)/shard_map/pallas_call | solution.py:521
  2.1 7.3 %all-to-all-start = ((bf16[8,384,128]{2,1,0:T(8,128)(2,1)}), bf16[8,384,128]{2,1,0:T(8,128)(2,1)S(1)}, u32[]{:S(2)}, u32[]{:S(2)}) async-start(bf16[8,384,128]{2,1,0:T(8,128)(2,1)} %shard_map.82), calls=%async_computation | async-start | bytes 1572864 | tf_op jit(solution)/shard_map/all_to_all | solution.py:582
  9.4 2.2 %shard_map.83.refs_3_ = f32[8,256]{1,0:T(8,128)} custom-call(bf16[256,1280]{1,0:T(8,128)(2,1)} %refs_0_, bf16[256,1280]{1,0:T(8,128)(2,1)} %refs_1_), custom_call_target="tpu_custom_call" | custom-call | tf_op jit(solution)/shard_map/pallas_call | solution.py:521
  13.5 1.4 %collective-permute-done.2.refs_6_ = f32[8,256]{1,0:T(8,128)S(1)} collective-permute-done((f32[8,256]{1,0:T(8,128)}, f32[8,256]{1,0:T(8,128)S(1)}, u32[]{:S(2)}, u32[]{:S(2)}) %collective-permute-start.2) | collective-permute-done | bytes 8224 | tf_op jit(solution)/shard_map/ppermute | solution.py:531
  14.9 1.3 %collective-permute-done.1.refs_5_ = f32[8,256]{1,0:T(8,128)S(1)} collective-permute-done((f32[8,256]{1,0:T(8,128)}, f32[8,256]{1,0:T(8,128)S(1)}, u32[]{:S(2)}, u32[]{:S(2)}) %collective-permute-start.1) | collective-permute-done | bytes 8224 | tf_op jit(solution)/shard_map/ppermute | solution.py:531
  16.9 4.2 %shard_map.84 = (bf16[592,128]{1,0:T(8,128)(2,1)}, bf16[592,128]{1,0:T(8,128)(2,1)}, bf16[592,128]{1,0:T(8,128)(2,1)}, bf16[592,128]{1,0:T(8,128)(2,1)}, bf16[59...) custom-call(bf16[256,1280]{1,0:T(8,128)(2,1)} %refs_0_, ...), custom_call_target="tpu_custom_call" | custom-call | tf_op jit(solution)/shard_map/pallas_call | solution.py:521
  21.1 1.7 %collective-permute-start.4 = (bf16[592,128]{1,0:T(8,128)(2,1)}, bf16[592,128]{1,0:T(8,128)(2,1)S(1)}, u32[]{:S(2)}, u32[]{:S(2)}) collective-permute-start(bf16[592,128]{1,0:T(8,128)(2,1)} %get-tuple-element.47), channel_id=1, source_target_pairs={{0,8},{4,12},{8,0},{12,4},{16,24},{20,28},{24,16},{28,20},{1,9},{5... | collective-permute-start | bytes 454664 | tf_op jit(solution)/shard_map/ppermute | solution.py:531
  22.8 1.4 %collective-permute-start.3 = (bf16[592,128]{1,0:T(8,128)(2,1)}, bf16[592,128]{1,0:T(8,128)(2,1)S(1)}, u32[]{:S(2)}, u32[]{:S(2)}) collective-permute-start(bf16[592,128]{1,0:T(8,128)(2,1)} %get-tuple-element.46), channel_id=1, source_target_pairs={{0,4},{4,0},{8,12},{12,8},{16,20},{20,16},{24,28},{28,24},{1,5},{5... | collective-permute-start | bytes 454664 | tf_op jit(solution)/shard_map/ppermute | solution.py:531
  24.9 2.5 %collective-permute-start.6 = (bf16[592,128]{1,0:T(8,128)(2,1)}, bf16[592,128]{1,0:T(8,128)(2,1)S(1)}, u32[]{:S(2)}, u32[]{:S(2)}) collective-permute-start(bf16[592,128]{1,0:T(8,128)(2,1)} %get-tuple-element.52), channel_id=1, source_target_pairs={{0,16},{4,20},{8,24},{12,28},{16,0},{20,4},{24,8},{28,12},{1,17},{... | collective-permute-start | bytes 454664 | tf_op jit(solution)/shard_map/ppermute | solution.py:531
  27.9 2.4 %collective-permute-start.8 = (bf16[592,128]{1,0:T(8,128)(2,1)}, bf16[592,128]{1,0:T(8,128)(2,1)S(1)}, u32[]{:S(2)}, u32[]{:S(2)}) collective-permute-start(bf16[592,128]{1,0:T(8,128)(2,1)} %get-tuple-element.54), channel_id=1, source_target_pairs={{0,24},{4,28},{8,16},{12,20},{16,8},{20,12},{24,0},{28,4},{1,25},{... | collective-permute-start | bytes 454664 | tf_op jit(solution)/shard_map/ppermute | solution.py:531
  30.6 3.5 %collective-permute-start.9 = (bf16[592,128]{1,0:T(8,128)(2,1)}, bf16[592,128]{1,0:T(8,128)(2,1)S(1)}, u32[]{:S(2)}, u32[]{:S(2)}) collective-permute-start(bf16[592,128]{1,0:T(8,128)(2,1)} %get-tuple-element.55), channel_id=1, source_target_pairs={{0,28},{4,24},{8,20},{12,16},{16,12},{20,8},{24,4},{28,0},{1,29},{... | collective-permute-start | bytes 454664 | tf_op jit(solution)/shard_map/ppermute | solution.py:531
  34.6 9.2 %all-to-all-done.v_ref = bf16[8,384,128]{2,1,0:T(8,128)(2,1)S(1)} async-done(((bf16[8,384,128]{2,1,0:T(8,128)(2,1)}), bf16[8,384,128]{2,1,0:T(8,128)(2,1)S(1)}, u32[]{:S(2)}, u32[]{:S(2)}) %all-to-all-start) | async-done | bytes 786464 | tf_op jit(solution)/shard_map/all_to_all | solution.py:582
  44.5 3.3 %all-to-all-start.1 = ((bf16[4,128,128]{2,1,0:T(8,128)(2,1)}), bf16[4,128,128]{2,1,0:T(8,128)(2,1)S(1)}, u32[]{:S(2)}, u32[]{:S(2)}) async-start(bf16[4,128,128]{2,1,0:T(8,128)(2,1)} %broadcast_in_dim.8), calls=%async_computation.1 | async-start | bytes 262144 | tf_op jit(solution)/shard_map/all_to_all | solution.py:617
  48.1 2.9 %collective-permute-done.7.refs_5_ = bf16[592,128]{1,0:T(8,128)(2,1)S(1)} collective-permute-done((bf16[592,128]{1,0:T(8,128)(2,1)}, bf16[592,128]{1,0:T(8,128)(2,1)S(1)}, u32[]{:S(2)}, u32[]{:S(2)}) %collective-permute-start.7) | collective-permute-done | bytes 151584 | tf_op jit(solution)/shard_map/ppermute | solution.py:531
  51.0 2.3 %collective-permute-done.5.refs_3_ = bf16[592,128]{1,0:T(8,128)(2,1)S(1)} collective-permute-done((bf16[592,128]{1,0:T(8,128)(2,1)}, bf16[592,128]{1,0:T(8,128)(2,1)S(1)}, u32[]{:S(2)}, u32[]{:S(2)}) %collective-permute-start.5) | collective-permute-done | bytes 151584 | tf_op jit(solution)/shard_map/ppermute | solution.py:531
  53.3 1.7 %shard_map.87 = (bf16[256,128]{1,0:T(8,128)(2,1)S(1)}, bf16[256,128]{1,0:T(8,128)(2,1)S(1)}, bf16[256,128]{1,0:T(8,128)(2,1)S(1)}, bf16[256,128]{1,0:T(8,128)(2,...) custom-call(s32[1]{0:T(128)} %copy.9.at_ref, ...), custom_call_target="tpu_custom_call" | custom-call | flops 805306368 | bytes 2097152 | tf_op jit(solution)/shard_map/pallas_call | solution.py:521
  56.0 3.8 %collective-permute-start.11 = (bf16[336,128]{1,0:T(8,128)(2,1)S(1)}, bf16[336,128]{1,0:T(8,128)(2,1)S(1)}, u32[]{:S(2)}, u32[]{:S(2)}) collective-permute-start(bf16[336,128]{1,0:T(8,128)(2,1)S(1)} %get-tuple-element.68), channel_id=1, source_target_pairs={{0,16},{4,20},{8,24},{12,28},{16,0},{20,4},{24,8},{28,12},{1,17},{... | collective-permute-start | bytes 258056 | tf_op jit(solution)/shard_map/ppermute | solution.py:531
  59.8 2.3 %collective-permute-start.13 = (bf16[336,128]{1,0:T(8,128)(2,1)S(1)}, bf16[336,128]{1,0:T(8,128)(2,1)S(1)}, u32[]{:S(2)}, u32[]{:S(2)}) collective-permute-start(bf16[336,128]{1,0:T(8,128)(2,1)S(1)} %get-tuple-element.71), channel_id=1, source_target_pairs={{0,24},{4,28},{8,16},{12,20},{16,8},{20,12},{24,0},{28,4},{1,25},{... | collective-permute-start | bytes 258056 | tf_op jit(solution)/shard_map/ppermute | solution.py:531
  62.8 2.3 %collective-permute-start.16 = (bf16[336,128]{1,0:T(8,128)(2,1)S(1)}, bf16[336,128]{1,0:T(8,128)(2,1)S(1)}, u32[]{:S(2)}, u32[]{:S(2)}) collective-permute-start(bf16[336,128]{1,0:T(8,128)(2,1)S(1)} %get-tuple-element.74), channel_id=1, source_target_pairs={{0,28},{4,24},{8,20},{12,16},{16,12},{20,8},{24,4},{28,0},{1,29},{... | collective-permute-start | bytes 258056 | tf_op jit(solution)/shard_map/ppermute | solution.py:531
  65.1 5.1 %collective-permute-done.11.refs_4_ = bf16[336,128]{1,0:T(8,128)(2,1)S(1)} collective-permute-done((bf16[336,128]{1,0:T(8,128)(2,1)S(1)}, bf16[336,128]{1,0:T(8,128)(2,1)S(1)}, u32[]{:S(2)}, u32[]{:S(2)}) %collective-permute-start.11) | collective-permute-done | bytes 86048 | tf_op jit(solution)/shard_map/ppermute | solution.py:531
  70.2 2.6 %collective-permute-start.14 = (bf16[336,128]{1,0:T(8,128)(2,1)S(1)}, bf16[336,128]{1,0:T(8,128)(2,1)S(1)}, u32[]{:S(2)}, u32[]{:S(2)}) collective-permute-start(bf16[336,128]{1,0:T(8,128)(2,1)S(1)} %get-tuple-element.72), channel_id=1, source_target_pairs={{0,12},{4,8},{8,4},{12,0},{16,28},{20,24},{24,20},{28,16},{1,13},{... | collective-permute-start | bytes 258056 | tf_op jit(solution)/shard_map/ppermute | solution.py:531
  72.9 1.2 %collective-permute-done.15.refs_5_ = bf16[336,128]{1,0:T(8,128)(2,1)S(1)} collective-permute-done((bf16[336,128]{1,0:T(8,128)(2,1)S(1)}, bf16[336,128]{1,0:T(8,128)(2,1)S(1)}, u32[]{:S(2)}, u32[]{:S(2)}) %collective-permute-start.15) | collective-permute-done | bytes 86048 | tf_op jit(solution)/shard_map/ppermute | solution.py:531
  74.1 1.4 %collective-permute-done.12.refs_2_ = bf16[336,128]{1,0:T(8,128)(2,1)S(1)} collective-permute-done((bf16[336,128]{1,0:T(8,128)(2,1)S(1)}, bf16[336,128]{1,0:T(8,128)(2,1)S(1)}, u32[]{:S(2)}, u32[]{:S(2)}) %collective-permute-start.12) | collective-permute-done | bytes 86048 | tf_op jit(solution)/shard_map/ppermute | solution.py:531
  75.6 1.2 %shard_map.89 = bf16[256,1280]{1,0:T(8,128)(2,1)} custom-call(f32[256,1280]{1,0:T(8,128)S(1)} %copy-done, bf16[336,128]{1,0:T(8,128)(2,1)S(1)} %get-tuple-element.65.refs_0_, bf16[336,128]{1,0:T(8,128)(2,1)S(1)} %collective-permute-done.10.refs_1_, bf16[336,128]{1,0:T(8,128)(2,1)S(1)} %collective-permute-done.12.refs_2_, ...), custom_call_target="tpu_custom_call" | custom-call | tf_op jit(solution)/shard_map/pallas_call | solution.py:521
  (36 shorter events, 6.7 us)
Async XLA Ops:
  2.1 41.7 %all-to-all-start = ((bf16[8,384,128]{2,1,0:T(8,128)(2,1)}), bf16[8,384,128]{2,1,0:T(8,128)(2,1)S(1)}, u32[]{:S(2)}, u32[]{:S(2)}) async-start(bf16[8,384,128]{2,1,0:T(8,128)(2,1)} %shard_map.82), calls=%async_computation | async-start | bytes 1572864 | tf_op jit(solution)/shard_map/all_to_all | solution.py:582
  11.6 3.4 %collective-permute-start.2 = (f32[8,256]{1,0:T(8,128)}, f32[8,256]{1,0:T(8,128)S(1)}, u32[]{:S(2)}, u32[]{:S(2)}) collective-permute-start(f32[8,256]{1,0:T(8,128)} %shard_map.83.refs_3_), channel_id=1, source_target_pairs={{0,3},{1,2},{2,1},{3,0},{4,7},{5,6},{6,5},{7,4},{8,11},{9,10},{10,... | collective-permute-start | bytes 24584 | tf_op jit(solution)/shard_map/ppermute | solution.py:531
  12.3 3.9 %collective-permute-start.1 = (f32[8,256]{1,0:T(8,128)}, f32[8,256]{1,0:T(8,128)S(1)}, u32[]{:S(2)}, u32[]{:S(2)}) collective-permute-start(f32[8,256]{1,0:T(8,128)} %shard_map.83.refs_3_), channel_id=1, source_target_pairs={{0,2},{1,3},{2,0},{3,1},{4,6},{5,7},{6,4},{7,5},{8,10},{9,11},{10,... | collective-permute-start | bytes 24584 | tf_op jit(solution)/shard_map/ppermute | solution.py:531
  13.2 3.0 %collective-permute-start = (f32[8,256]{1,0:T(8,128)}, f32[8,256]{1,0:T(8,128)S(1)}, u32[]{:S(2)}, u32[]{:S(2)}) collective-permute-start(f32[8,256]{1,0:T(8,128)} %shard_map.83.refs_3_), channel_id=1, source_target_pairs={{0,1},{1,0},{2,3},{3,2},{4,5},{5,4},{6,7},{7,6},{8,9},{9,8},{10,11... | collective-permute-start | bytes 24584 | tf_op jit(solution)/shard_map/ppermute | solution.py:531
  14.9 1.3 %copy-start.3 = (f32[8,256]{1,0:T(8,128)}, f32[8,256]{1,0:T(8,128)S(1)}, u32[]{:S(2)}) copy-start(f32[8,256]{1,0:T(8,128)S(1)} %collective-permute-done.2.refs_6_) | copy-start | bytes 24580
  16.2 0.6 copy-start.5
  21.1 27.0 %copy-start.1 = (bf16[592,128]{1,0:T(8,128)(2,1)S(1)}, bf16[592,128]{1,0:T(8,128)(2,1)}, u32[]{:S(2)}) copy-start(bf16[592,128]{1,0:T(8,128)(2,1)} %get-tuple-element.49.in_ref) | copy-start | bytes 454660
  21.1 9.5 %collective-permute-start.4 = (bf16[592,128]{1,0:T(8,128)(2,1)}, bf16[592,128]{1,0:T(8,128)(2,1)S(1)}, u32[]{:S(2)}, u32[]{:S(2)}) collective-permute-start(bf16[592,128]{1,0:T(8,128)(2,1)} %get-tuple-element.47), channel_id=1, source_target_pairs={{0,8},{4,12},{8,0},{12,4},{16,24},{20,28},{24,16},{28,20},{1,9},{5... | collective-permute-start | bytes 454664 | tf_op jit(solution)/shard_map/ppermute | solution.py:531
  22.8 11.3 %collective-permute-start.3 = (bf16[592,128]{1,0:T(8,128)(2,1)}, bf16[592,128]{1,0:T(8,128)(2,1)S(1)}, u32[]{:S(2)}, u32[]{:S(2)}) collective-permute-start(bf16[592,128]{1,0:T(8,128)(2,1)} %get-tuple-element.46), channel_id=1, source_target_pairs={{0,4},{4,0},{8,12},{12,8},{16,20},{20,16},{24,28},{28,24},{1,5},{5... | collective-permute-start | bytes 454664 | tf_op jit(solution)/shard_map/ppermute | solution.py:531
  24.9 23.2 %collective-permute-start.6 = (bf16[592,128]{1,0:T(8,128)(2,1)}, bf16[592,128]{1,0:T(8,128)(2,1)S(1)}, u32[]{:S(2)}, u32[]{:S(2)}) collective-permute-start(bf16[592,128]{1,0:T(8,128)(2,1)} %get-tuple-element.52), channel_id=1, source_target_pairs={{0,16},{4,20},{8,24},{12,28},{16,0},{20,4},{24,8},{28,12},{1,17},{... | collective-permute-start | bytes 454664 | tf_op jit(solution)/shard_map/ppermute | solution.py:531
  27.4 23.6 %collective-permute-start.7 = (bf16[592,128]{1,0:T(8,128)(2,1)}, bf16[592,128]{1,0:T(8,128)(2,1)S(1)}, u32[]{:S(2)}, u32[]{:S(2)}) collective-permute-start(bf16[592,128]{1,0:T(8,128)(2,1)} %get-tuple-element.53), channel_id=1, source_target_pairs={{0,20},{4,16},{8,28},{12,24},{16,4},{20,0},{24,12},{28,8},{1,21},{... | collective-permute-start | bytes 454664 | tf_op jit(solution)/shard_map/ppermute | solution.py:531
  27.9 23.1 %collective-permute-start.8 = (bf16[592,128]{1,0:T(8,128)(2,1)}, bf16[592,128]{1,0:T(8,128)(2,1)S(1)}, u32[]{:S(2)}, u32[]{:S(2)}) collective-permute-start(bf16[592,128]{1,0:T(8,128)(2,1)} %get-tuple-element.54), channel_id=1, source_target_pairs={{0,24},{4,28},{8,16},{12,20},{16,8},{20,12},{24,0},{28,4},{1,25},{... | collective-permute-start | bytes 454664 | tf_op jit(solution)/shard_map/ppermute | solution.py:531
  30.6 20.4 %collective-permute-start.9 = (bf16[592,128]{1,0:T(8,128)(2,1)}, bf16[592,128]{1,0:T(8,128)(2,1)S(1)}, u32[]{:S(2)}, u32[]{:S(2)}) collective-permute-start(bf16[592,128]{1,0:T(8,128)(2,1)} %get-tuple-element.55), channel_id=1, source_target_pairs={{0,28},{4,24},{8,20},{12,16},{16,12},{20,8},{24,4},{28,0},{1,29},{... | collective-permute-start | bytes 454664 | tf_op jit(solution)/shard_map/ppermute | solution.py:531
  34.1 19.2 %collective-permute-start.5 = (bf16[592,128]{1,0:T(8,128)(2,1)}, bf16[592,128]{1,0:T(8,128)(2,1)S(1)}, u32[]{:S(2)}, u32[]{:S(2)}) collective-permute-start(bf16[592,128]{1,0:T(8,128)(2,1)} %get-tuple-element.51), channel_id=1, source_target_pairs={{0,12},{4,8},{8,4},{12,0},{16,28},{20,24},{24,20},{28,16},{1,13},{... | collective-permute-start | bytes 454664 | tf_op jit(solution)/shard_map/ppermute | solution.py:531
  44.5 10.5 %all-to-all-start.1 = ((bf16[4,128,128]{2,1,0:T(8,128)(2,1)}), bf16[4,128,128]{2,1,0:T(8,128)(2,1)S(1)}, u32[]{:S(2)}, u32[]{:S(2)}) async-start(bf16[4,128,128]{2,1,0:T(8,128)(2,1)} %broadcast_in_dim.8), calls=%async_computation.1 | async-start | bytes 262144 | tf_op jit(solution)/shard_map/all_to_all | solution.py:617
  48.1 6.9 %copy-start.2 = (f32[1280]{0:T(1024)S(1)}, f32[1280]{0:T(1024)}, u32[]{:S(2)}) copy-start(f32[1280]{0:T(1024)} %param.12) | copy-start | bytes 15364
  55.0 20.6 %copy-start = (f32[256,1280]{1,0:T(8,128)S(1)}, f32[256,1280]{1,0:T(8,128)}, u32[]{:S(2)}) copy-start(f32[256,1280]{1,0:T(8,128)} %get-tuple-element.43.own_ref) | copy-start | bytes 3932164
  56.0 14.2 %collective-permute-start.11 = (bf16[336,128]{1,0:T(8,128)(2,1)S(1)}, bf16[336,128]{1,0:T(8,128)(2,1)S(1)}, u32[]{:S(2)}, u32[]{:S(2)}) collective-permute-start(bf16[336,128]{1,0:T(8,128)(2,1)S(1)} %get-tuple-element.68), channel_id=1, source_target_pairs={{0,16},{4,20},{8,24},{12,28},{16,0},{20,4},{24,8},{28,12},{1,17},{... | collective-permute-start | bytes 258056 | tf_op jit(solution)/shard_map/ppermute | solution.py:531
  59.8 10.4 %collective-permute-start.13 = (bf16[336,128]{1,0:T(8,128)(2,1)S(1)}, bf16[336,128]{1,0:T(8,128)(2,1)S(1)}, u32[]{:S(2)}, u32[]{:S(2)}) collective-permute-start(bf16[336,128]{1,0:T(8,128)(2,1)S(1)} %get-tuple-element.71), channel_id=1, source_target_pairs={{0,24},{4,28},{8,16},{12,20},{16,8},{20,12},{24,0},{28,4},{1,25},{... | collective-permute-start | bytes 258056 | tf_op jit(solution)/shard_map/ppermute | solution.py:531
  62.1 10.7 %collective-permute-start.10 = (bf16[336,128]{1,0:T(8,128)(2,1)S(1)}, bf16[336,128]{1,0:T(8,128)(2,1)S(1)}, u32[]{:S(2)}, u32[]{:S(2)}) collective-permute-start(bf16[336,128]{1,0:T(8,128)(2,1)S(1)} %get-tuple-element.66), channel_id=1, source_target_pairs={{0,4},{4,0},{8,12},{12,8},{16,20},{20,16},{24,28},{28,24},{1,5},{5... | collective-permute-start | bytes 258056 | tf_op jit(solution)/shard_map/ppermute | solution.py:531
  62.8 11.2 %collective-permute-start.15 = (bf16[336,128]{1,0:T(8,128)(2,1)S(1)}, bf16[336,128]{1,0:T(8,128)(2,1)S(1)}, u32[]{:S(2)}, u32[]{:S(2)}) collective-permute-start(bf16[336,128]{1,0:T(8,128)(2,1)S(1)} %get-tuple-element.73), channel_id=1, source_target_pairs={{0,20},{4,16},{8,28},{12,24},{16,4},{20,0},{24,12},{28,8},{1,21},{... | collective-permute-start | bytes 258056 | tf_op jit(solution)/shard_map/ppermute | solution.py:531
  62.8 11.2 %collective-permute-start.16 = (bf16[336,128]{1,0:T(8,128)(2,1)S(1)}, bf16[336,128]{1,0:T(8,128)(2,1)S(1)}, u32[]{:S(2)}, u32[]{:S(2)}) collective-permute-start(bf16[336,128]{1,0:T(8,128)(2,1)S(1)} %get-tuple-element.74), channel_id=1, source_target_pairs={{0,28},{4,24},{8,20},{12,16},{16,12},{20,8},{24,4},{28,0},{1,29},{... | collective-permute-start | bytes 258056 | tf_op jit(solution)/shard_map/ppermute | solution.py:531
  70.2 5.2 %collective-permute-start.12 = (bf16[336,128]{1,0:T(8,128)(2,1)S(1)}, bf16[336,128]{1,0:T(8,128)(2,1)S(1)}, u32[]{:S(2)}, u32[]{:S(2)}) collective-permute-start(bf16[336,128]{1,0:T(8,128)(2,1)S(1)} %get-tuple-element.69), channel_id=1, source_target_pairs={{0,8},{4,12},{8,0},{12,4},{16,24},{20,28},{24,16},{28,20},{1,9},{5... | collective-permute-start | bytes 258056 | tf_op jit(solution)/shard_map/ppermute | solution.py:531
  70.2 5.4 %collective-permute-start.14 = (bf16[336,128]{1,0:T(8,128)(2,1)S(1)}, bf16[336,128]{1,0:T(8,128)(2,1)S(1)}, u32[]{:S(2)}, u32[]{:S(2)}) collective-permute-start(bf16[336,128]{1,0:T(8,128)(2,1)S(1)} %get-tuple-element.72), channel_id=1, source_target_pairs={{0,12},{4,8},{8,4},{12,0},{16,28},{20,24},{24,20},{28,16},{1,13},{... | collective-permute-start | bytes 258056 | tf_op jit(solution)/shard_map/ppermute | solution.py:531
  (1 other events, 0.6 us)

commit v8 on v7

--- a/solution.py
+++ b/solution.py
@@ -657,7 +657,7 @@
         in_specs=[sm] + [vm] * (2 * n + 5),
         scratch_shapes=[pltpu.VMEM((2, n, HD), f32), pltpu.VMEM((HD, HD), f32)],
     )
-    back = swap_blocks(result, (4, 6, 5, 7, 1, 2, 3), {2: 4, 3: 6})
+    back = swap_blocks(result, (4, 6, 5, 7, 1, 2, 3), {3: 4})
     return call(
         functools.partial(join_kernel, n, pos),
         shape((tok, width), bf16),

time: 77.3 us -> 75.8 us (0.981)
  waiting for transfers between devices: 25.4 us -> 23.5 us
    ppermute x17, waiting for transfers between devices: 16.2 us -> 14.3 us  [pairwise(): return lax.ppermute(array, axis, [(i, i ^ step) for i in range(size)])]
  transfers between devices with their start and end apart: 19 -> 19, of which waited for: 10 -> 9; matrix products, arithmetic and copies ran while one was open for 1% -> 1% of each run, Pallas kernels for 11% -> 11%
where the time goes in v8:
time: 75.8 us; the launch traced here: 75.4 us
  starting transfers between devices  37.2 us (49%)
  waiting for transfers between devices  23.5 us (31%)
  Pallas kernels  12.6 us (17%)
  local copies, waits for them, and re-layouts  1.29 us (2%)
  between operations  0.78 us (1%)
    ppermute x17, starting transfers between devices, pairwise(): return lax.ppermute(array, axis, [(i, i ^ step) for i in range(size)])  26.6 us
    ppermute x17, waiting for transfers between devices, pairwise(): return lax.ppermute(array, axis, [(i, i ^ step) for i in range(size)])  14.3 us
    pallas_call x8, Pallas kernels, call(): pl.pallas_call(kernel, out_shape=out_shape, compiler_params=pltpu.Compile...  12.6 us
    all_to_all x1, waiting for transfers between devices, local_heads(): lax.all_to_all(v_blocks, 'frame', split_axis=0, concat_axis=0, tiled=True)  9.23 us
    all_to_all x1, starting transfers between devices, local_heads(): lax.all_to_all(v_blocks, 'frame', split_axis=0, concat_axis=0, tiled=True)  7.27 us
    all_to_all x1, starting transfers between devices, local_heads(): lax.all_to_all(jnp.broadcast_to(mine, (parts, 2 * pos, HD)), 'frame', spl...  3.32 us
  transfers between devices with their start and end apart: 19, of which 9 were waited for; matrix products, arithmetic and copies ran while one was open for 1% of the time, Pallas kernels for 11%

profile of v8, /device:TPU:0, one launch (start us, length us, event | category | flops | bytes accessed | tf_op | source)
XLA Modules:
  0.0 75.4 jit_solution(7347148302305375553)
XLA Ops:
  0.0 2.1 %shard_map.82 = bf16[8,384,128]{2,1,0:T(8,128)(2,1)} custom-call(bf16[256,1280]{1,0:T(8,128)(2,1)} %refs_1_, bf16[256,1280]{1,0:T(8,128)(2,1)} %refs_2_), custom_call_target="tpu_custom_call" | custom-call | tf_op jit(solution)/shard_map/pallas_call | solution.py:521
  2.1 7.3 %all-to-all-start = ((bf16[8,384,128]{2,1,0:T(8,128)(2,1)}), bf16[8,384,128]{2,1,0:T(8,128)(2,1)S(1)}, u32[]{:S(2)}, u32[]{:S(2)}) async-start(bf16[8,384,128]{2,1,0:T(8,128)(2,1)} %shard_map.82), calls=%async_computation | async-start | bytes 1572864 | tf_op jit(solution)/shard_map/all_to_all | solution.py:582
  9.4 2.2 %shard_map.83.refs_3_ = f32[8,256]{1,0:T(8,128)} custom-call(bf16[256,1280]{1,0:T(8,128)(2,1)} %refs_0_, bf16[256,1280]{1,0:T(8,128)(2,1)} %refs_1_), custom_call_target="tpu_custom_call" | custom-call | tf_op jit(solution)/shard_map/pallas_call | solution.py:521
  13.5 1.4 %collective-permute-done.2.refs_6_ = f32[8,256]{1,0:T(8,128)S(1)} collective-permute-done((f32[8,256]{1,0:T(8,128)}, f32[8,256]{1,0:T(8,128)S(1)}, u32[]{:S(2)}, u32[]{:S(2)}) %collective-permute-start.2) | collective-permute-done | bytes 8224 | tf_op jit(solution)/shard_map/ppermute | solution.py:531
  14.9 1.3 %collective-permute-done.1.refs_5_ = f32[8,256]{1,0:T(8,128)S(1)} collective-permute-done((f32[8,256]{1,0:T(8,128)}, f32[8,256]{1,0:T(8,128)S(1)}, u32[]{:S(2)}, u32[]{:S(2)}) %collective-permute-start.1) | collective-permute-done | bytes 8224 | tf_op jit(solution)/shard_map/ppermute | solution.py:531
  16.9 4.2 %shard_map.84 = (bf16[592,128]{1,0:T(8,128)(2,1)}, bf16[592,128]{1,0:T(8,128)(2,1)}, bf16[592,128]{1,0:T(8,128)(2,1)}, bf16[592,128]{1,0:T(8,128)(2,1)}, bf16[59...) custom-call(bf16[256,1280]{1,0:T(8,128)(2,1)} %refs_0_, ...), custom_call_target="tpu_custom_call" | custom-call | tf_op jit(solution)/shard_map/pallas_call | solution.py:521
  21.1 1.7 %collective-permute-start.4 = (bf16[592,128]{1,0:T(8,128)(2,1)}, bf16[592,128]{1,0:T(8,128)(2,1)S(1)}, u32[]{:S(2)}, u32[]{:S(2)}) collective-permute-start(bf16[592,128]{1,0:T(8,128)(2,1)} %get-tuple-element.46), channel_id=1, source_target_pairs={{0,8},{4,12},{8,0},{12,4},{16,24},{20,28},{24,16},{28,20},{1,9},{5... | collective-permute-start | bytes 454664 | tf_op jit(solution)/shard_map/ppermute | solution.py:531
  22.8 1.4 %collective-permute-start.3 = (bf16[592,128]{1,0:T(8,128)(2,1)}, bf16[592,128]{1,0:T(8,128)(2,1)S(1)}, u32[]{:S(2)}, u32[]{:S(2)}) collective-permute-start(bf16[592,128]{1,0:T(8,128)(2,1)} %get-tuple-element.45), channel_id=1, source_target_pairs={{0,4},{4,0},{8,12},{12,8},{16,20},{20,16},{24,28},{28,24},{1,5},{5... | collective-permute-start | bytes 454664 | tf_op jit(solution)/shard_map/ppermute | solution.py:531
  24.9 2.5 %collective-permute-start.6 = (bf16[592,128]{1,0:T(8,128)(2,1)}, bf16[592,128]{1,0:T(8,128)(2,1)S(1)}, u32[]{:S(2)}, u32[]{:S(2)}) collective-permute-start(bf16[592,128]{1,0:T(8,128)(2,1)} %get-tuple-element.51), channel_id=1, source_target_pairs={{0,16},{4,20},{8,24},{12,28},{16,0},{20,4},{24,8},{28,12},{1,17},{... | collective-permute-start | bytes 454664 | tf_op jit(solution)/shard_map/ppermute | solution.py:531
  27.9 2.4 %collective-permute-start.8 = (bf16[592,128]{1,0:T(8,128)(2,1)}, bf16[592,128]{1,0:T(8,128)(2,1)S(1)}, u32[]{:S(2)}, u32[]{:S(2)}) collective-permute-start(bf16[592,128]{1,0:T(8,128)(2,1)} %get-tuple-element.53), channel_id=1, source_target_pairs={{0,24},{4,28},{8,16},{12,20},{16,8},{20,12},{24,0},{28,4},{1,25},{... | collective-permute-start | bytes 454664 | tf_op jit(solution)/shard_map/ppermute | solution.py:531
  30.6 3.5 %collective-permute-start.9 = (bf16[592,128]{1,0:T(8,128)(2,1)}, bf16[592,128]{1,0:T(8,128)(2,1)S(1)}, u32[]{:S(2)}, u32[]{:S(2)}) collective-permute-start(bf16[592,128]{1,0:T(8,128)(2,1)} %get-tuple-element.54), channel_id=1, source_target_pairs={{0,28},{4,24},{8,20},{12,16},{16,12},{20,8},{24,4},{28,0},{1,29},{... | collective-permute-start | bytes 454664 | tf_op jit(solution)/shard_map/ppermute | solution.py:531
  34.6 9.2 %all-to-all-done.v_ref = bf16[8,384,128]{2,1,0:T(8,128)(2,1)S(1)} async-done(((bf16[8,384,128]{2,1,0:T(8,128)(2,1)}), bf16[8,384,128]{2,1,0:T(8,128)(2,1)S(1)}, u32[]{:S(2)}, u32[]{:S(2)}) %all-to-all-start) | async-done | bytes 786464 | tf_op jit(solution)/shard_map/all_to_all | solution.py:582
  44.5 3.3 %all-to-all-start.1 = ((bf16[4,128,128]{2,1,0:T(8,128)(2,1)}), bf16[4,128,128]{2,1,0:T(8,128)(2,1)S(1)}, u32[]{:S(2)}, u32[]{:S(2)}) async-start(bf16[4,128,128]{2,1,0:T(8,128)(2,1)} %broadcast_in_dim.8), calls=%async_computation.1 | async-start | bytes 262144 | tf_op jit(solution)/shard_map/all_to_all | solution.py:617
  48.1 2.9 %collective-permute-done.7.refs_5_ = bf16[592,128]{1,0:T(8,128)(2,1)S(1)} collective-permute-done((bf16[592,128]{1,0:T(8,128)(2,1)}, bf16[592,128]{1,0:T(8,128)(2,1)S(1)}, u32[]{:S(2)}, u32[]{:S(2)}) %collective-permute-start.7) | collective-permute-done | bytes 151584 | tf_op jit(solution)/shard_map/ppermute | solution.py:531
  51.0 2.3 %collective-permute-done.5.refs_3_ = bf16[592,128]{1,0:T(8,128)(2,1)S(1)} collective-permute-done((bf16[592,128]{1,0:T(8,128)(2,1)}, bf16[592,128]{1,0:T(8,128)(2,1)S(1)}, u32[]{:S(2)}, u32[]{:S(2)}) %collective-permute-start.5) | collective-permute-done | bytes 151584 | tf_op jit(solution)/shard_map/ppermute | solution.py:531
  53.3 1.7 %shard_map.87 = (bf16[256,128]{1,0:T(8,128)(2,1)S(1)}, bf16[256,128]{1,0:T(8,128)(2,1)S(1)}, bf16[256,128]{1,0:T(8,128)(2,1)S(1)}, bf16[256,128]{1,0:T(8,128)(2,...) custom-call(s32[1]{0:T(128)} %copy.9.at_ref, ...), custom_call_target="tpu_custom_call" | custom-call | flops 805306368 | bytes 2097152 | tf_op jit(solution)/shard_map/pallas_call | solution.py:521
  55.0 1.0 %shard_map.88 = (bf16[336,128]{1,0:T(8,128)(2,1)S(1)}, bf16[336,128]{1,0:T(8,128)(2,1)S(1)}, bf16[336,128]{1,0:T(8,128)(2,1)S(1)}, bf16[336,128]{1,0:T(8,128)(2,...) custom-call(s32[1]{0:T(128)} %copy.9.at_ref, ...), custom_call_target="tpu_custom_call" | custom-call | tf_op jit(solution)/shard_map/pallas_call | solution.py:521
  56.0 3.8 %collective-permute-start.12 = (bf16[336,128]{1,0:T(8,128)(2,1)S(1)}, bf16[336,128]{1,0:T(8,128)(2,1)S(1)}, u32[]{:S(2)}, u32[]{:S(2)}) collective-permute-start(bf16[336,128]{1,0:T(8,128)(2,1)S(1)} %get-tuple-element.68), channel_id=1, source_target_pairs={{0,16},{4,20},{8,24},{12,28},{16,0},{20,4},{24,8},{28,12},{1,17},{... | collective-permute-start | bytes 258056 | tf_op jit(solution)/shard_map/ppermute | solution.py:531
  60.6 3.6 %collective-permute-start.14 = (bf16[336,128]{1,0:T(8,128)(2,1)S(1)}, bf16[336,128]{1,0:T(8,128)(2,1)S(1)}, u32[]{:S(2)}, u32[]{:S(2)}) collective-permute-start(bf16[336,128]{1,0:T(8,128)(2,1)S(1)} %get-tuple-element.70), channel_id=1, source_target_pairs={{0,20},{4,16},{8,28},{12,24},{16,4},{20,0},{24,12},{28,8},{1,21},{... | collective-permute-start | bytes 258056 | tf_op jit(solution)/shard_map/ppermute | solution.py:531
  64.2 1.5 %collective-permute-start.15 = (bf16[336,128]{1,0:T(8,128)(2,1)S(1)}, bf16[336,128]{1,0:T(8,128)(2,1)S(1)}, u32[]{:S(2)}, u32[]{:S(2)}) collective-permute-start(bf16[336,128]{1,0:T(8,128)(2,1)S(1)} %get-tuple-element.71), channel_id=1, source_target_pairs={{0,24},{4,28},{8,16},{12,20},{16,8},{20,12},{24,0},{28,4},{1,25},{... | collective-permute-start | bytes 258056 | tf_op jit(solution)/shard_map/ppermute | solution.py:531
  65.7 2.5 %collective-permute-start.16 = (bf16[336,128]{1,0:T(8,128)(2,1)S(1)}, bf16[336,128]{1,0:T(8,128)(2,1)S(1)}, u32[]{:S(2)}, u32[]{:S(2)}) collective-permute-start(bf16[336,128]{1,0:T(8,128)(2,1)S(1)} %get-tuple-element.72), channel_id=1, source_target_pairs={{0,28},{4,24},{8,20},{12,16},{16,12},{20,8},{24,4},{28,0},{1,29},{... | collective-permute-start | bytes 258056 | tf_op jit(solution)/shard_map/ppermute | solution.py:531
  68.2 3.9 %collective-permute-done.14.refs_5_ = bf16[336,128]{1,0:T(8,128)(2,1)S(1)} collective-permute-done((bf16[336,128]{1,0:T(8,128)(2,1)S(1)}, bf16[336,128]{1,0:T(8,128)(2,1)S(1)}, u32[]{:S(2)}, u32[]{:S(2)}) %collective-permute-start.14) | collective-permute-done | bytes 86048 | tf_op jit(solution)/shard_map/ppermute | solution.py:531
  72.1 1.2 %collective-permute-done.16.refs_7_ = bf16[336,128]{1,0:T(8,128)(2,1)S(1)} collective-permute-done((bf16[336,128]{1,0:T(8,128)(2,1)S(1)}, bf16[336,128]{1,0:T(8,128)(2,1)S(1)}, u32[]{:S(2)}, u32[]{:S(2)}) %collective-permute-start.16) | collective-permute-done | bytes 86048 | tf_op jit(solution)/shard_map/ppermute | solution.py:531
  74.2 1.2 %shard_map.89 = bf16[256,1280]{1,0:T(8,128)(2,1)} custom-call(f32[256,1280]{1,0:T(8,128)S(1)} %copy-done, bf16[336,128]{1,0:T(8,128)(2,1)S(1)} %get-tuple-element.64.refs_0_, bf16[336,128]{1,0:T(8,128)(2,1)S(1)} %collective-permute-done.10.refs_1_, bf16[336,128]{1,0:T(8,128)(2,1)S(1)} %collective-permute-done.11.refs_2_, ...), custom_call_target="tpu_custom_call" | custom-call | tf_op jit(solution)/shard_map/pallas_call | solution.py:521
  (36 shorter events, 6.5 us)
Async XLA Ops:
  2.1 41.7 %all-to-all-start = ((bf16[8,384,128]{2,1,0:T(8,128)(2,1)}), bf16[8,384,128]{2,1,0:T(8,128)(2,1)S(1)}, u32[]{:S(2)}, u32[]{:S(2)}) async-start(bf16[8,384,128]{2,1,0:T(8,128)(2,1)} %shard_map.82), calls=%async_computation | async-start | bytes 1572864 | tf_op jit(solution)/shard_map/all_to_all | solution.py:582
  11.6 3.4 %collective-permute-start.2 = (f32[8,256]{1,0:T(8,128)}, f32[8,256]{1,0:T(8,128)S(1)}, u32[]{:S(2)}, u32[]{:S(2)}) collective-permute-start(f32[8,256]{1,0:T(8,128)} %shard_map.83.refs_3_), channel_id=1, source_target_pairs={{0,3},{1,2},{2,1},{3,0},{4,7},{5,6},{6,5},{7,4},{8,11},{9,10},{10,... | collective-permute-start | bytes 24584 | tf_op jit(solution)/shard_map/ppermute | solution.py:531
  12.3 3.9 %collective-permute-start.1 = (f32[8,256]{1,0:T(8,128)}, f32[8,256]{1,0:T(8,128)S(1)}, u32[]{:S(2)}, u32[]{:S(2)}) collective-permute-start(f32[8,256]{1,0:T(8,128)} %shard_map.83.refs_3_), channel_id=1, source_target_pairs={{0,2},{1,3},{2,0},{3,1},{4,6},{5,7},{6,4},{7,5},{8,10},{9,11},{10,... | collective-permute-start | bytes 24584 | tf_op jit(solution)/shard_map/ppermute | solution.py:531
  13.2 3.0 %collective-permute-start = (f32[8,256]{1,0:T(8,128)}, f32[8,256]{1,0:T(8,128)S(1)}, u32[]{:S(2)}, u32[]{:S(2)}) collective-permute-start(f32[8,256]{1,0:T(8,128)} %shard_map.83.refs_3_), channel_id=1, source_target_pairs={{0,1},{1,0},{2,3},{3,2},{4,5},{5,4},{6,7},{7,6},{8,9},{9,8},{10,11... | collective-permute-start | bytes 24584 | tf_op jit(solution)/shard_map/ppermute | solution.py:531
  14.9 1.3 %copy-start.3 = (f32[8,256]{1,0:T(8,128)}, f32[8,256]{1,0:T(8,128)S(1)}, u32[]{:S(2)}) copy-start(f32[8,256]{1,0:T(8,128)S(1)} %collective-permute-done.2.refs_6_) | copy-start | bytes 24580
  16.2 0.6 copy-start.5
  21.1 27.0 %copy-start.1 = (bf16[592,128]{1,0:T(8,128)(2,1)S(1)}, bf16[592,128]{1,0:T(8,128)(2,1)}, u32[]{:S(2)}) copy-start(bf16[592,128]{1,0:T(8,128)(2,1)} %get-tuple-element.48.in_ref) | copy-start | bytes 454660
  21.1 9.5 %collective-permute-start.4 = (bf16[592,128]{1,0:T(8,128)(2,1)}, bf16[592,128]{1,0:T(8,128)(2,1)S(1)}, u32[]{:S(2)}, u32[]{:S(2)}) collective-permute-start(bf16[592,128]{1,0:T(8,128)(2,1)} %get-tuple-element.46), channel_id=1, source_target_pairs={{0,8},{4,12},{8,0},{12,4},{16,24},{20,28},{24,16},{28,20},{1,9},{5... | collective-permute-start | bytes 454664 | tf_op jit(solution)/shard_map/ppermute | solution.py:531
  22.8 11.3 %collective-permute-start.3 = (bf16[592,128]{1,0:T(8,128)(2,1)}, bf16[592,128]{1,0:T(8,128)(2,1)S(1)}, u32[]{:S(2)}, u32[]{:S(2)}) collective-permute-start(bf16[592,128]{1,0:T(8,128)(2,1)} %get-tuple-element.45), channel_id=1, source_target_pairs={{0,4},{4,0},{8,12},{12,8},{16,20},{20,16},{24,28},{28,24},{1,5},{5... | collective-permute-start | bytes 454664 | tf_op jit(solution)/shard_map/ppermute | solution.py:531
  24.9 23.2 %collective-permute-start.6 = (bf16[592,128]{1,0:T(8,128)(2,1)}, bf16[592,128]{1,0:T(8,128)(2,1)S(1)}, u32[]{:S(2)}, u32[]{:S(2)}) collective-permute-start(bf16[592,128]{1,0:T(8,128)(2,1)} %get-tuple-element.51), channel_id=1, source_target_pairs={{0,16},{4,20},{8,24},{12,28},{16,0},{20,4},{24,8},{28,12},{1,17},{... | collective-permute-start | bytes 454664 | tf_op jit(solution)/shard_map/ppermute | solution.py:531
  27.4 23.6 %collective-permute-start.7 = (bf16[592,128]{1,0:T(8,128)(2,1)}, bf16[592,128]{1,0:T(8,128)(2,1)S(1)}, u32[]{:S(2)}, u32[]{:S(2)}) collective-permute-start(bf16[592,128]{1,0:T(8,128)(2,1)} %get-tuple-element.52), channel_id=1, source_target_pairs={{0,20},{4,16},{8,28},{12,24},{16,4},{20,0},{24,12},{28,8},{1,21},{... | collective-permute-start | bytes 454664 | tf_op jit(solution)/shard_map/ppermute | solution.py:531
  27.9 23.1 %collective-permute-start.8 = (bf16[592,128]{1,0:T(8,128)(2,1)}, bf16[592,128]{1,0:T(8,128)(2,1)S(1)}, u32[]{:S(2)}, u32[]{:S(2)}) collective-permute-start(bf16[592,128]{1,0:T(8,128)(2,1)} %get-tuple-element.53), channel_id=1, source_target_pairs={{0,24},{4,28},{8,16},{12,20},{16,8},{20,12},{24,0},{28,4},{1,25},{... | collective-permute-start | bytes 454664 | tf_op jit(solution)/shard_map/ppermute | solution.py:531
  30.6 20.4 %collective-permute-start.9 = (bf16[592,128]{1,0:T(8,128)(2,1)}, bf16[592,128]{1,0:T(8,128)(2,1)S(1)}, u32[]{:S(2)}, u32[]{:S(2)}) collective-permute-start(bf16[592,128]{1,0:T(8,128)(2,1)} %get-tuple-element.54), channel_id=1, source_target_pairs={{0,28},{4,24},{8,20},{12,16},{16,12},{20,8},{24,4},{28,0},{1,29},{... | collective-permute-start | bytes 454664 | tf_op jit(solution)/shard_map/ppermute | solution.py:531
  34.1 19.2 %collective-permute-start.5 = (bf16[592,128]{1,0:T(8,128)(2,1)}, bf16[592,128]{1,0:T(8,128)(2,1)S(1)}, u32[]{:S(2)}, u32[]{:S(2)}) collective-permute-start(bf16[592,128]{1,0:T(8,128)(2,1)} %get-tuple-element.50), channel_id=1, source_target_pairs={{0,12},{4,8},{8,4},{12,0},{16,28},{20,24},{24,20},{28,16},{1,13},{... | collective-permute-start | bytes 454664 | tf_op jit(solution)/shard_map/ppermute | solution.py:531
  44.5 10.5 %all-to-all-start.1 = ((bf16[4,128,128]{2,1,0:T(8,128)(2,1)}), bf16[4,128,128]{2,1,0:T(8,128)(2,1)S(1)}, u32[]{:S(2)}, u32[]{:S(2)}) async-start(bf16[4,128,128]{2,1,0:T(8,128)(2,1)} %broadcast_in_dim.8), calls=%async_computation.1 | async-start | bytes 262144 | tf_op jit(solution)/shard_map/all_to_all | solution.py:617
  48.1 6.9 %copy-start.2 = (f32[1280]{0:T(1024)S(1)}, f32[1280]{0:T(1024)}, u32[]{:S(2)}) copy-start(f32[1280]{0:T(1024)} %param.12) | copy-start | bytes 15364
  55.0 19.2 %copy-start = (f32[256,1280]{1,0:T(8,128)S(1)}, f32[256,1280]{1,0:T(8,128)}, u32[]{:S(2)}) copy-start(f32[256,1280]{1,0:T(8,128)} %get-tuple-element.42.own_ref) | copy-start | bytes 3932164
  56.0 9.6 %collective-permute-start.12 = (bf16[336,128]{1,0:T(8,128)(2,1)S(1)}, bf16[336,128]{1,0:T(8,128)(2,1)S(1)}, u32[]{:S(2)}, u32[]{:S(2)}) collective-permute-start(bf16[336,128]{1,0:T(8,128)(2,1)S(1)} %get-tuple-element.68), channel_id=1, source_target_pairs={{0,16},{4,20},{8,24},{12,28},{16,0},{20,4},{24,8},{28,12},{1,17},{... | collective-permute-start | bytes 258056 | tf_op jit(solution)/shard_map/ppermute | solution.py:531
  59.8 8.3 %collective-permute-start.10 = (bf16[336,128]{1,0:T(8,128)(2,1)S(1)}, bf16[336,128]{1,0:T(8,128)(2,1)S(1)}, u32[]{:S(2)}, u32[]{:S(2)}) collective-permute-start(bf16[336,128]{1,0:T(8,128)(2,1)S(1)} %get-tuple-element.65), channel_id=1, source_target_pairs={{0,4},{4,0},{8,12},{12,8},{16,20},{20,16},{24,28},{28,24},{1,5},{5... | collective-permute-start | bytes 258056 | tf_op jit(solution)/shard_map/ppermute | solution.py:531
  60.2 7.9 %collective-permute-start.11 = (bf16[336,128]{1,0:T(8,128)(2,1)S(1)}, bf16[336,128]{1,0:T(8,128)(2,1)S(1)}, u32[]{:S(2)}, u32[]{:S(2)}) collective-permute-start(bf16[336,128]{1,0:T(8,128)(2,1)S(1)} %get-tuple-element.66), channel_id=1, source_target_pairs={{0,8},{4,12},{8,0},{12,4},{16,24},{20,28},{24,16},{28,20},{1,9},{5... | collective-permute-start | bytes 258056 | tf_op jit(solution)/shard_map/ppermute | solution.py:531
  60.6 11.5 %collective-permute-start.14 = (bf16[336,128]{1,0:T(8,128)(2,1)S(1)}, bf16[336,128]{1,0:T(8,128)(2,1)S(1)}, u32[]{:S(2)}, u32[]{:S(2)}) collective-permute-start(bf16[336,128]{1,0:T(8,128)(2,1)S(1)} %get-tuple-element.70), channel_id=1, source_target_pairs={{0,20},{4,16},{8,28},{12,24},{16,4},{20,0},{24,12},{28,8},{1,21},{... | collective-permute-start | bytes 258056 | tf_op jit(solution)/shard_map/ppermute | solution.py:531
  64.2 7.9 %collective-permute-start.15 = (bf16[336,128]{1,0:T(8,128)(2,1)S(1)}, bf16[336,128]{1,0:T(8,128)(2,1)S(1)}, u32[]{:S(2)}, u32[]{:S(2)}) collective-permute-start(bf16[336,128]{1,0:T(8,128)(2,1)S(1)} %get-tuple-element.71), channel_id=1, source_target_pairs={{0,24},{4,28},{8,16},{12,20},{16,8},{20,12},{24,0},{28,4},{1,25},{... | collective-permute-start | bytes 258056 | tf_op jit(solution)/shard_map/ppermute | solution.py:531
  65.7 7.6 %collective-permute-start.16 = (bf16[336,128]{1,0:T(8,128)(2,1)S(1)}, bf16[336,128]{1,0:T(8,128)(2,1)S(1)}, u32[]{:S(2)}, u32[]{:S(2)}) collective-permute-start(bf16[336,128]{1,0:T(8,128)(2,1)S(1)} %get-tuple-element.72), channel_id=1, source_target_pairs={{0,28},{4,24},{8,20},{12,16},{16,12},{20,8},{24,4},{28,0},{1,29},{... | collective-permute-start | bytes 258056 | tf_op jit(solution)/shard_map/ppermute | solution.py:531
  68.1 6.0 %collective-permute-start.13 = (bf16[336,128]{1,0:T(8,128)(2,1)S(1)}, bf16[336,128]{1,0:T(8,128)(2,1)S(1)}, u32[]{:S(2)}, u32[]{:S(2)}) collective-permute-start(bf16[336,128]{1,0:T(8,128)(2,1)S(1)} %get-tuple-element.69), channel_id=1, source_target_pairs={{0,12},{4,8},{8,4},{12,0},{16,28},{20,24},{24,20},{28,16},{1,13},{... | collective-permute-start | bytes 258056 | tf_op jit(solution)/shard_map/ppermute | solution.py:531
  (1 other events, 0.6 us)

commit v9 on v8

--- a/solution.py
+++ b/solution.py
@@ -657,7 +657,7 @@
         in_specs=[sm] + [vm] * (2 * n + 5),
         scratch_shapes=[pltpu.VMEM((2, n, HD), f32), pltpu.VMEM((HD, HD), f32)],
     )
-    back = swap_blocks(result, (4, 6, 5, 7, 1, 2, 3), {3: 4})
+    back = swap_blocks(result, (4, 6, 5, 7, 1, 2, 3), {1: 4})
     return call(
         functools.partial(join_kernel, n, pos),
         shape((tok, width), bf16),

time: 75.8 us -> 75.7 us (level)
  waiting for transfers between devices: 23.5 us -> 22.5 us
    ppermute x17, waiting for transfers between devices: 14.3 us -> 13.3 us  [pairwise(): return lax.ppermute(array, axis, [(i, i ^ step) for i in range(size)])]
    ppermute x17, starting transfers between devices: 26.6 us -> 27.3 us  [pairwise(): return lax.ppermute(array, axis, [(i, i ^ step) for i in range(size)])]
  transfers between devices with their start and end apart: 19 -> 19, of which waited for: 9 -> 7; matrix products, arithmetic and copies ran while one was open for 1% -> 1% of each run, Pallas kernels for 11% -> 11%
where the time goes in v9:
time: 75.7 us; the launch traced here: 75.1 us
  starting transfers between devices  37.9 us (50%)
  waiting for transfers between devices  22.5 us (30%)
  Pallas kernels  12.6 us (17%)
  local copies, waits for them, and re-layouts  1.29 us (2%)
  between operations  0.79 us (1%)
    ppermute x17, starting transfers between devices, pairwise(): return lax.ppermute(array, axis, [(i, i ^ step) for i in range(size)])  27.3 us
    ppermute x17, waiting for transfers between devices, pairwise(): return lax.ppermute(array, axis, [(i, i ^ step) for i in range(size)])  13.3 us
    pallas_call x8, Pallas kernels, call(): pl.pallas_call(kernel, out_shape=out_shape, compiler_params=pltpu.Compile...  12.6 us
    all_to_all x1, waiting for transfers between devices, local_heads(): lax.all_to_all(v_blocks, 'frame', split_axis=0, concat_axis=0, tiled=True)  9.23 us
    all_to_all x1, starting transfers between devices, local_heads(): lax.all_to_all(v_blocks, 'frame', split_axis=0, concat_axis=0, tiled=True)  7.27 us
    all_to_all x1, starting transfers between devices, local_heads(): lax.all_to_all(jnp.broadcast_to(mine, (parts, 2 * pos, HD)), 'frame', spl...  3.32 us
  transfers between devices with their start and end apart: 19, of which 7 were waited for; matrix products, arithmetic and copies ran while one was open for 1% of the time, Pallas kernels for 11%

profile of v9, /device:TPU:0, one launch (start us, length us, event | category | flops | bytes accessed | tf_op | source)
XLA Modules:
  0.0 75.1 jit_solution(8344564230442803264)
XLA Ops:
  0.0 2.1 %shard_map.82 = bf16[8,384,128]{2,1,0:T(8,128)(2,1)} custom-call(bf16[256,1280]{1,0:T(8,128)(2,1)} %refs_1_, bf16[256,1280]{1,0:T(8,128)(2,1)} %refs_2_), custom_call_target="tpu_custom_call" | custom-call | tf_op jit(solution)/shard_map/pallas_call | solution.py:521
  2.1 7.3 %all-to-all-start = ((bf16[8,384,128]{2,1,0:T(8,128)(2,1)}), bf16[8,384,128]{2,1,0:T(8,128)(2,1)S(1)}, u32[]{:S(2)}, u32[]{:S(2)}) async-start(bf16[8,384,128]{2,1,0:T(8,128)(2,1)} %shard_map.82), calls=%async_computation | async-start | bytes 1572864 | tf_op jit(solution)/shard_map/all_to_all | solution.py:582
  9.4 2.2 %shard_map.83.refs_3_ = f32[8,256]{1,0:T(8,128)} custom-call(bf16[256,1280]{1,0:T(8,128)(2,1)} %refs_0_, bf16[256,1280]{1,0:T(8,128)(2,1)} %refs_1_), custom_call_target="tpu_custom_call" | custom-call | tf_op jit(solution)/shard_map/pallas_call | solution.py:521
  13.5 1.4 %collective-permute-done.2.refs_6_ = f32[8,256]{1,0:T(8,128)S(1)} collective-permute-done((f32[8,256]{1,0:T(8,128)}, f32[8,256]{1,0:T(8,128)S(1)}, u32[]{:S(2)}, u32[]{:S(2)}) %collective-permute-start.2) | collective-permute-done | bytes 8224 | tf_op jit(solution)/shard_map/ppermute | solution.py:531
  14.9 1.3 %collective-permute-done.1.refs_5_ = f32[8,256]{1,0:T(8,128)S(1)} collective-permute-done((f32[8,256]{1,0:T(8,128)}, f32[8,256]{1,0:T(8,128)S(1)}, u32[]{:S(2)}, u32[]{:S(2)}) %collective-permute-start.1) | collective-permute-done | bytes 8224 | tf_op jit(solution)/shard_map/ppermute | solution.py:531
  16.9 4.2 %shard_map.84 = (bf16[592,128]{1,0:T(8,128)(2,1)}, bf16[592,128]{1,0:T(8,128)(2,1)}, bf16[592,128]{1,0:T(8,128)(2,1)}, bf16[592,128]{1,0:T(8,128)(2,1)}, bf16[59...) custom-call(bf16[256,1280]{1,0:T(8,128)(2,1)} %refs_0_, ...), custom_call_target="tpu_custom_call" | custom-call | tf_op jit(solution)/shard_map/pallas_call | solution.py:521
  21.1 1.7 %collective-permute-start.4 = (bf16[592,128]{1,0:T(8,128)(2,1)}, bf16[592,128]{1,0:T(8,128)(2,1)S(1)}, u32[]{:S(2)}, u32[]{:S(2)}) collective-permute-start(bf16[592,128]{1,0:T(8,128)(2,1)} %get-tuple-element.46), channel_id=1, source_target_pairs={{0,8},{4,12},{8,0},{12,4},{16,24},{20,28},{24,16},{28,20},{1,9},{5... | collective-permute-start | bytes 454664 | tf_op jit(solution)/shard_map/ppermute | solution.py:531
  22.8 1.4 %collective-permute-start.3 = (bf16[592,128]{1,0:T(8,128)(2,1)}, bf16[592,128]{1,0:T(8,128)(2,1)S(1)}, u32[]{:S(2)}, u32[]{:S(2)}) collective-permute-start(bf16[592,128]{1,0:T(8,128)(2,1)} %get-tuple-element.45), channel_id=1, source_target_pairs={{0,4},{4,0},{8,12},{12,8},{16,20},{20,16},{24,28},{28,24},{1,5},{5... | collective-permute-start | bytes 454664 | tf_op jit(solution)/shard_map/ppermute | solution.py:531
  24.9 2.5 %collective-permute-start.6 = (bf16[592,128]{1,0:T(8,128)(2,1)}, bf16[592,128]{1,0:T(8,128)(2,1)S(1)}, u32[]{:S(2)}, u32[]{:S(2)}) collective-permute-start(bf16[592,128]{1,0:T(8,128)(2,1)} %get-tuple-element.51), channel_id=1, source_target_pairs={{0,16},{4,20},{8,24},{12,28},{16,0},{20,4},{24,8},{28,12},{1,17},{... | collective-permute-start | bytes 454664 | tf_op jit(solution)/shard_map/ppermute | solution.py:531
  27.9 2.4 %collective-permute-start.8 = (bf16[592,128]{1,0:T(8,128)(2,1)}, bf16[592,128]{1,0:T(8,128)(2,1)S(1)}, u32[]{:S(2)}, u32[]{:S(2)}) collective-permute-start(bf16[592,128]{1,0:T(8,128)(2,1)} %get-tuple-element.53), channel_id=1, source_target_pairs={{0,24},{4,28},{8,16},{12,20},{16,8},{20,12},{24,0},{28,4},{1,25},{... | collective-permute-start | bytes 454664 | tf_op jit(solution)/shard_map/ppermute | solution.py:531
  30.6 3.5 %collective-permute-start.9 = (bf16[592,128]{1,0:T(8,128)(2,1)}, bf16[592,128]{1,0:T(8,128)(2,1)S(1)}, u32[]{:S(2)}, u32[]{:S(2)}) collective-permute-start(bf16[592,128]{1,0:T(8,128)(2,1)} %get-tuple-element.54), channel_id=1, source_target_pairs={{0,28},{4,24},{8,20},{12,16},{16,12},{20,8},{24,4},{28,0},{1,29},{... | collective-permute-start | bytes 454664 | tf_op jit(solution)/shard_map/ppermute | solution.py:531
  34.6 9.2 %all-to-all-done.v_ref = bf16[8,384,128]{2,1,0:T(8,128)(2,1)S(1)} async-done(((bf16[8,384,128]{2,1,0:T(8,128)(2,1)}), bf16[8,384,128]{2,1,0:T(8,128)(2,1)S(1)}, u32[]{:S(2)}, u32[]{:S(2)}) %all-to-all-start) | async-done | bytes 786464 | tf_op jit(solution)/shard_map/all_to_all | solution.py:582
  44.5 3.3 %all-to-all-start.1 = ((bf16[4,128,128]{2,1,0:T(8,128)(2,1)}), bf16[4,128,128]{2,1,0:T(8,128)(2,1)S(1)}, u32[]{:S(2)}, u32[]{:S(2)}) async-start(bf16[4,128,128]{2,1,0:T(8,128)(2,1)} %broadcast_in_dim.8), calls=%async_computation.1 | async-start | bytes 262144 | tf_op jit(solution)/shard_map/all_to_all | solution.py:617
  48.1 2.9 %collective-permute-done.7.refs_5_ = bf16[592,128]{1,0:T(8,128)(2,1)S(1)} collective-permute-done((bf16[592,128]{1,0:T(8,128)(2,1)}, bf16[592,128]{1,0:T(8,128)(2,1)S(1)}, u32[]{:S(2)}, u32[]{:S(2)}) %collective-permute-start.7) | collective-permute-done | bytes 151584 | tf_op jit(solution)/shard_map/ppermute | solution.py:531
  51.0 2.3 %collective-permute-done.5.refs_3_ = bf16[592,128]{1,0:T(8,128)(2,1)S(1)} collective-permute-done((bf16[592,128]{1,0:T(8,128)(2,1)}, bf16[592,128]{1,0:T(8,128)(2,1)S(1)}, u32[]{:S(2)}, u32[]{:S(2)}) %collective-permute-start.5) | collective-permute-done | bytes 151584 | tf_op jit(solution)/shard_map/ppermute | solution.py:531
  53.3 1.7 %shard_map.87 = (bf16[256,128]{1,0:T(8,128)(2,1)S(1)}, bf16[256,128]{1,0:T(8,128)(2,1)S(1)}, bf16[256,128]{1,0:T(8,128)(2,1)S(1)}, bf16[256,128]{1,0:T(8,128)(2,...) custom-call(s32[1]{0:T(128)} %copy.9.at_ref, ...), custom_call_target="tpu_custom_call" | custom-call | flops 805306368 | bytes 2097152 | tf_op jit(solution)/shard_map/pallas_call | solution.py:521
  56.0 3.8 %collective-permute-start.10 = (bf16[336,128]{1,0:T(8,128)(2,1)S(1)}, bf16[336,128]{1,0:T(8,128)(2,1)S(1)}, u32[]{:S(2)}, u32[]{:S(2)}) collective-permute-start(bf16[336,128]{1,0:T(8,128)(2,1)S(1)} %get-tuple-element.66), channel_id=1, source_target_pairs={{0,16},{4,20},{8,24},{12,28},{16,0},{20,4},{24,8},{28,12},{1,17},{... | collective-permute-start | bytes 258056 | tf_op jit(solution)/shard_map/ppermute | solution.py:531
  59.9 1.8 %collective-permute-start.13 = (bf16[336,128]{1,0:T(8,128)(2,1)S(1)}, bf16[336,128]{1,0:T(8,128)(2,1)S(1)}, u32[]{:S(2)}, u32[]{:S(2)}) collective-permute-start(bf16[336,128]{1,0:T(8,128)(2,1)S(1)} %get-tuple-element.69), channel_id=1, source_target_pairs={{0,12},{4,8},{8,4},{12,0},{16,28},{20,24},{24,20},{28,16},{1,13},{... | collective-permute-start | bytes 258056 | tf_op jit(solution)/shard_map/ppermute | solution.py:531
  61.7 1.9 %collective-permute-start.14 = (bf16[336,128]{1,0:T(8,128)(2,1)S(1)}, bf16[336,128]{1,0:T(8,128)(2,1)S(1)}, u32[]{:S(2)}, u32[]{:S(2)}) collective-permute-start(bf16[336,128]{1,0:T(8,128)(2,1)S(1)} %get-tuple-element.70), channel_id=1, source_target_pairs={{0,20},{4,16},{8,28},{12,24},{16,4},{20,0},{24,12},{28,8},{1,21},{... | collective-permute-start | bytes 258056 | tf_op jit(solution)/shard_map/ppermute | solution.py:531
  63.6 1.5 %collective-permute-start.15 = (bf16[336,128]{1,0:T(8,128)(2,1)S(1)}, bf16[336,128]{1,0:T(8,128)(2,1)S(1)}, u32[]{:S(2)}, u32[]{:S(2)}) collective-permute-start(bf16[336,128]{1,0:T(8,128)(2,1)S(1)} %get-tuple-element.71), channel_id=1, source_target_pairs={{0,24},{4,28},{8,16},{12,20},{16,8},{20,12},{24,0},{28,4},{1,25},{... | collective-permute-start | bytes 258056 | tf_op jit(solution)/shard_map/ppermute | solution.py:531
  65.2 2.4 %collective-permute-start.16 = (bf16[336,128]{1,0:T(8,128)(2,1)S(1)}, bf16[336,128]{1,0:T(8,128)(2,1)S(1)}, u32[]{:S(2)}, u32[]{:S(2)}) collective-permute-start(bf16[336,128]{1,0:T(8,128)(2,1)S(1)} %get-tuple-element.72), channel_id=1, source_target_pairs={{0,28},{4,24},{8,20},{12,16},{16,12},{20,8},{24,4},{28,0},{1,29},{... | collective-permute-start | bytes 258056 | tf_op jit(solution)/shard_map/ppermute | solution.py:531
  67.6 1.3 %collective-permute-start.11 = (bf16[336,128]{1,0:T(8,128)(2,1)S(1)}, bf16[336,128]{1,0:T(8,128)(2,1)S(1)}, u32[]{:S(2)}, u32[]{:S(2)}) collective-permute-start(bf16[336,128]{1,0:T(8,128)(2,1)S(1)} %get-tuple-element.67), channel_id=1, source_target_pairs={{0,4},{4,0},{8,12},{12,8},{16,20},{20,16},{24,28},{28,24},{1,5},{5... | collective-permute-start | bytes 258056 | tf_op jit(solution)/shard_map/ppermute | solution.py:531
  68.9 5.0 %collective-permute-done.14.refs_5_ = bf16[336,128]{1,0:T(8,128)(2,1)S(1)} collective-permute-done((bf16[336,128]{1,0:T(8,128)(2,1)S(1)}, bf16[336,128]{1,0:T(8,128)(2,1)S(1)}, u32[]{:S(2)}, u32[]{:S(2)}) %collective-permute-start.14) | collective-permute-done | bytes 86048 | tf_op jit(solution)/shard_map/ppermute | solution.py:531
  73.9 1.2 %shard_map.89 = bf16[256,1280]{1,0:T(8,128)(2,1)} custom-call(f32[256,1280]{1,0:T(8,128)S(1)} %copy-done, bf16[336,128]{1,0:T(8,128)(2,1)S(1)} %get-tuple-element.64.refs_0_, bf16[336,128]{1,0:T(8,128)(2,1)S(1)} %collective-permute-done.11.refs_1_, bf16[336,128]{1,0:T(8,128)(2,1)S(1)} %collective-permute-done.12.refs_2_, ...), custom_call_target="tpu_custom_call" | custom-call | tf_op jit(solution)/shard_map/pallas_call | solution.py:521
  (36 shorter events, 5.9 us)
Async XLA Ops:
  2.1 41.7 %all-to-all-start = ((bf16[8,384,128]{2,1,0:T(8,128)(2,1)}), bf16[8,384,128]{2,1,0:T(8,128)(2,1)S(1)}, u32[]{:S(2)}, u32[]{:S(2)}) async-start(bf16[8,384,128]{2,1,0:T(8,128)(2,1)} %shard_map.82), calls=%async_computation | async-start | bytes 1572864 | tf_op jit(solution)/shard_map/all_to_all | solution.py:582
  11.6 3.4 %collective-permute-start.2 = (f32[8,256]{1,0:T(8,128)}, f32[8,256]{1,0:T(8,128)S(1)}, u32[]{:S(2)}, u32[]{:S(2)}) collective-permute-start(f32[8,256]{1,0:T(8,128)} %shard_map.83.refs_3_), channel_id=1, source_target_pairs={{0,3},{1,2},{2,1},{3,0},{4,7},{5,6},{6,5},{7,4},{8,11},{9,10},{10,... | collective-permute-start | bytes 24584 | tf_op jit(solution)/shard_map/ppermute | solution.py:531
  12.3 3.9 %collective-permute-start.1 = (f32[8,256]{1,0:T(8,128)}, f32[8,256]{1,0:T(8,128)S(1)}, u32[]{:S(2)}, u32[]{:S(2)}) collective-permute-start(f32[8,256]{1,0:T(8,128)} %shard_map.83.refs_3_), channel_id=1, source_target_pairs={{0,2},{1,3},{2,0},{3,1},{4,6},{5,7},{6,4},{7,5},{8,10},{9,11},{10,... | collective-permute-start | bytes 24584 | tf_op jit(solution)/shard_map/ppermute | solution.py:531
  13.2 3.0 %collective-permute-start = (f32[8,256]{1,0:T(8,128)}, f32[8,256]{1,0:T(8,128)S(1)}, u32[]{:S(2)}, u32[]{:S(2)}) collective-permute-start(f32[8,256]{1,0:T(8,128)} %shard_map.83.refs_3_), channel_id=1, source_target_pairs={{0,1},{1,0},{2,3},{3,2},{4,5},{5,4},{6,7},{7,6},{8,9},{9,8},{10,11... | collective-permute-start | bytes 24584 | tf_op jit(solution)/shard_map/ppermute | solution.py:531
  14.9 1.3 %copy-start.3 = (f32[8,256]{1,0:T(8,128)}, f32[8,256]{1,0:T(8,128)S(1)}, u32[]{:S(2)}) copy-start(f32[8,256]{1,0:T(8,128)S(1)} %collective-permute-done.2.refs_6_) | copy-start | bytes 24580
  16.2 0.6 copy-start.5
  21.1 27.0 %copy-start.1 = (bf16[592,128]{1,0:T(8,128)(2,1)S(1)}, bf16[592,128]{1,0:T(8,128)(2,1)}, u32[]{:S(2)}) copy-start(bf16[592,128]{1,0:T(8,128)(2,1)} %get-tuple-element.48.in_ref) | copy-start | bytes 454660
  21.1 9.5 %collective-permute-start.4 = (bf16[592,128]{1,0:T(8,128)(2,1)}, bf16[592,128]{1,0:T(8,128)(2,1)S(1)}, u32[]{:S(2)}, u32[]{:S(2)}) collective-permute-start(bf16[592,128]{1,0:T(8,128)(2,1)} %get-tuple-element.46), channel_id=1, source_target_pairs={{0,8},{4,12},{8,0},{12,4},{16,24},{20,28},{24,16},{28,20},{1,9},{5... | collective-permute-start | bytes 454664 | tf_op jit(solution)/shard_map/ppermute | solution.py:531
  22.8 11.3 %collective-permute-start.3 = (bf16[592,128]{1,0:T(8,128)(2,1)}, bf16[592,128]{1,0:T(8,128)(2,1)S(1)}, u32[]{:S(2)}, u32[]{:S(2)}) collective-permute-start(bf16[592,128]{1,0:T(8,128)(2,1)} %get-tuple-element.45), channel_id=1, source_target_pairs={{0,4},{4,0},{8,12},{12,8},{16,20},{20,16},{24,28},{28,24},{1,5},{5... | collective-permute-start | bytes 454664 | tf_op jit(solution)/shard_map/ppermute | solution.py:531
  24.9 23.2 %collective-permute-start.6 = (bf16[592,128]{1,0:T(8,128)(2,1)}, bf16[592,128]{1,0:T(8,128)(2,1)S(1)}, u32[]{:S(2)}, u32[]{:S(2)}) collective-permute-start(bf16[592,128]{1,0:T(8,128)(2,1)} %get-tuple-element.51), channel_id=1, source_target_pairs={{0,16},{4,20},{8,24},{12,28},{16,0},{20,4},{24,8},{28,12},{1,17},{... | collective-permute-start | bytes 454664 | tf_op jit(solution)/shard_map/ppermute | solution.py:531
  27.4 23.6 %collective-permute-start.7 = (bf16[592,128]{1,0:T(8,128)(2,1)}, bf16[592,128]{1,0:T(8,128)(2,1)S(1)}, u32[]{:S(2)}, u32[]{:S(2)}) collective-permute-start(bf16[592,128]{1,0:T(8,128)(2,1)} %get-tuple-element.52), channel_id=1, source_target_pairs={{0,20},{4,16},{8,28},{12,24},{16,4},{20,0},{24,12},{28,8},{1,21},{... | collective-permute-start | bytes 454664 | tf_op jit(solution)/shard_map/ppermute | solution.py:531
  27.9 23.1 %collective-permute-start.8 = (bf16[592,128]{1,0:T(8,128)(2,1)}, bf16[592,128]{1,0:T(8,128)(2,1)S(1)}, u32[]{:S(2)}, u32[]{:S(2)}) collective-permute-start(bf16[592,128]{1,0:T(8,128)(2,1)} %get-tuple-element.53), channel_id=1, source_target_pairs={{0,24},{4,28},{8,16},{12,20},{16,8},{20,12},{24,0},{28,4},{1,25},{... | collective-permute-start | bytes 454664 | tf_op jit(solution)/shard_map/ppermute | solution.py:531
  30.6 20.4 %collective-permute-start.9 = (bf16[592,128]{1,0:T(8,128)(2,1)}, bf16[592,128]{1,0:T(8,128)(2,1)S(1)}, u32[]{:S(2)}, u32[]{:S(2)}) collective-permute-start(bf16[592,128]{1,0:T(8,128)(2,1)} %get-tuple-element.54), channel_id=1, source_target_pairs={{0,28},{4,24},{8,20},{12,16},{16,12},{20,8},{24,4},{28,0},{1,29},{... | collective-permute-start | bytes 454664 | tf_op jit(solution)/shard_map/ppermute | solution.py:531
  34.1 19.2 %collective-permute-start.5 = (bf16[592,128]{1,0:T(8,128)(2,1)}, bf16[592,128]{1,0:T(8,128)(2,1)S(1)}, u32[]{:S(2)}, u32[]{:S(2)}) collective-permute-start(bf16[592,128]{1,0:T(8,128)(2,1)} %get-tuple-element.50), channel_id=1, source_target_pairs={{0,12},{4,8},{8,4},{12,0},{16,28},{20,24},{24,20},{28,16},{1,13},{... | collective-permute-start | bytes 454664 | tf_op jit(solution)/shard_map/ppermute | solution.py:531
  44.5 10.5 %all-to-all-start.1 = ((bf16[4,128,128]{2,1,0:T(8,128)(2,1)}), bf16[4,128,128]{2,1,0:T(8,128)(2,1)S(1)}, u32[]{:S(2)}, u32[]{:S(2)}) async-start(bf16[4,128,128]{2,1,0:T(8,128)(2,1)} %broadcast_in_dim.8), calls=%async_computation.1 | async-start | bytes 262144 | tf_op jit(solution)/shard_map/all_to_all | solution.py:617
  48.1 6.9 %copy-start.2 = (f32[1280]{0:T(1024)S(1)}, f32[1280]{0:T(1024)}, u32[]{:S(2)}) copy-start(f32[1280]{0:T(1024)} %param.12) | copy-start | bytes 15364
  55.0 18.9 %copy-start = (f32[256,1280]{1,0:T(8,128)S(1)}, f32[256,1280]{1,0:T(8,128)}, u32[]{:S(2)}) copy-start(f32[256,1280]{1,0:T(8,128)} %get-tuple-element.42.own_ref) | copy-start | bytes 3932164
  56.0 9.1 %collective-permute-start.10 = (bf16[336,128]{1,0:T(8,128)(2,1)S(1)}, bf16[336,128]{1,0:T(8,128)(2,1)S(1)}, u32[]{:S(2)}, u32[]{:S(2)}) collective-permute-start(bf16[336,128]{1,0:T(8,128)(2,1)S(1)} %get-tuple-element.66), channel_id=1, source_target_pairs={{0,16},{4,20},{8,24},{12,28},{16,0},{20,4},{24,8},{28,12},{1,17},{... | collective-permute-start | bytes 258056 | tf_op jit(solution)/shard_map/ppermute | solution.py:531
  59.8 7.8 %collective-permute-start.12 = (bf16[336,128]{1,0:T(8,128)(2,1)S(1)}, bf16[336,128]{1,0:T(8,128)(2,1)S(1)}, u32[]{:S(2)}, u32[]{:S(2)}) collective-permute-start(bf16[336,128]{1,0:T(8,128)(2,1)S(1)} %get-tuple-element.68), channel_id=1, source_target_pairs={{0,8},{4,12},{8,0},{12,4},{16,24},{20,28},{24,16},{28,20},{1,9},{5... | collective-permute-start | bytes 258056 | tf_op jit(solution)/shard_map/ppermute | solution.py:531
  59.9 9.0 %collective-permute-start.13 = (bf16[336,128]{1,0:T(8,128)(2,1)S(1)}, bf16[336,128]{1,0:T(8,128)(2,1)S(1)}, u32[]{:S(2)}, u32[]{:S(2)}) collective-permute-start(bf16[336,128]{1,0:T(8,128)(2,1)S(1)} %get-tuple-element.69), channel_id=1, source_target_pairs={{0,12},{4,8},{8,4},{12,0},{16,28},{20,24},{24,20},{28,16},{1,13},{... | collective-permute-start | bytes 258056 | tf_op jit(solution)/shard_map/ppermute | solution.py:531
  61.7 12.2 %collective-permute-start.14 = (bf16[336,128]{1,0:T(8,128)(2,1)S(1)}, bf16[336,128]{1,0:T(8,128)(2,1)S(1)}, u32[]{:S(2)}, u32[]{:S(2)}) collective-permute-start(bf16[336,128]{1,0:T(8,128)(2,1)S(1)} %get-tuple-element.70), channel_id=1, source_target_pairs={{0,20},{4,16},{8,28},{12,24},{16,4},{20,0},{24,12},{28,8},{1,21},{... | collective-permute-start | bytes 258056 | tf_op jit(solution)/shard_map/ppermute | solution.py:531
  63.6 10.3 %collective-permute-start.15 = (bf16[336,128]{1,0:T(8,128)(2,1)S(1)}, bf16[336,128]{1,0:T(8,128)(2,1)S(1)}, u32[]{:S(2)}, u32[]{:S(2)}) collective-permute-start(bf16[336,128]{1,0:T(8,128)(2,1)S(1)} %get-tuple-element.71), channel_id=1, source_target_pairs={{0,24},{4,28},{8,16},{12,20},{16,8},{20,12},{24,0},{28,4},{1,25},{... | collective-permute-start | bytes 258056 | tf_op jit(solution)/shard_map/ppermute | solution.py:531
  65.2 8.8 %collective-permute-start.16 = (bf16[336,128]{1,0:T(8,128)(2,1)S(1)}, bf16[336,128]{1,0:T(8,128)(2,1)S(1)}, u32[]{:S(2)}, u32[]{:S(2)}) collective-permute-start(bf16[336,128]{1,0:T(8,128)(2,1)S(1)} %get-tuple-element.72), channel_id=1, source_target_pairs={{0,28},{4,24},{8,20},{12,16},{16,12},{20,8},{24,4},{28,0},{1,29},{... | collective-permute-start | bytes 258056 | tf_op jit(solution)/shard_map/ppermute | solution.py:531
  67.6 6.3 %collective-permute-start.11 = (bf16[336,128]{1,0:T(8,128)(2,1)S(1)}, bf16[336,128]{1,0:T(8,128)(2,1)S(1)}, u32[]{:S(2)}, u32[]{:S(2)}) collective-permute-start(bf16[336,128]{1,0:T(8,128)(2,1)S(1)} %get-tuple-element.67), channel_id=1, source_target_pairs={{0,4},{4,0},{8,12},{12,8},{16,20},{20,16},{24,28},{28,24},{1,5},{5... | collective-permute-start | bytes 258056 | tf_op jit(solution)/shard_map/ppermute | solution.py:531
  (1 other events, 0.6 us)
